TPU v7x, 32 devices: a whole 2x2x4 slice. The times are simulated.
32 devices in a mesh: groups: 2 (over y), fibre: 4 (over z), seg: 2 (over x), rec: 2 (over core).
Axes of the slice: x: 2, y: 2, z: 4, core: 2. Of those that a mesh axis runs over, the one named last changes fastest.
Arguments:
- records: bfloat16 [2, 2048, 1024], P('rec', 'fibre', ('groups', 'seg')), parts along dimension 2, may hold values from -6 to 6
- pairs: int32 [16, 2], replicated, may hold values from 0 to 15
- observed: float32 [32, 32, 256], P(('groups', 'fibre', 'seg')), parts along dimension 0, may hold values from -6 to 6
- lag_mask: int32 [32, 256], P(('groups', 'fibre', 'seg')), parts along dimension 0, may hold values 0 or 1
Outputs:
- adjoint_sources: bfloat16 [2, 2048, 1024], P('rec', 'fibre', ('groups', 'seg')), parts along dimension 2
There are 2 independent parts, one for each index of `groups`. A program takes and returns all parts, laid end to end along the dimension named above; an argument that names none is the same for every part. Nothing has to cross between parts.
All inputs are finite; a program needn't handle non-finite values. No bound on the sum of `lag_mask` on one device may be relied on, other than what follows from the above.
Results may differ from a plain program's by a relative error of at most 0.015.
Values may be sent and summed in bfloat16 or wider, within the bound.
No kernel may reach another device: no remote copies, remote signals or barrier semaphores. Data moves between devices by JAX's collectives and lax.ppermute only.
A program may use at most 64 MiB of HBM per device.

v0:
```python
import jax
import jax.numpy as jnp
from jax import lax
from jax.sharding import PartitionSpec as P

S = 2048
F = 1024
LAGS = 256
BLOCK = 32
CH_DEV = 64


def forward_table():
    freq_index = jnp.arange(F, dtype=jnp.int32)
    time_index = jnp.arange(S, dtype=jnp.int32)
    phase = freq_index[:, None] * time_index[None, :] % S
    angles = phase.astype(jnp.float32) * (2.0 * jnp.pi / S)
    scale = 1.0 / jnp.sqrt(jnp.float32(S))
    return jnp.stack(
        [
            (jnp.cos(angles) * scale).astype(jnp.bfloat16),
            (-jnp.sin(angles) * scale).astype(jnp.bfloat16),
        ],
        axis=1,
    )


def lag_table():
    freq_index = jnp.arange(F, dtype=jnp.int32)
    shifts = (jnp.arange(LAGS, dtype=jnp.int32) - LAGS // 2) % S
    phase = freq_index[:, None] * shifts[None, :] % S
    angles = phase.astype(jnp.float32) * (2.0 * jnp.pi / S)
    scale = 1.0 / jnp.sqrt(jnp.float32(F))
    return jnp.stack(
        [
            (jnp.cos(angles) * scale).astype(jnp.bfloat16),
            (-jnp.sin(angles) * scale).astype(jnp.bfloat16),
        ],
        axis=1,
    )


def synthesize(incoming, table):
    count = incoming.shape[-1]
    flat = incoming.reshape(2 * F, count)
    result = jnp.einsum(
        "qn,qt->tn", flat, table.reshape(2 * F, S), preferred_element_type=jnp.float32
    )
    return result.astype(jnp.bfloat16)


def on_device(records, pairs, observed, lag_mask):
    fibre_count = lax.axis_size("fibre")
    seg_count = lax.axis_size("seg")
    spread_count = fibre_count * seg_count
    freq_dev = F // spread_count
    blocks_dev = CH_DEV // BLOCK
    block_count = CH_DEV * spread_count // BLOCK
    pair_total = pairs.shape[0]
    pairs_dev = pair_total // spread_count
    table = forward_table()
    lags = lag_table()
    spans = records.reshape(1, S // fibre_count, fibre_count, CH_DEV)
    incoming = lax.all_to_all(spans, "fibre", split_axis=2, concat_axis=1, tiled=True)
    count = incoming.shape[3]
    signal = incoming.reshape(S, count)
    result = jnp.einsum(
        "qs,sn->qn", table.reshape(2 * F, S), signal, preferred_element_type=jnp.float32
    )
    spectra = result.reshape(F, 2, count).astype(jnp.bfloat16)
    widened = lax.all_to_all(spectra, ("fibre", "seg"), split_axis=0, concat_axis=2, tiled=True)
    seg_blocks = fibre_count * blocks_dev
    slot_ids = (
        pairs % seg_blocks // blocks_dev * seg_count + pairs // seg_blocks
    ) * blocks_dev + pairs % blocks_dev
    blocks_grid = widened.reshape(freq_dev, 2, block_count, BLOCK)
    first_side = jnp.take(blocks_grid, slot_ids[:, 0], axis=2).astype(jnp.float32)
    second_side = jnp.take(blocks_grid, slot_ids[:, 1], axis=2).astype(jnp.float32)
    first_re, first_im = (first_side[:, 0], first_side[:, 1])
    second_re, second_im = (second_side[:, 0], second_side[:, 1])
    cross_re = first_re * second_re + first_im * second_im
    cross_im = first_im * second_re - first_re * second_im
    cross_spec = jnp.stack([cross_re, cross_im], axis=1).astype(jnp.bfloat16)
    cross_spec = cross_spec.reshape(freq_dev, 2, spread_count, pairs_dev * BLOCK)
    owned_spec = lax.all_to_all(
        cross_spec, ("fibre", "seg"), split_axis=2, concat_axis=0, tiled=True
    )
    owned_spec = owned_spec.reshape(F, 2, pairs_dev * BLOCK)
    partial_corr = jnp.einsum("wpx,wpl->xl", owned_spec, lags, preferred_element_type=jnp.float32)
    synthetic = (
        lax.psum(partial_corr.astype(jnp.bfloat16), "rec")
        .astype(jnp.float32)
        .reshape(pairs_dev, BLOCK, LAGS)
    )
    weights = lag_mask[:, None, :].astype(jnp.float32) * jnp.tanh(synthetic - observed)
    weights_low = weights.astype(jnp.bfloat16).reshape(pairs_dev * BLOCK, LAGS)
    adjoint_spec = jnp.einsum("xl,wpl->wpx", weights_low, lags, preferred_element_type=jnp.float32)
    adjoint_spec = adjoint_spec.astype(jnp.bfloat16).reshape(F, 2, 1, pairs_dev * BLOCK)
    returned = lax.all_to_all(
        adjoint_spec, ("fibre", "seg"), split_axis=0, concat_axis=2, tiled=True
    )
    returned = returned.reshape(freq_dev, 2, pair_total, BLOCK).astype(jnp.float32)
    adjoint_re, adjoint_im = (returned[:, 0], returned[:, 1])
    grad_first = jnp.stack(
        [
            adjoint_re * second_re - adjoint_im * second_im,
            adjoint_re * second_im + adjoint_im * second_re,
        ],
        axis=1,
    )
    grad_second = jnp.stack(
        [
            adjoint_re * first_re + adjoint_im * first_im,
            adjoint_re * first_im - adjoint_im * first_re,
        ],
        axis=1,
    )
    contributions = jnp.concatenate([grad_first, grad_second], axis=2)
    endpoint_ids = jnp.concatenate([slot_ids[:, 0], slot_ids[:, 1]])
    summed = jax.ops.segment_sum(
        jnp.moveaxis(contributions, 2, 0), endpoint_ids, num_segments=block_count
    )
    block_adjoint = jnp.moveaxis(summed, 0, 2).astype(jnp.bfloat16)
    outgoing = block_adjoint.reshape(freq_dev, 2, spread_count, CH_DEV)
    sources = synthesize(
        lax.all_to_all(outgoing, ("fibre", "seg"), split_axis=2, concat_axis=0, tiled=True), table
    )
    regrouped = lax.all_to_all(sources, "fibre", split_axis=0, concat_axis=1, tiled=True)
    return regrouped[None]


def solution(mesh):
    in_specs = (
        P("rec", "fibre", ("groups", "seg")),
        P(),
        P(("groups", "fibre", "seg"), None, None),
        P(("groups", "fibre", "seg"), None),
    )
    out_specs = P("rec", "fibre", ("groups", "seg"))
    return jax.shard_map(
        on_device, mesh=mesh, in_specs=in_specs, out_specs=out_specs, check_vma=False
    )
```

profile of v0, /device:TPU:0, one launch (start us, length us, event | category | flops | bytes accessed | tf_op | source)
XLA Modules:
  0.0 163.2 jit_solution(8597783628842389983)
XLA Ops:
  0.0 1.8 %copy.59 = bf16[1,512,256]{1,2,0:T(8,128)(2,1)} copy(bf16[1,512,256]{2,1,0:T(8,128)(2,1)} %param.6) | data formatting | bytes 524288 | tf_op args[0]
  1.8 6.3 %all-to-all-start = ((bf16[1,512,4,64]{1,3,0,2:T(8,128)(2,1)}), bf16[1,512,4,64]{1,3,0,2:T(8,128)(2,1)S(1)}, u32[]{:S(2)}, u32[]{:S(2)}) async-start(bf16[1,512,4,64]{1,3,0,2:T(8,128)(2,1)} %bitcast.3), calls=%async_computation | async-start | bytes 524288 | tf_op jit(solution)/shard_map/all_to_all | solution.py:64
  8.1 35.0 %multiply_convert_fusion = (bf16[1024,1,2048]{2,0,1:T(8,128)(2,1)}, bf16[1024,1,2048]{2,0,1:T(8,128)(2,1)}) fusion(), kind=kLoop, calls=%fused_computation.10 | loop fusion | flops 39845888 | bytes 8388608 | tf_op jit(solution)/shard_map/convert_element_type | solution.py:22
  43.6 5.1 %convolution_convert_fusion.1 = bf16[1024,2,64]{0,2,1:T(8,128)(2,1)S(1)} fusion(bf16[2048,64,1]{0,1,2:T(8,128)(2,1)S(1)} %reshape.311, bf16[1024,1,2048]{2,0,1:T(8,128)(2,1)} %get-tuple-element.24, bf16[1024,1,2048]{2,0,1:T(8,128)(2,1)} %get-tuple-element.25), kind=kOutput, calls=%fused_computation.19 | convolution fusion | flops 541196288 | bytes 8912896 | tf_op jit(solution)/shard_map/qs,sn->qn/dot_general | solution.py:67
  49.1 1.1 reshape.316
  50.2 6.0 %all-to-all-start.1 = ((bf16[8,2,8192]{2,1,0:T(2,128)(2,1)}), bf16[8,2,8192]{2,1,0:T(2,128)(2,1)S(1)}, u32[]{:S(2)}, u32[]{:S(2)}) async-start(bf16[8,2,8192]{2,1,0:T(2,128)(2,1)} %reshape.316), calls=%async_computation.1 | async-start | bytes 524288 | tf_op jit(solution)/shard_map/all_to_all | solution.py:71
  56.2 8.4 %all-to-all-done.1 = bf16[8,2,8192]{2,1,0:T(2,128)(2,1)S(1)} async-done(((bf16[8,2,8192]{2,1,0:T(2,128)(2,1)}), bf16[8,2,8192]{2,1,0:T(2,128)(2,1)S(1)}, u32[]{:S(2)}, u32[]{:S(2)}) %all-to-all-start.1) | async-done | bytes 262176 | tf_op jit(solution)/shard_map/all_to_all | solution.py:71
  67.0 0.7 pad_maximum_fusion.4
  67.7 3.4 %all-to-all-start.2 = ((bf16[128,2,8,64]{0,3,1,2:T(8,128)(2,1)}), bf16[128,2,8,64]{0,3,1,2:T(8,128)(2,1)S(1)}, u32[]{:S(2)}, u32[]{:S(2)}) async-start(bf16[128,2,8,64]{0,3,1,2:T(8,128)(2,1)} %pad_maximum_fusion.4), calls=%async_computation.2 | async-start | bytes 524288 | tf_op jit(solution)/shard_map/all_to_all | solution.py:85
  71.2 4.5 %multiply_convert_fusion.3 = (bf16[1024,1,256]{2,0,1:T(8,128)(2,1)S(1)}, bf16[1024,1,256]{2,0,1:T(8,128)(2,1)S(1)}) fusion(s32[256]{0:T(256)S(1)} %and_select_fusion), kind=kLoop, calls=%fused_computation.30 | loop fusion | flops 4980736 | bytes 1049600 | tf_op jit(solution)/shard_map/convert_element_type | solution.py:36
  75.7 4.0 %all-to-all-done.2 = bf16[128,2,8,64]{0,3,1,2:T(8,128)(2,1)S(1)} async-done(((bf16[128,2,8,64]{0,3,1,2:T(8,128)(2,1)}), bf16[128,2,8,64]{0,3,1,2:T(8,128)(2,1)S(1)}, u32[]{:S(2)}, u32[]{:S(2)}) %all-to-all-start.2) | async-done | bytes 262176 | tf_op jit(solution)/shard_map/all_to_all | solution.py:85
  80.3 3.4 %psum.7 = bf16[2,32,256]{2,1,0:T(8,128)(2,1)S(1)} all-reduce(bf16[2,32,256]{2,1,0:T(8,128)(2,1)S(1)} %bitcast.121), channel_id=1, replica_groups=mesh['groups'=2,'fibre'=4,'seg'=2,'rec'=2] {'rec'}, use_global_device_ids=true, to_apply=%region_0.2 | all-reduce | flops 16384 | bytes 65536 | tf_op jit(solution)/shard_map/psum | solution.py:91
  84.6 1.1 reshape.318
  85.7 3.5 %all-to-all-start.3 = ((bf16[8,2,8192]{2,1,0:T(2,128)(2,1)}), bf16[8,2,8192]{2,1,0:T(2,128)(2,1)S(1)}, u32[]{:S(2)}, u32[]{:S(2)}) async-start(bf16[8,2,8192]{2,1,0:T(2,128)(2,1)} %reshape.318), calls=%async_computation.3 | async-start | bytes 524288 | tf_op jit(solution)/shard_map/all_to_all | solution.py:99
  89.2 9.5 %all-to-all-done.3 = bf16[8,2,8192]{2,1,0:T(2,128)(2,1)S(1)} async-done(((bf16[8,2,8192]{2,1,0:T(2,128)(2,1)}), bf16[8,2,8192]{2,1,0:T(2,128)(2,1)S(1)}, u32[]{:S(2)}, u32[]{:S(2)}) %all-to-all-start.3) | async-done | bytes 262176 | tf_op jit(solution)/shard_map/all_to_all | solution.py:99
  100.1 2.1 %scatter_fusion = f32[16,128,2,32]{1,3,2,0:T(8,128)S(1)} fusion(f32[16,128,2,32]{1,3,2,0:T(8,128)S(1)} %broadcast_in_dim.23, s32[32]{0:T(128)S(1)} %pad_add_fusion, f32[32,128,2,32]{1,3,2,0:T(8,128)S(1)} %maximum_bitcast_fusion), kind=kCustom, calls=%fused_computation.2 | custom fusion | flops 262144 | bytes 3145856 | tf_op jit(solution)/shard_map/scatter-add | solution.py:120
  102.3 0.7 copy.74
  103.0 3.6 %all-to-all-start.4 = ((bf16[128,2,8,64]{0,3,1,2:T(8,128)(2,1)}), bf16[128,2,8,64]{0,3,1,2:T(8,128)(2,1)S(1)}, u32[]{:S(2)}, u32[]{:S(2)}) async-start(bf16[128,2,8,64]{0,3,1,2:T(8,128)(2,1)} %copy.74), calls=%async_computation.4 | async-start | bytes 524288 | tf_op jit(solution)/shard_map/all_to_all | solution.py:126
  106.6 7.5 %pad_maximum_fusion = bf16[1024,2,2048]{2,0,1:T(8,128)(2,1)} fusion(bf16[1024,1,2048]{2,0,1:T(8,128)(2,1)} %get-tuple-element.24, bf16[1024,1,2048]{2,0,1:T(8,128)(2,1)} %get-tuple-element.25), kind=kLoop, calls=%fused_computation.9 | loop fusion | flops 4194304 | bytes 16777216 | tf_op jit(solution)/shard_map/stack | solution.py:19
  114.1 16.4 %copy.58 = bf16[1024,2,2048]{2,1,0:T(2,128)(2,1)} copy(bf16[1024,2,2048]{2,0,1:T(8,128)(2,1)} %pad_maximum_fusion) | data formatting | bytes 16777216 | tf_op jit(solution)/shard_map/stack | solution.py:19
  130.5 13.1 %reshape.267 = bf16[2048,2048]{1,0:T(8,128)(2,1)} reshape(bf16[1024,2,2048]{2,1,0:T(2,128)(2,1)} %copy.58) | data formatting | bytes 16777216 | tf_op jit(solution)/shard_map/reshape | solution.py:47
  144.0 5.0 %convolution_convert_fusion = bf16[2048,64]{0,1:T(8,128)(2,1)S(1)} fusion(bf16[2048,2048]{1,0:T(8,128)(2,1)} %reshape.267, bf16[2048,64]{1,0:T(8,128)(2,1)S(1)} %bitcast.106), kind=kOutput, calls=%fused_computation.15 | convolution fusion | flops 537001984 | bytes 8912896 | tf_op jit(solution)/shard_map/qn,qt->tn/dot_general | solution.py:46
  149.0 13.3 %all_to_all.85 = bf16[4,512,64]{1,2,0:T(8,128)(2,1)S(1)} all-to-all(bf16[4,512,64]{1,2,0:T(8,128)(2,1)S(1)} %bitcast.117), channel_id=1, replica_groups=mesh['groups'=2,'fibre'=4,'seg'=2,'rec'=2] {'fibre'}, dimensions={0} | all-to-all | bytes 524288 | tf_op jit(solution)/shard_map/all_to_all | solution.py:128
  162.4 0.8 copy.77
  (43 shorter events, 6.4 us)
Async XLA Ops:
  1.8 41.4 %all-to-all-start = ((bf16[1,512,4,64]{1,3,0,2:T(8,128)(2,1)}), bf16[1,512,4,64]{1,3,0,2:T(8,128)(2,1)S(1)}, u32[]{:S(2)}, u32[]{:S(2)}) async-start(bf16[1,512,4,64]{1,3,0,2:T(8,128)(2,1)} %bitcast.3), calls=%async_computation | async-start | bytes 524288 | tf_op jit(solution)/shard_map/all_to_all | solution.py:64
  43.6 12.6 %copy-start.2 = (s32[16,2]{0,1:T(2,128)S(1)}, s32[16,2]{0,1:T(2,128)}, u32[]{:S(2)}) copy-start(s32[16,2]{0,1:T(2,128)} %param.7) | copy-start | bytes 388
  48.6 22.5 %copy-start.1 = (s32[2,256]{1,0:T(2,128)S(1)}, s32[2,256]{1,0:T(2,128)}, u32[]{:S(2)}) copy-start(s32[2,256]{1,0:T(2,128)} %param.9) | copy-start | bytes 6148
  48.6 35.0 %copy-start = (f32[2,32,256]{2,1,0:T(8,128)S(1)}, f32[2,32,256]{2,1,0:T(8,128)}, u32[]{:S(2)}) copy-start(f32[2,32,256]{2,1,0:T(8,128)} %param.8) | copy-start | bytes 196612
  50.2 14.5 %all-to-all-start.1 = ((bf16[8,2,8192]{2,1,0:T(2,128)(2,1)}), bf16[8,2,8192]{2,1,0:T(2,128)(2,1)S(1)}, u32[]{:S(2)}, u32[]{:S(2)}) async-start(bf16[8,2,8192]{2,1,0:T(2,128)(2,1)} %reshape.316), calls=%async_computation.1 | async-start | bytes 524288 | tf_op jit(solution)/shard_map/all_to_all | solution.py:71
  67.7 12.0 %all-to-all-start.2 = ((bf16[128,2,8,64]{0,3,1,2:T(8,128)(2,1)}), bf16[128,2,8,64]{0,3,1,2:T(8,128)(2,1)S(1)}, u32[]{:S(2)}, u32[]{:S(2)}) async-start(bf16[128,2,8,64]{0,3,1,2:T(8,128)(2,1)} %pad_maximum_fusion.4), calls=%async_computation.2 | async-start | bytes 524288 | tf_op jit(solution)/shard_map/all_to_all | solution.py:85
  85.7 13.1 %all-to-all-start.3 = ((bf16[8,2,8192]{2,1,0:T(2,128)(2,1)}), bf16[8,2,8192]{2,1,0:T(2,128)(2,1)S(1)}, u32[]{:S(2)}, u32[]{:S(2)}) async-start(bf16[8,2,8192]{2,1,0:T(2,128)(2,1)} %reshape.318), calls=%async_computation.3 | async-start | bytes 524288 | tf_op jit(solution)/shard_map/all_to_all | solution.py:99
  103.0 40.6 %all-to-all-start.4 = ((bf16[128,2,8,64]{0,3,1,2:T(8,128)(2,1)}), bf16[128,2,8,64]{0,3,1,2:T(8,128)(2,1)S(1)}, u32[]{:S(2)}, u32[]{:S(2)}) async-start(bf16[128,2,8,64]{0,3,1,2:T(8,128)(2,1)} %copy.74), calls=%async_computation.4 | async-start | bytes 524288 | tf_op jit(solution)/shard_map/all_to_all | solution.py:126
where the time goes:
time: 164 us; the launch traced here: 163 us
  other arithmetic  50.7 us (31%)
  local copies, waits for them, and re-layouts  39.9 us (24%)
  starting transfers between devices  22.9 us (14%)
  waiting for transfers between devices  21.9 us (13%)
  blocking collectives  16.7 us (10%)
  matrix products  10.8 us (7%)
    convert_element_type x1, other arithmetic, forward_table(): (-jnp.sin(angles) * scale).astype(jnp.bfloat16)  35 us
    another operation x1, local copies, waits for them, and re-layouts, forward_table(): jnp.stack([(jnp.cos(angles) * scale).astype(jnp.bfloat16), (-jnp.sin(angl...  16.4 us
    all_to_all x1, blocking collectives, on_device(): lax.all_to_all(sources, 'fibre', split_axis=0, concat_axis=1, tiled=True)  13.3 us
    reshape x1, local copies, waits for them, and re-layouts, synthesize(): table.reshape(2 * F, S)  13.1 us
    all_to_all x1, waiting for transfers between devices, on_device(): lax.all_to_all(adjoint_spec, ('fibre', 'seg'), split_axis=0, concat_axis=...  9.49 us
    all_to_all x1, waiting for transfers between devices, on_device(): lax.all_to_all(spectra, ('fibre', 'seg'), split_axis=0, concat_axis=2, ti...  8.44 us
    another operation x1, other arithmetic, forward_table(): jnp.stack([(jnp.cos(angles) * scale).astype(jnp.bfloat16), (-jnp.sin(angl...  7.45 us
    all_to_all x1, starting transfers between devices, on_device(): lax.all_to_all(spans, 'fibre', split_axis=2, concat_axis=1, tiled=True)  6.32 us
  transfers between devices with their start and end apart: 5, of which 3 were waited for; matrix products, arithmetic and copies ran while one was open for 47% of the time, Pallas kernels for 0%

commit v1 on v0

v1 whole, which is shorter than its diff:
```python
import functools

import jax
import jax.numpy as jnp
import numpy as np
from jax import lax
from jax.experimental import pallas as pl
from jax.experimental.pallas import tpu as pltpu
from jax.sharding import PartitionSpec as P

S = 2048
F = 1024
LAGS = 256
BLOCK = 32
SPANS = 4
MASKED = 16384.0
LANES = 128
EVERY = ("fibre", "seg", "rec")

_NT = (((1,), (1,)), ((), ()))
_TN = (((0,), (0,)), ((), ()))


def wave_table(freq, shift, scale):
    phase = freq[:, None].astype(np.int64) * shift[None, :] % S
    angles = phase.astype(np.float32) * np.float32(2.0 * np.pi / S)
    factor = np.float32(1.0) / np.sqrt(np.float32(scale))
    parts = [(np.cos(angles) * factor), (-np.sin(angles) * factor)]
    return np.stack(parts, axis=1).astype(jnp.bfloat16)


def forward_table():
    return wave_table(np.arange(F), np.arange(S), S)


def lag_table():
    return wave_table(np.arange(F), (np.arange(LAGS) - LAGS // 2) % S, F)


def dot(a, b, dims=(((1,), (0,)), ((), ()))):
    return lax.dot_general(a, b, dims, preferred_element_type=jnp.float32)


def one_hot(rows, cols, hit):
    row = lax.broadcasted_iota(jnp.int32, (rows, cols), 0)
    col = lax.broadcasted_iota(jnp.int32, (rows, cols), 1)
    return jnp.where(hit(row, col), 1.0, 0.0).astype(jnp.bfloat16)


def channel_of(row, blocks, own):
    return row % (blocks * own) // own * BLOCK + row // (blocks * own) * own + row % own


def pack_kernel(blocks, own, records_ref, observed_ref, mask_ref, out_ref):
    count = records_ref.shape[1]
    span = records_ref.shape[0]
    dests = BLOCK // own
    rows = blocks * own
    order = one_hot(count, count, lambda r, c: c == channel_of(r, blocks, own))
    moved = dot(order, records_ref[...], _NT).astype(jnp.bfloat16)
    out_ref[:, :, 0:span] = moved.reshape(dests, rows, span)
    pair_rows = observed_ref.shape[0]
    seen = jnp.where(mask_ref[...] != 0, observed_ref[...], MASKED)
    high = seen.astype(jnp.bfloat16)
    low = (seen - high.astype(jnp.float32)).astype(jnp.bfloat16)
    halves = LAGS // LANES
    parts = [v[:, h * LANES : (h + 1) * LANES] for v in (high, low) for h in range(halves)]
    stacked = jnp.concatenate(parts, axis=0)
    place = one_hot(
        count,
        stacked.shape[0],
        lambda r, c: (c % pair_rows // own == r // rows)
        & (c // pair_rows * own + c % own == r % rows),
    )
    packed = dot(place, stacked).astype(jnp.bfloat16)
    out_ref[:, :, span:] = packed.reshape(dests, rows, LANES)


def unpack_kernel(blocks, own, rows_ref, out_ref):
    count = out_ref.shape[1]
    order = one_hot(count, count, lambda r, c: c == channel_of(r, blocks, own))
    held = rows_ref[...].reshape(count, rows_ref.shape[2])
    out_ref[...] = dot(held, order, _TN).astype(jnp.bfloat16)


def main_kernel(segs, recs, blocks, own, pairs_ref, rows_ref, table_ref, lag_ref, out_ref):
    pair_total = pairs_ref.shape[0]
    span = S // SPANS
    band = F // SPANS
    count = segs * recs * blocks * own
    lines = pair_total * own
    every = recs * lines
    ways = segs * recs
    folds = [
        rows_ref[f * ways : (f + 1) * ways, :, 0:span].reshape(count, span).astype(jnp.float32)
        for f in range(SPANS)
    ]
    even, odd = folds[0] + folds[2], folds[1] + folds[3]
    e_part, d_part = folds[0] - folds[2], folds[1] - folds[3]
    both = jnp.concatenate([e_part, d_part], axis=0).astype(jnp.bfloat16)
    spectra = []
    for j in range(SPANS):
        if j % 2 == 0:
            signal = even + odd if j == 0 else even - odd
            part = dot(signal.astype(jnp.bfloat16), table_ref[j])
        else:
            mixed = dot(both, table_ref[j])
            e_c, e_s = mixed[:count, :band], mixed[:count, band:]
            d_c, d_s = mixed[count:, :band], mixed[count:, band:]
            sign = 1.0 if j == 1 else -1.0
            part = jnp.concatenate([e_c + sign * d_s, e_s - sign * d_c], axis=1)
        spectra.append(part.astype(jnp.bfloat16))

    def row_of(line, block):
        record, k = line // lines, line % own
        return ((block // blocks * recs + record) * blocks + block % blocks) * own + k

    def picks(side, line):
        pair = line % lines // own
        block = jnp.zeros_like(line)
        for n in range(pair_total):
            block = jnp.where(pair == n, pairs_ref[n, side], block)
        return row_of(line, block)

    take, give = [], []
    for side in range(2):
        line = lax.broadcasted_iota(jnp.int32, (every, count), 0)
        row = lax.broadcasted_iota(jnp.int32, (every, count), 1)
        take.append(jnp.where(picks(side, line) == row, 1.0, 0.0).astype(jnp.bfloat16))
        line = lax.broadcasted_iota(jnp.int32, (count, every), 1)
        row = lax.broadcasted_iota(jnp.int32, (count, every), 0)
        give.append(jnp.where(picks(side, line) == row, 1.0, 0.0).astype(jnp.bfloat16))
    take = jnp.concatenate(take, axis=0)
    give = jnp.concatenate(give + give, axis=1)

    sides = []
    total = None
    for j in range(SPANS):
        chosen = dot(take, spectra[j])
        a0, a1 = chosen[:every, :band], chosen[:every, band:]
        b0, b1 = chosen[every:, :band], chosen[every:, band:]
        sides.append((a0, a1, b0, b1))
        cross = jnp.concatenate([a0 * b0 + a1 * b1, a1 * b0 - a0 * b1], axis=1)
        term = dot(cross.astype(jnp.bfloat16), lag_ref[j])
        total = term if total is None else total + term
    synthetic = total[:lines]
    for r in range(1, recs):
        synthetic = synthetic + total[r * lines : (r + 1) * lines]

    halves = LAGS // LANES
    packed = rows_ref[:, :, span:].reshape(count * SPANS, LANES)
    rows = blocks * own
    seen = []
    for h in range(halves):
        find = one_hot(
            lines,
            packed.shape[0],
            lambda q, c: (q // own == c // rows)
            & ((c % rows == h * own + q % own) | (c % rows == (halves + h) * own + q % own)),
        )
        seen.append(dot(find, packed))
    seen = jnp.concatenate(seen, axis=1)
    weights = jnp.where(seen < 0.5 * MASKED, jnp.tanh(synthetic - seen), 0.0).astype(jnp.bfloat16)

    even, odd = None, None
    for j in range(SPANS):
        a0, a1, b0, b1 = sides[j]
        adjoint = dot(weights, lag_ref[j], _NT).astype(jnp.bfloat16).astype(jnp.float32)
        adjoint = jnp.concatenate([adjoint] * recs, axis=0)
        g0, g1 = adjoint[:, :band], adjoint[:, band:]
        first = jnp.concatenate([g0 * b0 - g1 * b1, g0 * b1 + g1 * b0], axis=1)
        second = jnp.concatenate([g0 * a0 + g1 * a1, g0 * a1 - g1 * a0], axis=1)
        terms = jnp.concatenate([first, second], axis=0)
        high = terms.astype(jnp.bfloat16)
        low = (terms - high.astype(jnp.float32)).astype(jnp.bfloat16)
        grad = dot(give, jnp.concatenate([high, low], axis=0))
        if j % 2 == 0:
            part = dot(grad.astype(jnp.bfloat16), table_ref[j], _NT)
            even = (part, part) if j == 0 else (even[0] + part, even[1] - part)
        else:
            turned = jnp.concatenate([-grad[:, band:], grad[:, :band]], axis=1)
            stacked = jnp.concatenate([grad, turned], axis=0).astype(jnp.bfloat16)
            part = dot(stacked, table_ref[j], _NT)
            u, v = part[:count], part[count:]
            odd = (u, v) if j == 1 else (odd[0] + u, odd[1] - v)
    rows = blocks * own
    for f in range(SPANS):
        base, side = even[f % 2], odd[f % 2]
        value = base + side if f < 2 else base - side
        out_ref[f * ways : (f + 1) * ways, :, :] = value.astype(jnp.bfloat16).reshape(ways, rows, span)


def by_own_k(records, pairs, observed, lag_mask):
    fibres, segs, recs = (lax.axis_size(a) for a in EVERY)
    devices = fibres * segs * recs
    own = BLOCK // devices
    span, count = records.shape[1:]
    blocks = count // BLOCK
    rows = blocks * own
    pairs_dev = observed.shape[0]
    share = pairs_dev // recs
    part = lax.axis_index("rec") * share
    observed = lax.dynamic_slice_in_dim(observed, part, share, 0).reshape(share * BLOCK, LAGS)
    lag_mask = lax.dynamic_slice_in_dim(lag_mask, part, share, 0)
    table = forward_table().reshape(F // SPANS, SPANS, 2, SPANS, span)[:, :, :, 0]
    table = np.ascontiguousarray(table.transpose(1, 3, 2, 0)).reshape(SPANS, span, S // SPANS)
    lags = lag_table().reshape(F // SPANS, SPANS, 2, LAGS)
    lags = np.ascontiguousarray(lags.transpose(1, 2, 0, 3)).reshape(SPANS, S // SPANS, LAGS)
    vmem = pl.BlockSpec(memory_space=pltpu.VMEM)
    send = pl.pallas_call(
        functools.partial(pack_kernel, blocks, own),
        out_shape=jax.ShapeDtypeStruct((devices, rows, span + LANES), jnp.bfloat16),
        in_specs=[vmem] * 3,
        out_specs=vmem,
    )(records[0], observed, lag_mask)
    held = lax.all_to_all(send, EVERY, 0, 0, tiled=True)
    back = pl.pallas_call(
        functools.partial(main_kernel, segs, recs, blocks, own),
        out_shape=jax.ShapeDtypeStruct((devices, rows, span), jnp.bfloat16),
        in_specs=[pl.BlockSpec(memory_space=pltpu.SMEM)] + [vmem] * 3,
        out_specs=vmem,
        compiler_params=pltpu.CompilerParams(vmem_limit_bytes=48 * 2**20),
    )(pairs, held, jnp.asarray(table), jnp.asarray(lags))
    mine = lax.all_to_all(back, EVERY, 0, 0, tiled=True)
    out = pl.pallas_call(
        functools.partial(unpack_kernel, blocks, own),
        out_shape=jax.ShapeDtypeStruct((span, count), jnp.bfloat16),
        in_specs=[vmem],
        out_specs=vmem,
    )(mine)
    return out[None]


def by_band(records, pairs, observed, lag_mask):
    fibres, segs = lax.axis_size("fibre"), lax.axis_size("seg")
    own = BLOCK // fibres
    span, count = records.shape[1:]
    blocks = count // BLOCK
    total_blocks = blocks * segs
    pair_total, pairs_dev = pairs.shape[0], observed.shape[0]
    low = jnp.bfloat16
    band = F // segs
    start = lax.axis_index("seg") * band
    table = lax.dynamic_slice_in_dim(jnp.asarray(forward_table()), start, band, 0)
    lags = lax.dynamic_slice_in_dim(jnp.asarray(lag_table()), start, band, 0)
    f32 = functools.partial(jnp.einsum, preferred_element_type=jnp.float32)
    grid = records.reshape(span, blocks, fibres, own).transpose(2, 0, 1, 3)
    signal = lax.all_to_all(grid, "fibre", 0, 0, tiled=True).reshape(S, blocks, own)
    signal = lax.all_gather(signal, "seg", axis=1, tiled=True)
    spectra = f32("wpt,tbk->wpbk", table, signal).astype(low)
    ids = jnp.arange(total_blocks)
    take = [(pairs[:, side, None] == ids).astype(low) for side in range(2)]
    a0, a1 = (f32("nb,wbk->wnk", take[0], spectra[:, p]) for p in range(2))
    b0, b1 = (f32("nb,wbk->wnk", take[1], spectra[:, p]) for p in range(2))
    cross = jnp.stack([a0 * b0 + a1 * b1, a1 * b0 - a0 * b1], axis=1).astype(low)
    corr = f32("wpnk,wpl->nkl", cross, lags)
    corr = corr.reshape(fibres, segs, pairs_dev, own, LAGS)
    corr = lax.psum_scatter(corr, "seg", scatter_dimension=1)
    synthetic = lax.psum(corr, "rec").reshape(fibres * pairs_dev, own, LAGS)
    seen = observed.reshape(pairs_dev, fibres, own, LAGS).transpose(1, 0, 2, 3)
    seen = lax.all_to_all(seen, "fibre", 0, 0, tiled=True).reshape(fibres * pairs_dev, own, LAGS)
    window = lax.all_gather(lag_mask.astype(jnp.float32), "fibre", axis=0, tiled=True)
    weights = (window[:, None, :] * jnp.tanh(synthetic - seen)).astype(low)
    weights = lax.all_gather(weights.reshape(fibres, pairs_dev, own, LAGS), "seg", axis=1)
    weights = weights.reshape(pair_total, own, LAGS)
    adjoint = f32("nkl,wpl->wpnk", weights, lags).astype(low).astype(jnp.float32)
    g0, g1 = adjoint[:, 0], adjoint[:, 1]

    def added(side, terms):
        high = terms.astype(low)
        rest = (terms - high.astype(jnp.float32)).astype(low)
        return f32("nb,wnk->wbk", take[side], high) + f32("nb,wnk->wbk", take[side], rest)

    grad = jnp.stack(
        [
            added(0, g0 * b0 - g1 * b1) + added(1, g0 * a0 + g1 * a1),
            added(0, g0 * b1 + g1 * b0) + added(1, g0 * a1 - g1 * a0),
        ],
        axis=1,
    ).astype(low)
    sources = f32("wpbk,wpt->tbk", grad, table)
    sources = lax.psum_scatter(sources, "seg", scatter_dimension=1, tiled=True).astype(low)
    sources = sources.reshape(fibres, span, blocks, own)
    sources = lax.all_to_all(sources, "fibre", 0, 0, tiled=True)
    return sources.transpose(1, 2, 0, 3).reshape(1, span, count)


def solution(mesh):
    devices = mesh.shape["fibre"] * mesh.shape["seg"] * mesh.shape["rec"]
    in_specs = (
        P("rec", "fibre", ("groups", "seg")),
        P(),
        P(("groups", "fibre", "seg"), None, None),
        P(("groups", "fibre", "seg"), None),
    )
    out_specs = P("rec", "fibre", ("groups", "seg"))
    small = mesh.shape["fibre"] == SPANS and BLOCK % devices == 0
    return jax.shard_map(
        by_own_k if small else by_band,
        mesh=mesh,
        in_specs=in_specs,
        out_specs=out_specs,
        check_vma=False,
    )
```

time: 164 us -> 45.2 us (0.28)
  other arithmetic: 50.7 us -> 0 us
  local copies, waits for them, and re-layouts: 39.9 us -> 6.25 us
  starting transfers between devices: 22.9 us -> 7.36 us
  waiting for transfers between devices: 21.9 us -> 10.3 us
  matrix products: 10.8 us -> 0 us
  Pallas kernels: 0 us -> 7.46 us
  blocking collectives: 16.7 us -> 13.3 us
    convert_element_type x8 -> x0, other arithmetic: 39.8 us -> none  [the longest x1 35 us: forward_table(): (-jnp.sin(angles) * scale).astype(jnp.bfloat16)]
    another operation x1 -> x0, local copies, waits for them, and re-layouts: 16.4 us -> none  [forward_table(): jnp.stack([(jnp.cos(angles) * scale).astype(jnp.bfloat16), (-jnp.sin(angl...]
    all_to_all x5 -> x1, starting transfers between devices: 22.9 us -> 7.36 us  [by_own_k(): held = lax.all_to_all(send, EVERY, 0, 0, tiled=True)]
    reshape x5 -> x1, local copies, waits for them, and re-layouts: 14.5 us -> 0.62 us  [by_own_k(): lax.dynamic_slice_in_dim(observed, part, share, 0)]
    all_to_all x5 -> x1, waiting for transfers between devices: 21.9 us -> 10.3 us  [by_own_k(): held = lax.all_to_all(send, EVERY, 0, 0, tiled=True)]
    dot_general x4 -> x0, matrix products: 10.8 us -> none  [the longest x1 5.06 us: on_device(): jnp.einsum('qs,sn->qn', table.reshape(2 * F, S), signal, preferred_elemen...]
    another operation x3 -> x0, other arithmetic: 8.29 us -> none  [the longest x1 7.45 us: forward_table(): jnp.stack([(jnp.cos(angles) * scale).astype(jnp.bfloat16), (-jnp.sin(angl...]
    pallas_call x0 -> x3, Pallas kernels: none -> 7.46 us  [the longest x1 3.57 us: by_own_k(): pl.pallas_call(functools.partial(main_kernel, segs, recs, blocks, own), o...]
  transfers between devices with their start and end apart: 5 -> 1, of which waited for: 3 -> 1; matrix products, arithmetic and copies ran while one was open for 47% -> 2% of each run, Pallas kernels for 0% -> 0%
where the time goes in v1:
time: 45.2 us; the launch traced here: 44.8 us
  blocking collectives  13.3 us (29%)
  waiting for transfers between devices  10.3 us (23%)
  Pallas kernels  7.46 us (17%)
  starting transfers between devices  7.36 us (16%)
  local copies, waits for them, and re-layouts  6.25 us (14%)
    all_to_all x1, blocking collectives, by_own_k(): mine = lax.all_to_all(back, EVERY, 0, 0, tiled=True)  13.3 us
    all_to_all x1, waiting for transfers between devices, by_own_k(): held = lax.all_to_all(send, EVERY, 0, 0, tiled=True)  10.3 us
    all_to_all x1, starting transfers between devices, by_own_k(): held = lax.all_to_all(send, EVERY, 0, 0, tiled=True)  7.36 us
    unnamed x7, local copies, waits for them, and re-layouts  4.41 us
    pallas_call x1, Pallas kernels, by_own_k(): pl.pallas_call(functools.partial(main_kernel, segs, recs, blocks, own), o...  3.57 us
    pallas_call x1, Pallas kernels, by_own_k(): pl.pallas_call(functools.partial(pack_kernel, blocks, own), out_shape=jax...  1.97 us
    pallas_call x1, Pallas kernels, by_own_k(): pl.pallas_call(functools.partial(unpack_kernel, blocks, own), out_shape=j...  1.92 us
    dynamic_slice x1, local copies, waits for them, and re-layouts, by_own_k(): lag_mask = lax.dynamic_slice_in_dim(lag_mask, part, share, 0)  1.22 us
  transfers between devices with their start and end apart: 1, of which 1 were waited for; matrix products, arithmetic and copies ran while one was open for 2% of the time, Pallas kernels for 0%

profile of v1, /device:TPU:0, one launch (start us, length us, event | category | flops | bytes accessed | tf_op | source)
XLA Modules:
  0.0 44.8 jit_solution(11240932591432306192)
XLA Ops:
  0.0 0.0 copy-start
  0.0 0.8 %copy-done = f32[2,32,256]{2,1,0:T(8,128)S(1)} copy-done((f32[2,32,256]{2,1,0:T(8,128)S(1)}, f32[2,32,256]{2,1,0:T(8,128)}, u32[]{:S(2)}) %copy-start) | copy-done | bytes 65560
  0.8 0.6 %dynamic-slice_bitcast_fusion.observed_ref = f32[32,256]{1,0:T(8,128)} fusion(f32[2,32,256]{2,1,0:T(8,128)S(1)} %copy-done, s32[]{:T(128)S(6)} %select_n.4), kind=kLoop, calls=%fused_computation | loop fusion | bytes 65540 | tf_op jit(solution)/shard_map/reshape | solution.py:203
  1.5 1.2 %constant_dynamic-slice_fusion.mask_ref = s32[1,256]{1,0:T(1,128)} fusion(s32[2,256]{1,0:T(2,128)} %param.9, s32[]{:T(128)S(6)} %select_n.4), kind=kLoop, calls=%fused_computation.1 | loop fusion | bytes 2052 | tf_op jit(solution)/shard_map/dynamic_slice | solution.py:204
  2.7 2.0 %shard_map.64 = bf16[16,16,640]{2,1,0:T(8,128)(2,1)} custom-call(bf16[512,256]{1,0:T(8,128)(2,1)} %bitcast.4, f32[32,256]{1,0:T(8,128)} %dynamic-slice_bitcast_fusion.observed_ref, s32[1,256]{1,0:T(1,128)} %constant_dynamic-slice_fusion.mask_ref), custom_call_target="tpu_custom_call" | custom-call | tf_op jit(solution)/shard_map/pallas_call | solution.py:210
  4.7 7.4 %all-to-all-start = ((bf16[16,16,640]{2,1,0:T(8,128)(2,1)}), bf16[16,16,640]{2,1,0:T(8,128)(2,1)S(1)}, u32[]{:S(2)}, u32[]{:S(2)}) async-start(bf16[16,16,640]{2,1,0:T(8,128)(2,1)} %shard_map.64), calls=%async_computation | async-start | bytes 655360 | tf_op jit(solution)/shard_map/all_to_all | solution.py:216
  12.0 0.8 %copy.7.pairs_ref = s32[16,2]{1,0:T(8,128)S(1)} copy(s32[16,2]{0,1:T(2,128)} %param.7) | data formatting | bytes 256 | tf_op args[1]
  12.8 10.3 %all-to-all-done.rows_ref = bf16[16,16,640]{2,1,0:T(8,128)(2,1)S(1)} async-done(((bf16[16,16,640]{2,1,0:T(8,128)(2,1)}), bf16[16,16,640]{2,1,0:T(8,128)(2,1)S(1)}, u32[]{:S(2)}, u32[]{:S(2)}) %all-to-all-start) | async-done | bytes 327712 | tf_op jit(solution)/shard_map/all_to_all | solution.py:216
  23.1 0.0 copy-start.1
  23.1 1.6 %copy-done.1 = bf16[4,512,512]{2,1,0:T(8,128)(2,1)S(1)} copy-done((bf16[4,512,512]{2,1,0:T(8,128)(2,1)S(1)}, bf16[4,512,512]{2,1,0:T(8,128)(2,1)}, u32[]{:S(2)}) %copy-start.1) | copy-done | bytes 2097176
  24.7 0.0 copy-start.2
  24.7 1.2 %copy-done.2 = bf16[4,512,256]{2,1,0:T(8,128)(2,1)S(1)} copy-done((bf16[4,512,256]{2,1,0:T(8,128)(2,1)S(1)}, bf16[4,512,256]{2,1,0:T(8,128)(2,1)}, u32[]{:S(2)}) %copy-start.2) | copy-done | bytes 1048600
  25.9 3.6 %shard_map.65 = bf16[16,16,512]{2,1,0:T(8,128)(2,1)S(1)} custom-call(s32[16,2]{1,0:T(8,128)S(1)} %copy.7.pairs_ref, bf16[16,16,640]{2,1,0:T(8,128)(2,1)S(1)} %all-to-all-done.rows_ref, bf16[4,512,512]{2,1,0:T(8,128)(2,1)S(1)} %copy-done.1, bf16[4,512,256]{2,1,0:T(8,128)(2,1)S(1)} %copy-done.2), custom_call_target="tpu_custom_call" | custom-call | tf_op jit(solution)/shard_map/pallas_call | solution.py:217
  29.5 13.3 %all_to_all.10.rows_ref = bf16[16,16,512]{2,1,0:T(8,128)(2,1)} all-to-all(bf16[16,16,512]{2,1,0:T(8,128)(2,1)S(1)} %shard_map.65), channel_id=1, replica_groups=mesh['groups'=2,'fibre'=4,'seg'=2,'rec'=2] {'fibre','seg','rec'}, dimensions={0} | all-to-all | bytes 524288 | tf_op jit(solution)/shard_map/all_to_all | solution.py:224
  42.8 1.9 %shard_map.66 = bf16[512,256]{1,0:T(8,128)(2,1)} custom-call(bf16[16,16,512]{2,1,0:T(8,128)(2,1)} %all_to_all.10.rows_ref), custom_call_target="tpu_custom_call" | custom-call | tf_op jit(solution)/shard_map/pallas_call | solution.py:225
Async XLA Ops:
  0.0 0.8 %copy-start = (f32[2,32,256]{2,1,0:T(8,128)S(1)}, f32[2,32,256]{2,1,0:T(8,128)}, u32[]{:S(2)}) copy-start(f32[2,32,256]{2,1,0:T(8,128)} %param.8) | copy-start | bytes 196612
  4.7 18.5 %all-to-all-start = ((bf16[16,16,640]{2,1,0:T(8,128)(2,1)}), bf16[16,16,640]{2,1,0:T(8,128)(2,1)S(1)}, u32[]{:S(2)}, u32[]{:S(2)}) async-start(bf16[16,16,640]{2,1,0:T(8,128)(2,1)} %shard_map.64), calls=%async_computation | async-start | bytes 655360 | tf_op jit(solution)/shard_map/all_to_all | solution.py:216
  23.1 1.6 %copy-start.1 = (bf16[4,512,512]{2,1,0:T(8,128)(2,1)S(1)}, bf16[4,512,512]{2,1,0:T(8,128)(2,1)}, u32[]{:S(2)}) copy-start(bf16[4,512,512]{2,1,0:T(8,128)(2,1)} %constant.12.clone.table_ref) | copy-start | bytes 6291460
  24.7 1.2 %copy-start.2 = (bf16[4,512,256]{2,1,0:T(8,128)(2,1)S(1)}, bf16[4,512,256]{2,1,0:T(8,128)(2,1)}, u32[]{:S(2)}) copy-start(bf16[4,512,256]{2,1,0:T(8,128)(2,1)} %constant.13.clone.lag_ref) | copy-start | bytes 3145732

commit v2 on v1

--- a/solution.py
+++ b/solution.py
@@ -51,54 +51,138 @@
     return row % (blocks * own) // own * BLOCK + row // (blocks * own) * own + row % own
 
 
-def pack_kernel(blocks, own, records_ref, observed_ref, mask_ref, out_ref):
-    count = records_ref.shape[1]
-    span = records_ref.shape[0]
+def pack_kernel(blocks, own, records_hbm, observed_hbm, mask_hbm, out_ref, records, observed, mask, sems):
+    span, count = records.shape
     dests = BLOCK // own
     rows = blocks * own
+    tiles = span // LANES
+    share = observed.shape[0]
+    start = lax.axis_index("rec") * share
+    seen_copy = pltpu.make_async_copy(observed_hbm.at[pl.ds(start, share)], observed, sems.at[0])
+    mask_copy = pltpu.make_async_copy(mask_hbm, mask, sems.at[1])
+    copies = [
+        pltpu.make_async_copy(
+            records_hbm.at[pl.ds(q * LANES, LANES)], records.at[pl.ds(q * LANES, LANES)], sems.at[2 + q]
+        )
+        for q in range(tiles)
+    ]
+    for copy in [seen_copy, mask_copy] + copies:
+        copy.start()
     order = one_hot(count, count, lambda r, c: c == channel_of(r, blocks, own))
-    moved = dot(order, records_ref[...], _NT).astype(jnp.bfloat16)
-    out_ref[:, :, 0:span] = moved.reshape(dests, rows, span)
-    pair_rows = observed_ref.shape[0]
-    seen = jnp.where(mask_ref[...] != 0, observed_ref[...], MASKED)
+    lines = share * BLOCK
+    halves = LAGS // LANES
+    extra = 2 * halves * share * own
+    place = one_hot(
+        dests * extra,
+        2 * halves * lines,
+        lambda r, c: (c % BLOCK // own == r // extra)
+        & (c // BLOCK * own + c % own == r % extra),
+    )
+    seen_copy.wait()
+    mask_copy.wait()
+    window = jnp.concatenate(
+        [mask[pl.ds(start + i, 1), :] + jnp.zeros((BLOCK, 1), jnp.int32) for i in range(share)], axis=0
+    )
+    seen = jnp.where(window != 0, observed[...].reshape(lines, LAGS), MASKED)
     high = seen.astype(jnp.bfloat16)
     low = (seen - high.astype(jnp.float32)).astype(jnp.bfloat16)
+    parts = [v[:, h * LANES : (h + 1) * LANES] for v in (high, low) for h in range(halves)]
+    packed = dot(place, jnp.concatenate(parts, axis=0)).astype(jnp.bfloat16)
+    out_ref[:, tiles * rows :, :] = packed.reshape(dests, extra, LANES)
+    for q, copy in enumerate(copies):
+        copy.wait()
+        moved = dot(order, records[q * LANES : (q + 1) * LANES, :], _NT).astype(jnp.bfloat16)
+        out_ref[:, q * rows : (q + 1) * rows, :] = moved.reshape(dests, rows, LANES)
+
+
+def prepare_kernel(
+    segs, recs, blocks, own, after_ref, pairs_ref, table_hbm, lag_hbm, table_ref, lag_ref, take_ref, give_ref, find_ref, order_ref, sems
+):
+    copies = [
+        pltpu.make_async_copy(table_hbm, table_ref, sems.at[0]),
+        pltpu.make_async_copy(lag_hbm, lag_ref, sems.at[1]),
+    ]
+    for copy in copies:
+        copy.start()
+    pair_total = pairs_ref.shape[0]
+    count = segs * recs * blocks * own
+    lines = pair_total * own
+    every = recs * lines
+
+    def picks(side, line):
+        pair = line % lines // own
+        block = jnp.zeros_like(line)
+        for n in range(pair_total):
+            block = jnp.where(pair == n, pairs_ref[n, side], block)
+        return ((block // blocks * recs + line // lines) * blocks + block % blocks) * own + line % own
+
+    for side in range(2):
+        line = lax.broadcasted_iota(jnp.int32, (every, count), 0)
+        row = lax.broadcasted_iota(jnp.int32, (every, count), 1)
+        hit = jnp.where(picks(side, line) == row, 1.0, 0.0).astype(jnp.bfloat16)
+        take_ref[side * every : (side + 1) * every, :] = hit
+        line = lax.broadcasted_iota(jnp.int32, (count, 2 * every), 1)
+        row = lax.broadcasted_iota(jnp.int32, (count, 2 * every), 0)
+        hit = jnp.where(picks(side, line % every) == row, 1.0, 0.0)
+        if side == 0:
+            first = hit
+        else:
+            hit = jnp.where(line < every, first, hit).astype(jnp.bfloat16)
+            give_ref[:, 0 : 2 * every] = hit
+            give_ref[:, 2 * every :] = hit
     halves = LAGS // LANES
-    parts = [v[:, h * LANES : (h + 1) * LANES] for v in (high, low) for h in range(halves)]
-    stacked = jnp.concatenate(parts, axis=0)
-    place = one_hot(
-        count,
-        stacked.shape[0],
-        lambda r, c: (c % pair_rows // own == r // rows)
-        & (c // pair_rows * own + c % own == r % rows),
-    )
-    packed = dot(place, stacked).astype(jnp.bfloat16)
-    out_ref[:, :, span:] = packed.reshape(dests, rows, LANES)
-
-
-def unpack_kernel(blocks, own, rows_ref, out_ref):
-    count = out_ref.shape[1]
-    order = one_hot(count, count, lambda r, c: c == channel_of(r, blocks, own))
-    held = rows_ref[...].reshape(count, rows_ref.shape[2])
-    out_ref[...] = dot(held, order, _TN).astype(jnp.bfloat16)
-
-
-def main_kernel(segs, recs, blocks, own, pairs_ref, rows_ref, table_ref, lag_ref, out_ref):
-    pair_total = pairs_ref.shape[0]
+    extra = find_ref.shape[2]
+    for h in range(halves):
+        find_ref[h] = one_hot(
+            lines,
+            extra,
+            lambda q, c: (c % (2 * halves * own) % (halves * own) == h * own + q % own)
+            & (c // (2 * halves * own) == q // own),
+        )
+    side = order_ref.shape[0]
+    order_ref[...] = one_hot(side, side, lambda r, c: c == channel_of(r, blocks, own))
+    for copy in copies:
+        copy.wait()
+
+
+def unpack_kernel(rows_hbm, order_ref, out_hbm, rows, out, in_sems, out_sems):
+    span, count = out.shape
+    tiles = span // LANES
+    cuts = [pl.ds(q * LANES, LANES) for q in range(tiles)]
+    arrive = [pltpu.make_async_copy(rows_hbm.at[:, :, cut], rows.at[:, :, cut], in_sems.at[q]) for q, cut in enumerate(cuts)]
+    leave = [pltpu.make_async_copy(out.at[cut], out_hbm.at[cut], out_sems.at[q]) for q, cut in enumerate(cuts)]
+    for copy in arrive:
+        copy.start()
+    for q in range(tiles):
+        arrive[q].wait()
+        held = rows[:, :, q * LANES : (q + 1) * LANES].reshape(count, LANES)
+        out[q * LANES : (q + 1) * LANES, :] = dot(held, order_ref[...], _TN).astype(jnp.bfloat16)
+        leave[q].start()
+    for copy in leave:
+        copy.wait()
+
+
+def main_kernel(segs, recs, blocks, own, rows_ref, table_ref, lag_ref, take_ref, give_ref, find_ref, out_ref):
     span = S // SPANS
     band = F // SPANS
     count = segs * recs * blocks * own
-    lines = pair_total * own
-    every = recs * lines
+    every = take_ref.shape[0] // 2
+    lines = every // recs
+    rows = blocks * own
+    tiles = span // LANES
     ways = segs * recs
-    folds = [
-        rows_ref[f * ways : (f + 1) * ways, :, 0:span].reshape(count, span).astype(jnp.float32)
-        for f in range(SPANS)
-    ]
+    folds = []
+    for f in range(SPANS):
+        parts = [
+            rows_ref[f * ways : (f + 1) * ways, q * rows : (q + 1) * rows, :].reshape(count, LANES)
+            for q in range(tiles)
+        ]
+        folds.append(jnp.concatenate(parts, axis=1).astype(jnp.float32))
     even, odd = folds[0] + folds[2], folds[1] + folds[3]
     e_part, d_part = folds[0] - folds[2], folds[1] - folds[3]
     both = jnp.concatenate([e_part, d_part], axis=0).astype(jnp.bfloat16)
-    spectra = []
+    sides = []
+    total = None
     for j in range(SPANS):
         if j % 2 == 0:
             signal = even + odd if j == 0 else even - odd
@@ -109,34 +193,7 @@
             d_c, d_s = mixed[count:, :band], mixed[count:, band:]
             sign = 1.0 if j == 1 else -1.0
             part = jnp.concatenate([e_c + sign * d_s, e_s - sign * d_c], axis=1)
-        spectra.append(part.astype(jnp.bfloat16))
-
-    def row_of(line, block):
-        record, k = line // lines, line % own
-        return ((block // blocks * recs + record) * blocks + block % blocks) * own + k
-
-    def picks(side, line):
-        pair = line % lines // own
-        block = jnp.zeros_like(line)
-        for n in range(pair_total):
-            block = jnp.where(pair == n, pairs_ref[n, side], block)
-        return row_of(line, block)
-
-    take, give = [], []
-    for side in range(2):
-        line = lax.broadcasted_iota(jnp.int32, (every, count), 0)
-        row = lax.broadcasted_iota(jnp.int32, (every, count), 1)
-        take.append(jnp.where(picks(side, line) == row, 1.0, 0.0).astype(jnp.bfloat16))
-        line = lax.broadcasted_iota(jnp.int32, (count, every), 1)
-        row = lax.broadcasted_iota(jnp.int32, (count, every), 0)
-        give.append(jnp.where(picks(side, line) == row, 1.0, 0.0).astype(jnp.bfloat16))
-    take = jnp.concatenate(take, axis=0)
-    give = jnp.concatenate(give + give, axis=1)
-
-    sides = []
-    total = None
-    for j in range(SPANS):
-        chosen = dot(take, spectra[j])
+        chosen = dot(take_ref[...], part.astype(jnp.bfloat16))
         a0, a1 = chosen[:every, :band], chosen[:every, band:]
         b0, b1 = chosen[every:, :band], chosen[every:, band:]
         sides.append((a0, a1, b0, b1))
@@ -147,19 +204,8 @@
     for r in range(1, recs):
         synthetic = synthetic + total[r * lines : (r + 1) * lines]
 
-    halves = LAGS // LANES
-    packed = rows_ref[:, :, span:].reshape(count * SPANS, LANES)
-    rows = blocks * own
-    seen = []
-    for h in range(halves):
-        find = one_hot(
-            lines,
-            packed.shape[0],
-            lambda q, c: (q // own == c // rows)
-            & ((c % rows == h * own + q % own) | (c % rows == (halves + h) * own + q % own)),
-        )
-        seen.append(dot(find, packed))
-    seen = jnp.concatenate(seen, axis=1)
+    packed = rows_ref[:, tiles * rows :, :].reshape(find_ref.shape[2], LANES)
+    seen = jnp.concatenate([dot(find_ref[h], packed) for h in range(LAGS // LANES)], axis=1)
     weights = jnp.where(seen < 0.5 * MASKED, jnp.tanh(synthetic - seen), 0.0).astype(jnp.bfloat16)
 
     even, odd = None, None
@@ -173,7 +219,7 @@
         terms = jnp.concatenate([first, second], axis=0)
         high = terms.astype(jnp.bfloat16)
         low = (terms - high.astype(jnp.float32)).astype(jnp.bfloat16)
-        grad = dot(give, jnp.concatenate([high, low], axis=0))
+        grad = dot(give_ref[...], jnp.concatenate([high, low], axis=0))
         if j % 2 == 0:
             part = dot(grad.astype(jnp.bfloat16), table_ref[j], _NT)
             even = (part, part) if j == 0 else (even[0] + part, even[1] - part)
@@ -183,7 +229,6 @@
             part = dot(stacked, table_ref[j], _NT)
             u, v = part[:count], part[count:]
             odd = (u, v) if j == 1 else (odd[0] + u, odd[1] - v)
-    rows = blocks * own
     for f in range(SPANS):
         base, side = even[f % 2], odd[f % 2]
         value = base + side if f < 2 else base - side
@@ -197,37 +242,71 @@
     span, count = records.shape[1:]
     blocks = count // BLOCK
     rows = blocks * own
-    pairs_dev = observed.shape[0]
+    pair_total, pairs_dev = pairs.shape[0], observed.shape[0]
     share = pairs_dev // recs
-    part = lax.axis_index("rec") * share
-    observed = lax.dynamic_slice_in_dim(observed, part, share, 0).reshape(share * BLOCK, LAGS)
-    lag_mask = lax.dynamic_slice_in_dim(lag_mask, part, share, 0)
+    lines = pair_total * own
+    every = recs * lines
+    mine = segs * recs * rows
+    extra = 2 * LAGS // LANES * share * own
     table = forward_table().reshape(F // SPANS, SPANS, 2, SPANS, span)[:, :, :, 0]
     table = np.ascontiguousarray(table.transpose(1, 3, 2, 0)).reshape(SPANS, span, S // SPANS)
     lags = lag_table().reshape(F // SPANS, SPANS, 2, LAGS)
     lags = np.ascontiguousarray(lags.transpose(1, 2, 0, 3)).reshape(SPANS, S // SPANS, LAGS)
+    low = jnp.bfloat16
     vmem = pl.BlockSpec(memory_space=pltpu.VMEM)
+    hbm = pl.BlockSpec(memory_space=pl.ANY)
+    smem = pl.BlockSpec(memory_space=pltpu.SMEM)
+    limit = pltpu.CompilerParams(vmem_limit_bytes=48 * 2**20)
     send = pl.pallas_call(
         functools.partial(pack_kernel, blocks, own),
-        out_shape=jax.ShapeDtypeStruct((devices, rows, span + LANES), jnp.bfloat16),
-        in_specs=[vmem] * 3,
+        out_shape=jax.ShapeDtypeStruct((devices, span // LANES * rows + extra, LANES), low),
+        in_specs=[hbm] * 3,
         out_specs=vmem,
+        scratch_shapes=[
+            pltpu.VMEM((span, count), low),
+            pltpu.VMEM((share, BLOCK, LAGS), jnp.float32),
+            pltpu.VMEM(lag_mask.shape, jnp.int32),
+            pltpu.SemaphoreType.DMA((2 + span // LANES,)),
+        ],
     )(records[0], observed, lag_mask)
     held = lax.all_to_all(send, EVERY, 0, 0, tiled=True)
+    prepared = pl.pallas_call(
+        functools.partial(prepare_kernel, segs, recs, blocks, own),
+        out_shape=[
+            jax.ShapeDtypeStruct(table.shape, low),
+            jax.ShapeDtypeStruct(lags.shape, low),
+            jax.ShapeDtypeStruct((2 * every, mine), low),
+            jax.ShapeDtypeStruct((mine, 4 * every), low),
+            jax.ShapeDtypeStruct((LAGS // LANES, lines, devices * extra), low),
+            jax.ShapeDtypeStruct((count, count), low),
+        ],
+        in_specs=[hbm, smem, hbm, hbm],
+        out_specs=[vmem] * 6,
+        scratch_shapes=[pltpu.SemaphoreType.DMA((2,))],
+        compiler_params=limit,
+        cost_estimate=pl.CostEstimate(flops=0, bytes_accessed=4 * 2**20, transcendentals=0),
+    )(send, pairs, jnp.asarray(table), jnp.asarray(lags))
+    order = prepared[-1]
     back = pl.pallas_call(
         functools.partial(main_kernel, segs, recs, blocks, own),
-        out_shape=jax.ShapeDtypeStruct((devices, rows, span), jnp.bfloat16),
-        in_specs=[pl.BlockSpec(memory_space=pltpu.SMEM)] + [vmem] * 3,
+        out_shape=jax.ShapeDtypeStruct((devices, rows, span), low),
+        in_specs=[vmem] * 6,
         out_specs=vmem,
-        compiler_params=pltpu.CompilerParams(vmem_limit_bytes=48 * 2**20),
-    )(pairs, held, jnp.asarray(table), jnp.asarray(lags))
-    mine = lax.all_to_all(back, EVERY, 0, 0, tiled=True)
+        compiler_params=limit,
+    )(held, *prepared[:-1])
+    back = lax.all_to_all(back, EVERY, 0, 0, tiled=True)
     out = pl.pallas_call(
-        functools.partial(unpack_kernel, blocks, own),
-        out_shape=jax.ShapeDtypeStruct((span, count), jnp.bfloat16),
-        in_specs=[vmem],
-        out_specs=vmem,
-    )(mine)
+        unpack_kernel,
+        out_shape=jax.ShapeDtypeStruct((span, count), low),
+        in_specs=[hbm, vmem],
+        out_specs=hbm,
+        scratch_shapes=[
+            pltpu.VMEM((devices, rows, span), low),
+            pltpu.VMEM((span, count), low),
+            pltpu.SemaphoreType.DMA((span // LANES,)),
+            pltpu.SemaphoreType.DMA((span // LANES,)),
+        ],
+    )(back, order)
     return out[None]
 
 

time: 45.2 us -> 41 us (0.907)
  waiting for transfers between devices: 10.3 us -> 4.69 us
  Pallas kernels: 7.46 us -> 11.6 us
  local copies, waits for them, and re-layouts: 6.25 us -> 3.59 us
    all_to_all x1, waiting for transfers between devices: 10.3 us -> 4.69 us  [by_own_k(): held = lax.all_to_all(send, EVERY, 0, 0, tiled=True)]
    pallas_call x1 -> x2, Pallas kernels: 1.92 us -> 5.53 us  [the longest x1 3.25 us: by_own_k(): pl.pallas_call(unpack_kernel, out_shape=jax.ShapeDtypeStruct((span, count...]
    dynamic_slice x1 -> x0, local copies, waits for them, and re-layouts: 1.22 us -> none  [by_own_k(): lag_mask = lax.dynamic_slice_in_dim(lag_mask, part, share, 0)]
    unnamed x7, local copies, waits for them, and re-layouts: 4.41 us -> 3.59 us
    reshape x1 -> x0, local copies, waits for them, and re-layouts: 0.62 us -> none  [by_own_k(): lax.dynamic_slice_in_dim(observed, part, share, 0)]
    pallas_call x1, Pallas kernels: 1.97 us -> 2.54 us  [by_own_k(): pl.pallas_call(functools.partial(pack_kernel, blocks, own), out_shape=jax...]
  transfers between devices with their start and end apart: 1 -> 1, of which waited for: 1 -> 1; matrix products, arithmetic and copies ran while one was open for 2% -> 2% of each run, Pallas kernels for 0% -> 6%
where the time goes in v2:
time: 41 us; the launch traced here: 40.6 us
  blocking collectives  13.3 us (32%)
  Pallas kernels  11.6 us (28%)
  starting transfers between devices  7.37 us (18%)
  waiting for transfers between devices  4.69 us (11%)
  local copies, waits for them, and re-layouts  3.59 us (9%)
    all_to_all x1, blocking collectives, by_own_k(): back = lax.all_to_all(back, EVERY, 0, 0, tiled=True)  13.3 us
    all_to_all x1, starting transfers between devices, by_own_k(): held = lax.all_to_all(send, EVERY, 0, 0, tiled=True)  7.37 us
    all_to_all x1, waiting for transfers between devices, by_own_k(): held = lax.all_to_all(send, EVERY, 0, 0, tiled=True)  4.69 us
    unnamed x7, local copies, waits for them, and re-layouts  3.59 us
    pallas_call x1, Pallas kernels, by_own_k(): pl.pallas_call(functools.partial(main_kernel, segs, recs, blocks, own), o...  3.5 us
    pallas_call x1, Pallas kernels, by_own_k(): pl.pallas_call(unpack_kernel, out_shape=jax.ShapeDtypeStruct((span, count...  3.25 us
    pallas_call x1, Pallas kernels, by_own_k(): pl.pallas_call(functools.partial(pack_kernel, blocks, own), out_shape=jax...  2.54 us
    pallas_call x1, Pallas kernels, by_own_k(): pl.pallas_call(functools.partial(prepare_kernel, segs, recs, blocks, own)...  2.28 us
  transfers between devices with their start and end apart: 1, of which 1 were waited for; matrix products, arithmetic and copies ran while one was open for 2% of the time, Pallas kernels for 6%

profile of v2, /device:TPU:0, one launch (start us, length us, event | category | flops | bytes accessed | tf_op | source)
XLA Modules:
  0.0 40.6 jit_solution(15822871054613695230)
XLA Ops:
  0.0 2.5 %shard_map.64.after_ref = bf16[16,72,128]{2,1,0:T(8,128)(2,1)} custom-call(bf16[512,256]{1,0:T(8,128)(2,1)} %bitcast.2, f32[2,32,256]{2,1,0:T(8,128)} %observed_hbm.1, s32[2,256]{1,0:T(2,128)} %mask_hbm.1), custom_call_target="tpu_custom_call" | custom-call | tf_op jit(solution)/shard_map/pallas_call | solution.py:260
  2.5 7.4 %all-to-all-start = ((bf16[16,72,128]{2,1,0:T(8,128)(2,1)}), bf16[16,72,128]{2,1,0:T(8,128)(2,1)S(1)}, u32[]{:S(2)}, u32[]{:S(2)}) async-start(bf16[16,72,128]{2,1,0:T(8,128)(2,1)} %shard_map.64.after_ref), calls=%async_computation | async-start | bytes 589824 | tf_op jit(solution)/shard_map/all_to_all | solution.py:272
  9.9 0.8 %copy.7.pairs_ref = s32[16,2]{1,0:T(8,128)S(1)} copy(s32[16,2]{0,1:T(2,128)} %param.7) | data formatting | bytes 256 | tf_op args[1]
  10.7 0.0 copy-start
  10.7 1.0 %copy-done = bf16[16,72,128]{2,1,0:T(8,128)(2,1)S(1)} copy-done((bf16[16,72,128]{2,1,0:T(8,128)(2,1)S(1)}, bf16[16,72,128]{2,1,0:T(8,128)(2,1)}, u32[]{:S(2)}) %copy-start) | copy-done | bytes 294936
  11.6 0.0 copy-start.1
  11.6 1.2 %copy-done.1 = bf16[4,512,256]{2,1,0:T(8,128)(2,1)S(1)} copy-done((bf16[4,512,256]{2,1,0:T(8,128)(2,1)S(1)}, bf16[4,512,256]{2,1,0:T(8,128)(2,1)}, u32[]{:S(2)}) %copy-start.1) | copy-done | bytes 1048600
  12.9 2.3 %shard_map.65 = (bf16[4,512,512]{2,1,0:T(8,128)(2,1)S(1)}, bf16[4,512,256]{2,1,0:T(8,128)(2,1)S(1)}, bf16[128,64]{1,0:T(8,128)(2,1)S(1)}, bf16[64,256]{1,0:T(8,1...) custom-call(bf16[16,72,128]{2,1,0:T(8,128)(2,1)S(1)} %copy-done, s32[16,2]{1,0:T(8,128)S(1)} %copy.7.pairs_ref, ...), custom_call_target="tpu_custom_call" | custom-call | bytes 4194304 | tf_op jit(solution)/shard_map/pallas_call | solution.py:273
  15.2 0.0 copy-start.2
  15.2 0.6 %copy-done.2 = bf16[256,256]{1,0:T(8,128)(2,1)} copy-done((bf16[256,256]{1,0:T(8,128)(2,1)}, bf16[256,256]{1,0:T(8,128)(2,1)S(1)}, u32[]{:S(2)}) %copy-start.2) | copy-done | bytes 131096
  15.8 4.7 %all-to-all-done.rows_ref = bf16[16,72,128]{2,1,0:T(8,128)(2,1)S(1)} async-done(((bf16[16,72,128]{2,1,0:T(8,128)(2,1)}), bf16[16,72,128]{2,1,0:T(8,128)(2,1)S(1)}, u32[]{:S(2)}, u32[]{:S(2)}) %all-to-all-start) | async-done | bytes 294944 | tf_op jit(solution)/shard_map/all_to_all | solution.py:272
  20.5 3.5 %shard_map.66 = bf16[16,16,512]{2,1,0:T(8,128)(2,1)S(1)} custom-call(bf16[16,72,128]{2,1,0:T(8,128)(2,1)S(1)} %all-to-all-done.rows_ref, bf16[4,512,512]{2,1,0:T(8,128)(2,1)S(1)} %get-tuple-element.11.table_ref, bf16[4,512,256]{2,1,0:T(8,128)(2,1)S(1)} %get-tuple-element.12.lag_ref, bf16[128,64]{1,0:T(8,128)(2,1)S(1)} %get-tuple-element.13.take_ref, ...), custom_call_target="tpu_custom_call" | custom-call | tf_op jit(solution)/shard_map/pallas_call | solution.py:290
  24.0 13.3 %all_to_all.10.rows_hbm = bf16[16,16,512]{2,1,0:T(8,128)(2,1)} all-to-all(bf16[16,16,512]{2,1,0:T(8,128)(2,1)S(1)} %shard_map.66), channel_id=1, replica_groups=mesh['groups'=2,'fibre'=4,'seg'=2,'rec'=2] {'fibre','seg','rec'}, dimensions={0} | all-to-all | bytes 524288 | tf_op jit(solution)/shard_map/all_to_all | solution.py:297
  37.3 3.3 %shard_map.67 = bf16[512,256]{1,0:T(8,128)(2,1)} custom-call(bf16[16,16,512]{2,1,0:T(8,128)(2,1)} %all_to_all.10.rows_hbm, bf16[256,256]{1,0:T(8,128)(2,1)} %copy-done.2), custom_call_target="tpu_custom_call" | custom-call | tf_op jit(solution)/shard_map/pallas_call | solution.py:298
Async XLA Ops:
  2.5 17.9 %all-to-all-start = ((bf16[16,72,128]{2,1,0:T(8,128)(2,1)}), bf16[16,72,128]{2,1,0:T(8,128)(2,1)S(1)}, u32[]{:S(2)}, u32[]{:S(2)}) async-start(bf16[16,72,128]{2,1,0:T(8,128)(2,1)} %shard_map.64.after_ref), calls=%async_computation | async-start | bytes 589824 | tf_op jit(solution)/shard_map/all_to_all | solution.py:272
  10.7 1.0 %copy-start = (bf16[16,72,128]{2,1,0:T(8,128)(2,1)S(1)}, bf16[16,72,128]{2,1,0:T(8,128)(2,1)}, u32[]{:S(2)}) copy-start(bf16[16,72,128]{2,1,0:T(8,128)(2,1)} %shard_map.64.after_ref) | copy-start | bytes 884740
  11.6 1.2 %copy-start.1 = (bf16[4,512,256]{2,1,0:T(8,128)(2,1)S(1)}, bf16[4,512,256]{2,1,0:T(8,128)(2,1)}, u32[]{:S(2)}) copy-start(bf16[4,512,256]{2,1,0:T(8,128)(2,1)} %constant.5.clone.lag_hbm) | copy-start | bytes 3145732
  15.2 0.7 %copy-start.2 = (bf16[256,256]{1,0:T(8,128)(2,1)}, bf16[256,256]{1,0:T(8,128)(2,1)S(1)}, u32[]{:S(2)}) copy-start(bf16[256,256]{1,0:T(8,128)(2,1)S(1)} %get-tuple-element.16.order_ref) | copy-start | bytes 393220

commit v3 on v2

--- a/solution.py
+++ b/solution.py
@@ -60,13 +60,8 @@
     start = lax.axis_index("rec") * share
     seen_copy = pltpu.make_async_copy(observed_hbm.at[pl.ds(start, share)], observed, sems.at[0])
     mask_copy = pltpu.make_async_copy(mask_hbm, mask, sems.at[1])
-    copies = [
-        pltpu.make_async_copy(
-            records_hbm.at[pl.ds(q * LANES, LANES)], records.at[pl.ds(q * LANES, LANES)], sems.at[2 + q]
-        )
-        for q in range(tiles)
-    ]
-    for copy in [seen_copy, mask_copy] + copies:
+    records_copy = pltpu.make_async_copy(records_hbm, records, sems.at[2])
+    for copy in (records_copy, seen_copy, mask_copy):
         copy.start()
     order = one_hot(count, count, lambda r, c: c == channel_of(r, blocks, own))
     lines = share * BLOCK
@@ -76,7 +71,9 @@
         dests * extra,
         2 * halves * lines,
         lambda r, c: (c % BLOCK // own == r // extra)
-        & (c // BLOCK * own + c % own == r % extra),
+        & (c % own == r % own)
+        & (c // lines == r % (2 * halves * own) // own)
+        & (c % lines // BLOCK == r % extra // (2 * halves * own)),
     )
     seen_copy.wait()
     mask_copy.wait()
@@ -89,18 +86,18 @@
     parts = [v[:, h * LANES : (h + 1) * LANES] for v in (high, low) for h in range(halves)]
     packed = dot(place, jnp.concatenate(parts, axis=0)).astype(jnp.bfloat16)
     out_ref[:, tiles * rows :, :] = packed.reshape(dests, extra, LANES)
-    for q, copy in enumerate(copies):
-        copy.wait()
-        moved = dot(order, records[q * LANES : (q + 1) * LANES, :], _NT).astype(jnp.bfloat16)
-        out_ref[:, q * rows : (q + 1) * rows, :] = moved.reshape(dests, rows, LANES)
-
-
-def prepare_kernel(
-    segs, recs, blocks, own, after_ref, pairs_ref, table_hbm, lag_hbm, table_ref, lag_ref, take_ref, give_ref, find_ref, order_ref, sems
-):
+    records_copy.wait()
+    moved = dot(order, records[...], _NT).astype(jnp.bfloat16)
+    for q in range(tiles):
+        part = moved[:, q * LANES : (q + 1) * LANES]
+        out_ref[:, q * rows : (q + 1) * rows, :] = part.reshape(dests, rows, LANES)
+
+
+def prepare_kernel(segs, recs, blocks, own, pairs_ref, *refs):
+    constants = (len(refs) - 3) // 2
+    take_ref, give_ref = refs[2 * constants : 2 * constants + 2]
     copies = [
-        pltpu.make_async_copy(table_hbm, table_ref, sems.at[0]),
-        pltpu.make_async_copy(lag_hbm, lag_ref, sems.at[1]),
+        pltpu.make_async_copy(refs[i], refs[constants + i], refs[-1].at[i]) for i in range(constants)
     ]
     for copy in copies:
         copy.start()
@@ -121,40 +118,23 @@
         row = lax.broadcasted_iota(jnp.int32, (every, count), 1)
         hit = jnp.where(picks(side, line) == row, 1.0, 0.0).astype(jnp.bfloat16)
         take_ref[side * every : (side + 1) * every, :] = hit
-        line = lax.broadcasted_iota(jnp.int32, (count, 2 * every), 1)
-        row = lax.broadcasted_iota(jnp.int32, (count, 2 * every), 0)
-        hit = jnp.where(picks(side, line % every) == row, 1.0, 0.0)
-        if side == 0:
-            first = hit
-        else:
-            hit = jnp.where(line < every, first, hit).astype(jnp.bfloat16)
-            give_ref[:, 0 : 2 * every] = hit
-            give_ref[:, 2 * every :] = hit
-    halves = LAGS // LANES
-    extra = find_ref.shape[2]
-    for h in range(halves):
-        find_ref[h] = one_hot(
-            lines,
-            extra,
-            lambda q, c: (c % (2 * halves * own) % (halves * own) == h * own + q % own)
-            & (c // (2 * halves * own) == q // own),
-        )
-    side = order_ref.shape[0]
-    order_ref[...] = one_hot(side, side, lambda r, c: c == channel_of(r, blocks, own))
+    line = lax.broadcasted_iota(jnp.int32, (count, 2 * every), 1)
+    row = lax.broadcasted_iota(jnp.int32, (count, 2 * every), 0)
+    first, second = (picks(side, line % every) for side in range(2))
+    chosen = jnp.where(line < every, first, second)
+    hit = jnp.where(chosen == row, 1.0, 0.0).astype(jnp.bfloat16)
+    give_ref[:, 0 : 2 * every] = hit
+    give_ref[:, 2 * every :] = hit
     for copy in copies:
         copy.wait()
 
 
-def unpack_kernel(rows_hbm, order_ref, out_hbm, rows, out, in_sems, out_sems):
+def unpack_kernel(rows, order_ref, out_hbm, out, out_sems):
     span, count = out.shape
     tiles = span // LANES
     cuts = [pl.ds(q * LANES, LANES) for q in range(tiles)]
-    arrive = [pltpu.make_async_copy(rows_hbm.at[:, :, cut], rows.at[:, :, cut], in_sems.at[q]) for q, cut in enumerate(cuts)]
     leave = [pltpu.make_async_copy(out.at[cut], out_hbm.at[cut], out_sems.at[q]) for q, cut in enumerate(cuts)]
-    for copy in arrive:
-        copy.start()
     for q in range(tiles):
-        arrive[q].wait()
         held = rows[:, :, q * LANES : (q + 1) * LANES].reshape(count, LANES)
         out[q * LANES : (q + 1) * LANES, :] = dot(held, order_ref[...], _TN).astype(jnp.bfloat16)
         leave[q].start()
@@ -181,25 +161,26 @@
     even, odd = folds[0] + folds[2], folds[1] + folds[3]
     e_part, d_part = folds[0] - folds[2], folds[1] - folds[3]
     both = jnp.concatenate([e_part, d_part], axis=0).astype(jnp.bfloat16)
-    sides = []
-    total = None
+    reals, imags = [], []
     for j in range(SPANS):
         if j % 2 == 0:
             signal = even + odd if j == 0 else even - odd
             part = dot(signal.astype(jnp.bfloat16), table_ref[j])
+            real, imag = part[:, :band], part[:, band:]
         else:
             mixed = dot(both, table_ref[j])
             e_c, e_s = mixed[:count, :band], mixed[:count, band:]
             d_c, d_s = mixed[count:, :band], mixed[count:, band:]
-            sign = 1.0 if j == 1 else -1.0
-            part = jnp.concatenate([e_c + sign * d_s, e_s - sign * d_c], axis=1)
-        chosen = dot(take_ref[...], part.astype(jnp.bfloat16))
-        a0, a1 = chosen[:every, :band], chosen[:every, band:]
-        b0, b1 = chosen[every:, :band], chosen[every:, band:]
-        sides.append((a0, a1, b0, b1))
-        cross = jnp.concatenate([a0 * b0 + a1 * b1, a1 * b0 - a0 * b1], axis=1)
-        term = dot(cross.astype(jnp.bfloat16), lag_ref[j])
-        total = term if total is None else total + term
+            real, imag = (e_c + d_s, e_s - d_c) if j == 1 else (e_c - d_s, e_s + d_c)
+        reals.append(real.astype(jnp.bfloat16))
+        imags.append(imag.astype(jnp.bfloat16))
+    spectra = jnp.concatenate(reals + imags, axis=1)
+    chosen = dot(take_ref[...], spectra)
+    a0, a1 = chosen[:every, :F], chosen[:every, F:]
+    b0, b1 = chosen[every:, :F], chosen[every:, F:]
+    cross_re = (a0 * b0 + a1 * b1).astype(jnp.bfloat16)
+    cross_im = (a1 * b0 - a0 * b1).astype(jnp.bfloat16)
+    total = dot(jnp.concatenate([cross_re, cross_im], axis=1), lag_ref[...])
     synthetic = total[:lines]
     for r in range(1, recs):
         synthetic = synthetic + total[r * lines : (r + 1) * lines]
@@ -208,25 +189,26 @@
     seen = jnp.concatenate([dot(find_ref[h], packed) for h in range(LAGS // LANES)], axis=1)
     weights = jnp.where(seen < 0.5 * MASKED, jnp.tanh(synthetic - seen), 0.0).astype(jnp.bfloat16)
 
+    adjoint = dot(weights, lag_ref[...], _NT).astype(jnp.bfloat16).astype(jnp.float32)
+    adjoint = jnp.concatenate([adjoint] * recs, axis=0)
+    g0, g1 = adjoint[:, :F], adjoint[:, F:]
+    first = jnp.concatenate([g0 * b0 - g1 * b1, g0 * b1 + g1 * b0], axis=1)
+    second = jnp.concatenate([g0 * a0 + g1 * a1, g0 * a1 - g1 * a0], axis=1)
+    terms = jnp.concatenate([first, second], axis=0)
+    high = terms.astype(jnp.bfloat16)
+    low = (terms - high.astype(jnp.float32)).astype(jnp.bfloat16)
+    grad = dot(give_ref[...], jnp.concatenate([high, low], axis=0)).astype(jnp.bfloat16)
     even, odd = None, None
     for j in range(SPANS):
-        a0, a1, b0, b1 = sides[j]
-        adjoint = dot(weights, lag_ref[j], _NT).astype(jnp.bfloat16).astype(jnp.float32)
-        adjoint = jnp.concatenate([adjoint] * recs, axis=0)
-        g0, g1 = adjoint[:, :band], adjoint[:, band:]
-        first = jnp.concatenate([g0 * b0 - g1 * b1, g0 * b1 + g1 * b0], axis=1)
-        second = jnp.concatenate([g0 * a0 + g1 * a1, g0 * a1 - g1 * a0], axis=1)
-        terms = jnp.concatenate([first, second], axis=0)
-        high = terms.astype(jnp.bfloat16)
-        low = (terms - high.astype(jnp.float32)).astype(jnp.bfloat16)
-        grad = dot(give_ref[...], jnp.concatenate([high, low], axis=0))
+        real = grad[:, j * band : (j + 1) * band]
+        imag = grad[:, F + j * band : F + (j + 1) * band]
+        line = jnp.concatenate([real, imag], axis=1)
         if j % 2 == 0:
-            part = dot(grad.astype(jnp.bfloat16), table_ref[j], _NT)
+            part = dot(line, table_ref[j], _NT)
             even = (part, part) if j == 0 else (even[0] + part, even[1] - part)
         else:
-            turned = jnp.concatenate([-grad[:, band:], grad[:, :band]], axis=1)
-            stacked = jnp.concatenate([grad, turned], axis=0).astype(jnp.bfloat16)
-            part = dot(stacked, table_ref[j], _NT)
+            turned = jnp.concatenate([-imag, real], axis=1)
+            part = dot(jnp.concatenate([line, turned], axis=0), table_ref[j], _NT)
             u, v = part[:count], part[count:]
             odd = (u, v) if j == 1 else (odd[0] + u, odd[1] - v)
     for f in range(SPANS):
@@ -251,62 +233,62 @@
     table = forward_table().reshape(F // SPANS, SPANS, 2, SPANS, span)[:, :, :, 0]
     table = np.ascontiguousarray(table.transpose(1, 3, 2, 0)).reshape(SPANS, span, S // SPANS)
     lags = lag_table().reshape(F // SPANS, SPANS, 2, LAGS)
-    lags = np.ascontiguousarray(lags.transpose(1, 2, 0, 3)).reshape(SPANS, S // SPANS, LAGS)
+    lags = np.ascontiguousarray(lags.transpose(2, 1, 0, 3)).reshape(2 * F, LAGS)
     low = jnp.bfloat16
+    order = channel_of(np.arange(count), blocks, own)[:, None] == np.arange(count)
+    order = order.astype(low)
+    halves = LAGS // LANES
+    line, place = np.arange(lines)[:, None], np.arange(devices * extra)
+    same = (place // (extra // share) == line // own) & (place % own == line % own)
+    find = np.stack([same & (place % (halves * own) // own == h) for h in range(halves)]).astype(low)
     vmem = pl.BlockSpec(memory_space=pltpu.VMEM)
     hbm = pl.BlockSpec(memory_space=pl.ANY)
     smem = pl.BlockSpec(memory_space=pltpu.SMEM)
-    limit = pltpu.CompilerParams(vmem_limit_bytes=48 * 2**20)
+    limit = pltpu.CompilerParams(vmem_limit_bytes=16 * 2**20)
     send = pl.pallas_call(
         functools.partial(pack_kernel, blocks, own),
-        out_shape=jax.ShapeDtypeStruct((devices, span // LANES * rows + extra, LANES), low),
+        out_shape=pltpu.VMEM((devices, span // LANES * rows + extra, LANES), low),
         in_specs=[hbm] * 3,
         out_specs=vmem,
         scratch_shapes=[
             pltpu.VMEM((span, count), low),
             pltpu.VMEM((share, BLOCK, LAGS), jnp.float32),
             pltpu.VMEM(lag_mask.shape, jnp.int32),
-            pltpu.SemaphoreType.DMA((2 + span // LANES,)),
+            pltpu.SemaphoreType.DMA((3,)),
         ],
-    )(records[0], observed, lag_mask)
+        compiler_params=limit,
+    )(*(pltpu.with_memory_space_constraint(x, pltpu.HBM) for x in (records[0], observed, lag_mask)))
     held = lax.all_to_all(send, EVERY, 0, 0, tiled=True)
-    prepared = pl.pallas_call(
+    constants = [jnp.asarray(c) for c in (table, lags, find)]
+    table, lags, find, take, give = pl.pallas_call(
         functools.partial(prepare_kernel, segs, recs, blocks, own),
-        out_shape=[
-            jax.ShapeDtypeStruct(table.shape, low),
-            jax.ShapeDtypeStruct(lags.shape, low),
-            jax.ShapeDtypeStruct((2 * every, mine), low),
-            jax.ShapeDtypeStruct((mine, 4 * every), low),
-            jax.ShapeDtypeStruct((LAGS // LANES, lines, devices * extra), low),
-            jax.ShapeDtypeStruct((count, count), low),
-        ],
-        in_specs=[hbm, smem, hbm, hbm],
-        out_specs=[vmem] * 6,
-        scratch_shapes=[pltpu.SemaphoreType.DMA((2,))],
+        out_shape=[pltpu.VMEM(c.shape, low) for c in constants]
+        + [pltpu.VMEM((2 * every, mine), low), pltpu.VMEM((mine, 4 * every), low)],
+        in_specs=[smem] + [hbm] * len(constants),
+        out_specs=[vmem] * 5,
+        scratch_shapes=[pltpu.SemaphoreType.DMA((len(constants),))],
         compiler_params=limit,
         cost_estimate=pl.CostEstimate(flops=0, bytes_accessed=4 * 2**20, transcendentals=0),
-    )(send, pairs, jnp.asarray(table), jnp.asarray(lags))
-    order = prepared[-1]
+    )(pairs, *(pltpu.with_memory_space_constraint(c, pltpu.HBM) for c in constants))
     back = pl.pallas_call(
         functools.partial(main_kernel, segs, recs, blocks, own),
         out_shape=jax.ShapeDtypeStruct((devices, rows, span), low),
         in_specs=[vmem] * 6,
         out_specs=vmem,
         compiler_params=limit,
-    )(held, *prepared[:-1])
+    )(held, table, lags, take, give, find)
     back = lax.all_to_all(back, EVERY, 0, 0, tiled=True)
     out = pl.pallas_call(
         unpack_kernel,
         out_shape=jax.ShapeDtypeStruct((span, count), low),
-        in_specs=[hbm, vmem],
+        in_specs=[vmem, vmem],
         out_specs=hbm,
         scratch_shapes=[
-            pltpu.VMEM((devices, rows, span), low),
             pltpu.VMEM((span, count), low),
             pltpu.SemaphoreType.DMA((span // LANES,)),
-            pltpu.SemaphoreType.DMA((span // LANES,)),
         ],
-    )(back, order)
+        compiler_params=limit,
+    )(pltpu.with_memory_space_constraint(back, pltpu.VMEM), jnp.asarray(order))
     return out[None]
 
 

time: 41 us -> 36.6 us (0.89)
  Pallas kernels: 11.6 us -> 7.93 us
  local copies, waits for them, and re-layouts: 3.59 us -> 0.76 us
  waiting for transfers between devices: 4.69 us -> 7.26 us
    unnamed x7 -> x3, local copies, waits for them, and re-layouts: 3.59 us -> 0.76 us
    all_to_all x1, waiting for transfers between devices: 4.69 us -> 7.26 us  [by_own_k(): held = lax.all_to_all(send, EVERY, 0, 0, tiled=True)]
    pallas_call x1, Pallas kernels: 3.25 us -> 0.94 us  [by_own_k(): pl.pallas_call(unpack_kernel, out_shape=jax.ShapeDtypeStruct((span, count...]
    pallas_call x1, Pallas kernels: 3.5 us -> 2.45 us  [by_own_k(): pl.pallas_call(functools.partial(main_kernel, segs, recs, blocks, own), o...]
    pallas_call x1, Pallas kernels: 2.54 us -> 2 us  [by_own_k(): pl.pallas_call(functools.partial(pack_kernel, blocks, own), out_shape=plt...]
  transfers between devices with their start and end apart: 1 -> 1, of which waited for: 1 -> 1; matrix products, arithmetic and copies ran while one was open for 2% -> 2% of each run, Pallas kernels for 6% -> 7%
where the time goes in v3:
time: 36.6 us; the launch traced here: 36.3 us
  blocking collectives  12.9 us (35%)
  Pallas kernels  7.93 us (22%)
  starting transfers between devices  7.37 us (20%)
  waiting for transfers between devices  7.26 us (20%)
  local copies, waits for them, and re-layouts  0.76 us (2%)
    all_to_all x1, blocking collectives, by_own_k(): back = lax.all_to_all(back, EVERY, 0, 0, tiled=True)  12.9 us
    all_to_all x1, starting transfers between devices, by_own_k(): held = lax.all_to_all(send, EVERY, 0, 0, tiled=True)  7.37 us
    all_to_all x1, waiting for transfers between devices, by_own_k(): held = lax.all_to_all(send, EVERY, 0, 0, tiled=True)  7.26 us
    pallas_call x1, Pallas kernels, by_own_k(): pl.pallas_call(functools.partial(prepare_kernel, segs, recs, blocks, own)...  2.55 us
    pallas_call x1, Pallas kernels, by_own_k(): pl.pallas_call(functools.partial(main_kernel, segs, recs, blocks, own), o...  2.45 us
    pallas_call x1, Pallas kernels, by_own_k(): pl.pallas_call(functools.partial(pack_kernel, blocks, own), out_shape=plt...  2 us
    pallas_call x1, Pallas kernels, by_own_k(): pl.pallas_call(unpack_kernel, out_shape=jax.ShapeDtypeStruct((span, count...  0.94 us
    unnamed x3, local copies, waits for them, and re-layouts  0.76 us
  transfers between devices with their start and end apart: 1, of which 1 were waited for; matrix products, arithmetic and copies ran while one was open for 2% of the time, Pallas kernels for 7%

profile of v3, /device:TPU:0, one launch (start us, length us, event | category | flops | bytes accessed | tf_op | source)
XLA Modules:
  0.0 36.3 jit_solution(12227615350203882587)
XLA Ops:
  0.0 2.0 %shard_map.82 = bf16[16,72,128]{2,1,0:T(8,128)(2,1)} custom-call(bf16[512,256]{1,0:T(8,128)(2,1)} %bitcast.2, f32[2,32,256]{2,1,0:T(8,128)} %observed_hbm.1, s32[2,256]{1,0:T(2,128)} %mask_hbm.1), custom_call_target="tpu_custom_call" | custom-call | tf_op jit(solution)/shard_map/pallas_call | solution.py:248
  2.0 7.4 %all-to-all-start = ((bf16[16,72,128]{2,1,0:T(8,128)(2,1)}), bf16[16,72,128]{2,1,0:T(8,128)(2,1)S(1)}, u32[]{:S(2)}, u32[]{:S(2)}) async-start(bf16[16,72,128]{2,1,0:T(8,128)(2,1)} %shard_map.82), calls=%async_computation | async-start | bytes 589824 | tf_op jit(solution)/shard_map/all_to_all | solution.py:261
  9.4 0.8 %copy.9.pairs_ref = s32[16,2]{1,0:T(8,128)S(1)} copy(s32[16,2]{0,1:T(2,128)} %param.9) | data formatting | bytes 256 | tf_op args[1]
  10.1 2.5 %shard_map.83 = (bf16[4,512,512]{2,1,0:T(8,128)(2,1)S(1)}, bf16[2048,256]{1,0:T(8,128)(2,1)S(1)}, bf16[2,32,128]{2,1,0:T(8,128)(2,1)S(1)}, bf16[128,64]{1,0:T(8,128)(2,1)S(1)}, bf16[64,256]{1,0:T(8,128)(2,1)S(1)}) custom-call(s32[16,2]{1,0:T(8,128)S(1)} %copy.9.pairs_ref, bf16[4,512,512]{2,1,0:T(8,128)(2,1)} %constant.8.clone.refs_0_, ...), custom_call_target="tpu_custom_call" | custom-call | bytes 4194304 | tf_op jit(solution)/shard_map/pallas_call | solution.py:263
  12.7 7.3 %all-to-all-done.rows_ref = bf16[16,72,128]{2,1,0:T(8,128)(2,1)S(1)} async-done(((bf16[16,72,128]{2,1,0:T(8,128)(2,1)}), bf16[16,72,128]{2,1,0:T(8,128)(2,1)S(1)}, u32[]{:S(2)}, u32[]{:S(2)}) %all-to-all-start) | async-done | bytes 294944 | tf_op jit(solution)/shard_map/all_to_all | solution.py:261
  20.0 0.0 copy-start
  20.0 2.4 %shard_map.84 = bf16[16,16,512]{2,1,0:T(8,128)(2,1)S(1)} custom-call(bf16[16,72,128]{2,1,0:T(8,128)(2,1)S(1)} %all-to-all-done.rows_ref, bf16[4,512,512]{2,1,0:T(8,128)(2,1)S(1)} %get-tuple-element.10.table_ref, bf16[2048,256]{1,0:T(8,128)(2,1)S(1)} %get-tuple-element.11.lag_ref, bf16[128,64]{1,0:T(8,128)(2,1)S(1)} %get-tuple-element.12.take_ref, ...), custom_call_target="tpu_custom_call" | custom-call | tf_op jit(solution)/shard_map/pallas_call | solution.py:273
  22.4 12.9 %all_to_all.10.rows = bf16[16,16,512]{2,1,0:T(8,128)(2,1)S(1)} all-to-all(bf16[16,16,512]{2,1,0:T(8,128)(2,1)S(1)} %shard_map.84), channel_id=1, replica_groups=mesh['groups'=2,'fibre'=4,'seg'=2,'rec'=2] {'fibre','seg','rec'}, dimensions={0} | all-to-all | bytes 524288 | tf_op jit(solution)/shard_map/all_to_all | solution.py:280
  35.4 0.0 copy-done
  35.4 0.9 %shard_map.85 = bf16[512,256]{1,0:T(8,128)(2,1)} custom-call(bf16[16,16,512]{2,1,0:T(8,128)(2,1)S(1)} %all_to_all.10.rows, bf16[256,256]{1,0:T(8,128)(2,1)S(1)} %copy-done), custom_call_target="tpu_custom_call" | custom-call | tf_op jit(solution)/shard_map/pallas_call | solution.py:281
Async XLA Ops:
  2.0 17.9 %all-to-all-start = ((bf16[16,72,128]{2,1,0:T(8,128)(2,1)}), bf16[16,72,128]{2,1,0:T(8,128)(2,1)S(1)}, u32[]{:S(2)}, u32[]{:S(2)}) async-start(bf16[16,72,128]{2,1,0:T(8,128)(2,1)} %shard_map.82), calls=%async_computation | async-start | bytes 589824 | tf_op jit(solution)/shard_map/all_to_all | solution.py:261
  20.0 15.4 %copy-start = (bf16[256,256]{1,0:T(8,128)(2,1)S(1)}, bf16[256,256]{1,0:T(8,128)(2,1)}, u32[]{:S(2)}) copy-start(bf16[256,256]{1,0:T(8,128)(2,1)} %constant.11.clone.order_ref) | copy-start | bytes 393220

commit v4 on v3

v4 whole, which is shorter than its diff:
```python
import functools

import jax
import jax.numpy as jnp
import numpy as np
from jax import lax
from jax.experimental import pallas as pl
from jax.experimental.pallas import tpu as pltpu
from jax.sharding import PartitionSpec as P

S = 2048
F = 1024
LAGS = 256
BLOCK = 32
SPANS = 4
MASKED = 16384.0
LANES = 128

_NT = (((1,), (1,)), ((), ()))
_TN = (((0,), (0,)), ((), ()))


def wave_table(freq, shift, scale):
    phase = freq[:, None].astype(np.int64) * shift[None, :] % S
    angles = phase.astype(np.float32) * np.float32(2.0 * np.pi / S)
    factor = np.float32(1.0) / np.sqrt(np.float32(scale))
    parts = [(np.cos(angles) * factor), (-np.sin(angles) * factor)]
    return np.stack(parts, axis=1).astype(jnp.bfloat16)


def forward_table():
    return wave_table(np.arange(F), np.arange(S), S)


def lag_table():
    return wave_table(np.arange(F), (np.arange(LAGS) - LAGS // 2) % S, F)


def dot(a, b, dims=(((1,), (0,)), ((), ()))):
    return lax.dot_general(a, b, dims, preferred_element_type=jnp.float32)


def one_hot(rows, cols, hit):
    row = lax.broadcasted_iota(jnp.int32, (rows, cols), 0)
    col = lax.broadcasted_iota(jnp.int32, (rows, cols), 1)
    return jnp.where(hit(row, col), 1.0, 0.0).astype(jnp.bfloat16)


def channel_of(row, fibre, blocks, own):
    to = row // (blocks * own) ^ fibre
    return row % (blocks * own) // own * BLOCK + to * own + row % own


def channel_order(fibre, blocks, own):
    count = blocks * BLOCK
    return one_hot(count, count, lambda r, c: c == channel_of(r, fibre, blocks, own))


def pack_kernel(blocks, own, records_hbm, observed_hbm, mask_hbm, *refs):
    out_refs, (records, observed, mask, sems) = refs[:SPANS], refs[SPANS:]
    fibre = lax.axis_index("fibre")
    span, count = records.shape
    rows = blocks * own
    tiles = span // LANES
    share = observed.shape[0]
    start = lax.axis_index("rec") * share
    records_copy = pltpu.make_async_copy(records_hbm, records, sems.at[0])
    seen_copy = pltpu.make_async_copy(observed_hbm.at[pl.ds(start, share)], observed, sems.at[1])
    mask_copy = pltpu.make_async_copy(mask_hbm, mask, sems.at[2])
    for copy in (records_copy, seen_copy, mask_copy):
        copy.start()
    order = channel_order(fibre, blocks, own)
    lines = share * BLOCK
    halves = LAGS // LANES
    extra = 2 * halves * share * own
    place = one_hot(
        SPANS * extra,
        2 * halves * lines,
        lambda r, c: (c % BLOCK // own == r // extra ^ fibre)
        & (c % own == r % own)
        & (c // lines == r % (2 * halves * own) // own)
        & (c % lines // BLOCK == r % extra // (2 * halves * own)),
    )
    seen_copy.wait()
    mask_copy.wait()
    window = jnp.concatenate(
        [mask[pl.ds(start + i, 1), :] + jnp.zeros((BLOCK, 1), jnp.int32) for i in range(share)], axis=0
    )
    seen = jnp.where(window != 0, observed[...].reshape(lines, LAGS), MASKED)
    high = seen.astype(jnp.bfloat16)
    low = (seen - high.astype(jnp.float32)).astype(jnp.bfloat16)
    parts = [v[:, h * LANES : (h + 1) * LANES] for v in (high, low) for h in range(halves)]
    packed = dot(place, jnp.concatenate(parts, axis=0)).astype(jnp.bfloat16)
    for k, out_ref in enumerate(out_refs):
        out_ref[tiles * rows :, :] = packed[k * extra : (k + 1) * extra]
    records_copy.wait()
    moved = dot(order, records[...], _NT).astype(jnp.bfloat16)
    for k, out_ref in enumerate(out_refs):
        for q in range(tiles):
            part = moved[k * rows : (k + 1) * rows, q * LANES : (q + 1) * LANES]
            out_ref[q * rows : (q + 1) * rows, :] = part


def prepare_kernel(segs, blocks, own, pairs_dev, share, pairs_ref, *refs):
    constants = (len(refs) - 5) // 2
    take_ref, give_ref, find_ref, order_ref, sems = refs[2 * constants :]
    copies = [pltpu.make_async_copy(refs[i], refs[constants + i], sems.at[i]) for i in range(constants)]
    for copy in copies:
        copy.start()
    fibre, seg, rec = (lax.axis_index(axis) for axis in ("fibre", "seg", "rec"))
    pair_total = pairs_ref.shape[0]
    rows = blocks * own
    lines = pair_total * own

    def picks(side, line):
        block = jnp.zeros_like(line)
        for n in range(pair_total):
            block = jnp.where(line // own == n, pairs_ref[n, side], block)
        distance = (seg + segs - block // blocks) % segs
        return distance * rows + block % blocks * own + line % own

    for side in range(2):
        line = lax.broadcasted_iota(jnp.int32, (lines, segs * rows), 0)
        row = lax.broadcasted_iota(jnp.int32, (lines, segs * rows), 1)
        hit = jnp.where(picks(side, line) == row, 1.0, 0.0).astype(jnp.bfloat16)
        take_ref[side * lines : (side + 1) * lines, :] = hit
        line = lax.broadcasted_iota(jnp.int32, (rows, lines), 1)
        row = lax.broadcasted_iota(jnp.int32, (rows, lines), 0)
        hit = jnp.where(picks(side, line) == row, 1.0, 0.0).astype(jnp.bfloat16)
        give_ref[:, side * lines : (side + 1) * lines] = hit
    halves = LAGS // LANES
    extra = 2 * halves * share * own

    def here(half, line, place):
        part = place % extra
        owner = (place // extra % SPANS ^ fibre) * segs + (seg + segs - place // (extra * SPANS)) % segs
        pair = owner * pairs_dev + rec * share + part // (2 * halves * own)
        return (line // own == pair) & (line % own == part % own) & (part % (halves * own) // own == half)

    for h in range(halves):
        find_ref[h] = one_hot(lines, segs * SPANS * extra, functools.partial(here, h))
    order_ref[...] = channel_order(fibre, blocks, own)
    for copy in copies:
        copy.wait()


def correlate_kernel(segs, blocks, own, *refs):
    chunks = refs[: segs * SPANS]
    table_ref, lag_ref, take_ref, find_ref, chosen_ref, partial_ref = refs[segs * SPANS :]
    fibre = lax.axis_index("fibre")
    span = S // SPANS
    band = F // SPANS
    rows = blocks * own
    count = segs * rows
    lines = take_ref.shape[0] // 2
    tiles = span // LANES
    folds = []
    for k in range(SPANS):
        whole = [
            jnp.concatenate([chunks[u * SPANS + k][q * rows : (q + 1) * rows, :] for q in range(tiles)], axis=1)
            for u in range(segs)
        ]
        folds.append(jnp.concatenate(whole, axis=0).astype(jnp.float32))
    flip = fibre % 2 == 1
    turn = jnp.where(flip, -1.0, 1.0)
    late = jnp.where(fibre >= 2, -1.0, 1.0)
    near, far = folds[0] + folds[2], folds[1] + folds[3]
    near_gap, far_gap = folds[0] - folds[2], folds[1] - folds[3]
    e_part = late * jnp.where(flip, far_gap, near_gap)
    d_part = late * jnp.where(flip, near_gap, far_gap)
    both = jnp.concatenate([e_part, d_part], axis=0).astype(jnp.bfloat16)
    reals, imags = [], []
    for j in range(SPANS):
        if j % 2 == 0:
            signal = near + far if j == 0 else turn * (near - far)
            part = dot(signal.astype(jnp.bfloat16), table_ref[j])
            real, imag = part[:, :band], part[:, band:]
        else:
            mixed = dot(both, table_ref[j])
            e_c, e_s = mixed[:count, :band], mixed[:count, band:]
            d_c, d_s = mixed[count:, :band], mixed[count:, band:]
            real, imag = (e_c + d_s, e_s - d_c) if j == 1 else (e_c - d_s, e_s + d_c)
        reals.append(real.astype(jnp.bfloat16))
        imags.append(imag.astype(jnp.bfloat16))
    spectra = jnp.concatenate(reals + imags, axis=1)
    chosen = dot(take_ref[...], spectra)
    chosen_ref[...] = chosen.astype(jnp.bfloat16)
    a0, a1 = chosen[:lines, :F], chosen[:lines, F:]
    b0, b1 = chosen[lines:, :F], chosen[lines:, F:]
    cross_re = (a0 * b0 + a1 * b1).astype(jnp.bfloat16)
    cross_im = (a1 * b0 - a0 * b1).astype(jnp.bfloat16)
    partial = dot(jnp.concatenate([cross_re, cross_im], axis=1), lag_ref[...])
    packed = jnp.concatenate([chunk[tiles * rows :, :] for chunk in chunks], axis=0)
    seen = jnp.concatenate([dot(find_ref[h], packed) for h in range(LAGS // LANES)], axis=1)
    partial_ref[...] = partial - seen


def adjoint_kernel(blocks, own, chosen_ref, mine_ref, other_ref, table_ref, lag_ref, give_ref, *out_refs):
    fibre = lax.axis_index("fibre")
    band = F // SPANS
    lines = mine_ref.shape[0]
    count = blocks * own
    misfit = mine_ref[...] + other_ref[...]
    weights = jnp.where(misfit > -0.5 * MASKED, jnp.tanh(misfit), 0.0).astype(jnp.bfloat16)
    adjoint = dot(weights, lag_ref[...], _NT).astype(jnp.bfloat16).astype(jnp.float32)
    g0, g1 = adjoint[:, :F], adjoint[:, F:]
    a0 = chosen_ref[:lines, :F].astype(jnp.float32)
    a1 = chosen_ref[:lines, F:].astype(jnp.float32)
    b0 = chosen_ref[lines:, :F].astype(jnp.float32)
    b1 = chosen_ref[lines:, F:].astype(jnp.float32)
    low = jnp.bfloat16
    first = jnp.concatenate([(g0 * b0 - g1 * b1).astype(low), (g0 * b1 + g1 * b0).astype(low)], axis=1)
    second = jnp.concatenate([(g0 * a0 + g1 * a1).astype(low), (g0 * a1 - g1 * a0).astype(low)], axis=1)
    grad = dot(give_ref[...], jnp.concatenate([first, second], axis=0)).astype(low)
    even, odd = None, None
    for j in range(SPANS):
        real = grad[:, j * band : (j + 1) * band]
        imag = grad[:, F + j * band : F + (j + 1) * band]
        line = jnp.concatenate([real, imag], axis=1)
        if j % 2 == 0:
            part = dot(line, table_ref[j], _NT)
            even = (part, part) if j == 0 else (even[0] + part, even[1] - part)
        else:
            turned = jnp.concatenate([-imag, real], axis=1)
            part = dot(jnp.concatenate([line, turned], axis=0), table_ref[j], _NT)
            u, v = part[:count], part[count:]
            odd = (u, v) if j == 1 else (odd[0] + u, odd[1] - v)
    flip = fibre % 2 == 1
    late = jnp.where(fibre >= 2, -1.0, 1.0)
    for k, out_ref in enumerate(out_refs):
        other = flip if k % 2 == 0 else ~flip
        base = jnp.where(other, even[1], even[0])
        side = late * jnp.where(other, odd[1], odd[0])
        out_ref[...] = (base + side if k < 2 else base - side).astype(low)


def unpack_kernel(*refs):
    chunks, (order_ref, out_hbm, out, sems) = refs[:SPANS], refs[SPANS:]
    span = out.shape[0]
    cuts = [pl.ds(q * LANES, LANES) for q in range(span // LANES)]
    leave = [pltpu.make_async_copy(out.at[cut], out_hbm.at[cut], sems.at[q]) for q, cut in enumerate(cuts)]
    for q, copy in enumerate(leave):
        held = jnp.concatenate([chunk[:, q * LANES : (q + 1) * LANES] for chunk in chunks], axis=0)
        out[q * LANES : (q + 1) * LANES, :] = dot(held, order_ref[...], _TN).astype(jnp.bfloat16)
        copy.start()
    for copy in leave:
        copy.wait()


def by_own_k(records, pairs, observed, lag_mask):
    recs, segs, fibres = (lax.axis_size(axis) for axis in ("rec", "seg", "fibre"))
    own = BLOCK // fibres
    span, count = records.shape[1:]
    blocks = count // BLOCK
    rows = blocks * own
    pair_total, pairs_dev = pairs.shape[0], observed.shape[0]
    share = pairs_dev // recs
    lines = pair_total * own
    extra = 2 * LAGS // LANES * share * own
    table = forward_table().reshape(F // SPANS, SPANS, 2, SPANS, span)[:, :, :, 0]
    table = np.ascontiguousarray(table.transpose(1, 3, 2, 0)).reshape(SPANS, span, S // SPANS)
    lags = lag_table().reshape(F // SPANS, SPANS, 2, LAGS)
    lags = np.ascontiguousarray(lags.transpose(2, 1, 0, 3)).reshape(2 * F, LAGS)
    low = jnp.bfloat16
    vmem = pl.BlockSpec(memory_space=pltpu.VMEM)
    hbm = pl.BlockSpec(memory_space=pl.ANY)
    smem = pl.BlockSpec(memory_space=pltpu.SMEM)
    limit = pltpu.CompilerParams(vmem_limit_bytes=16 * 2**20)

    def along(axis, array, target):
        return lax.ppermute(array, axis, [(i, target(i)) for i in range(lax.axis_size(axis))])

    send = pl.pallas_call(
        functools.partial(pack_kernel, blocks, own),
        out_shape=[pltpu.VMEM((span // LANES * rows + extra, LANES), low)] * SPANS,
        in_specs=[hbm] * 3,
        out_specs=[vmem] * SPANS,
        scratch_shapes=[
            pltpu.VMEM((span, count), low),
            pltpu.VMEM((share, BLOCK, LAGS), jnp.float32),
            pltpu.VMEM(lag_mask.shape, jnp.int32),
            pltpu.SemaphoreType.DMA((3,)),
        ],
        compiler_params=limit,
    )(*(pltpu.with_memory_space_constraint(x, pltpu.HBM) for x in (records[0], observed, lag_mask)))
    held = [send[0]] + [along("fibre", send[k], lambda i: i ^ k) for k in range(1, SPANS)]
    for u in range(1, segs):
        held += [along("seg", chunk, lambda i: (i + u) % segs) for chunk in held[:SPANS]]
    constants = [jnp.asarray(c) for c in (table, lags)]
    table, lags, take, give, find, order = pl.pallas_call(
        functools.partial(prepare_kernel, segs, blocks, own, pairs_dev, share),
        out_shape=[pltpu.VMEM(c.shape, low) for c in constants]
        + [
            pltpu.VMEM((2 * lines, segs * rows), low),
            pltpu.VMEM((rows, 2 * lines), low),
            pltpu.VMEM((LAGS // LANES, lines, segs * SPANS * extra), low),
            pltpu.VMEM((count, count), low),
        ],
        in_specs=[smem] + [hbm] * len(constants),
        out_specs=[vmem] * (len(constants) + 4),
        scratch_shapes=[pltpu.SemaphoreType.DMA((len(constants),))],
        compiler_params=limit,
        cost_estimate=pl.CostEstimate(flops=0, bytes_accessed=4 * 2**20, transcendentals=0),
    )(pairs, *(pltpu.with_memory_space_constraint(c, pltpu.HBM) for c in constants))
    chosen, partial = pl.pallas_call(
        functools.partial(correlate_kernel, segs, blocks, own),
        out_shape=[pltpu.VMEM((2 * lines, 2 * F), low), pltpu.VMEM((lines, LAGS), jnp.float32)],
        in_specs=[vmem] * (segs * SPANS + 4),
        out_specs=[vmem] * 2,
        compiler_params=limit,
    )(*held, table, lags, take, find)
    mine, other = partial, along("rec", partial, lambda i: (i + 1) % recs)
    for _ in range(2, recs):
        mine, other = mine + other, along("rec", other, lambda i: (i + 1) % recs)
    back = pl.pallas_call(
        functools.partial(adjoint_kernel, blocks, own),
        out_shape=[pltpu.VMEM((rows, span), low)] * SPANS,
        in_specs=[vmem] * 6,
        out_specs=[vmem] * SPANS,
        compiler_params=limit,
    )(chosen, mine, other, table, lags, give)
    back = [back[0]] + [along("fibre", back[k], lambda i: i ^ k) for k in range(1, SPANS)]
    out = pl.pallas_call(
        unpack_kernel,
        out_shape=jax.ShapeDtypeStruct((span, count), low),
        in_specs=[vmem] * (SPANS + 1),
        out_specs=hbm,
        scratch_shapes=[
            pltpu.VMEM((span, count), low),
            pltpu.SemaphoreType.DMA((span // LANES,)),
        ],
        compiler_params=limit,
    )(*back, order)
    return out[None]


def by_band(records, pairs, observed, lag_mask):
    fibres, segs = lax.axis_size("fibre"), lax.axis_size("seg")
    own = BLOCK // fibres
    span, count = records.shape[1:]
    blocks = count // BLOCK
    total_blocks = blocks * segs
    pair_total, pairs_dev = pairs.shape[0], observed.shape[0]
    low = jnp.bfloat16
    band = F // segs
    start = lax.axis_index("seg") * band
    table = lax.dynamic_slice_in_dim(jnp.asarray(forward_table()), start, band, 0)
    lags = lax.dynamic_slice_in_dim(jnp.asarray(lag_table()), start, band, 0)
    f32 = functools.partial(jnp.einsum, preferred_element_type=jnp.float32)
    grid = records.reshape(span, blocks, fibres, own).transpose(2, 0, 1, 3)
    signal = lax.all_to_all(grid, "fibre", 0, 0, tiled=True).reshape(S, blocks, own)
    signal = lax.all_gather(signal, "seg", axis=1, tiled=True)
    spectra = f32("wpt,tbk->wpbk", table, signal).astype(low)
    ids = jnp.arange(total_blocks)
    take = [(pairs[:, side, None] == ids).astype(low) for side in range(2)]
    a0, a1 = (f32("nb,wbk->wnk", take[0], spectra[:, p]) for p in range(2))
    b0, b1 = (f32("nb,wbk->wnk", take[1], spectra[:, p]) for p in range(2))
    cross = jnp.stack([a0 * b0 + a1 * b1, a1 * b0 - a0 * b1], axis=1).astype(low)
    corr = f32("wpnk,wpl->nkl", cross, lags)
    corr = corr.reshape(fibres, segs, pairs_dev, own, LAGS)
    corr = lax.psum_scatter(corr, "seg", scatter_dimension=1)
    synthetic = lax.psum(corr, "rec").reshape(fibres * pairs_dev, own, LAGS)
    seen = observed.reshape(pairs_dev, fibres, own, LAGS).transpose(1, 0, 2, 3)
    seen = lax.all_to_all(seen, "fibre", 0, 0, tiled=True).reshape(fibres * pairs_dev, own, LAGS)
    window = lax.all_gather(lag_mask.astype(jnp.float32), "fibre", axis=0, tiled=True)
    weights = (window[:, None, :] * jnp.tanh(synthetic - seen)).astype(low)
    weights = lax.all_gather(weights.reshape(fibres, pairs_dev, own, LAGS), "seg", axis=1)
    weights = weights.reshape(pair_total, own, LAGS)
    adjoint = f32("nkl,wpl->wpnk", weights, lags).astype(low).astype(jnp.float32)
    g0, g1 = adjoint[:, 0], adjoint[:, 1]

    def added(side, terms):
        high = terms.astype(low)
        rest = (terms - high.astype(jnp.float32)).astype(low)
        return f32("nb,wnk->wbk", take[side], high) + f32("nb,wnk->wbk", take[side], rest)

    grad = jnp.stack(
        [
            added(0, g0 * b0 - g1 * b1) + added(1, g0 * a0 + g1 * a1),
            added(0, g0 * b1 + g1 * b0) + added(1, g0 * a1 - g1 * a0),
        ],
        axis=1,
    ).astype(low)
    sources = f32("wpbk,wpt->tbk", grad, table)
    sources = lax.psum_scatter(sources, "seg", scatter_dimension=1, tiled=True).astype(low)
    sources = sources.reshape(fibres, span, blocks, own)
    sources = lax.all_to_all(sources, "fibre", 0, 0, tiled=True)
    return sources.transpose(1, 2, 0, 3).reshape(1, span, count)


def solution(mesh):
    in_specs = (
        P("rec", "fibre", ("groups", "seg")),
        P(),
        P(("groups", "fibre", "seg"), None, None),
        P(("groups", "fibre", "seg"), None),
    )
    out_specs = P("rec", "fibre", ("groups", "seg"))
    small = mesh.shape["fibre"] == SPANS
    return jax.shard_map(
        by_own_k if small else by_band,
        mesh=mesh,
        in_specs=in_specs,
        out_specs=out_specs,
        check_vma=False,
    )
```

time: 36.6 us -> 33.8 us (0.923)
  blocking collectives: 12.9 us -> 0 us
  starting transfers between devices: 7.37 us -> 14.8 us
  waiting for transfers between devices: 7.26 us -> 10.1 us
    ppermute x0 -> x11, starting transfers between devices: none -> 14.8 us  [along(): lax.ppermute(array, axis, [(i, target(i)) for i in range(lax.axis_size(ax...]
    all_to_all x1 -> x0, blocking collectives: 12.9 us -> none  [by_own_k(): back = lax.all_to_all(back, EVERY, 0, 0, tiled=True)]
    ppermute x0 -> x11, waiting for transfers between devices: none -> 10.1 us  [along(): lax.ppermute(array, axis, [(i, target(i)) for i in range(lax.axis_size(ax...]
    all_to_all x1 -> x0, starting transfers between devices: 7.37 us -> none  [by_own_k(): held = lax.all_to_all(send, EVERY, 0, 0, tiled=True)]
    all_to_all x1 -> x0, waiting for transfers between devices: 7.26 us -> none  [by_own_k(): held = lax.all_to_all(send, EVERY, 0, 0, tiled=True)]
    unnamed x3 -> x1, local copies, waits for them, and re-layouts: 0.76 us -> 0.75 us
    pallas_call x3 -> x4, Pallas kernels: 6.99 us -> 6.99 us  [the longest x1 2.54 us: by_own_k(): pl.pallas_call(functools.partial(prepare_kernel, segs, blocks, own, pairs...]
  transfers between devices with their start and end apart: 1 -> 11, of which waited for: 1 -> 4; matrix products, arithmetic and copies ran while one was open for 2% -> 2% of each run, Pallas kernels for 7% -> 8%
where the time goes in v4:
time: 33.8 us; the launch traced here: 33.6 us
  starting transfers between devices  14.8 us (44%)
  waiting for transfers between devices  10.1 us (30%)
  Pallas kernels  7.93 us (23%)
  local copies, waits for them, and re-layouts  0.75 us (2%)
    ppermute x11, starting transfers between devices, along(): lax.ppermute(array, axis, [(i, target(i)) for i in range(lax.axis_size(ax...  14.8 us
    ppermute x11, waiting for transfers between devices, along(): lax.ppermute(array, axis, [(i, target(i)) for i in range(lax.axis_size(ax...  10.1 us
    pallas_call x1, Pallas kernels, by_own_k(): pl.pallas_call(functools.partial(prepare_kernel, segs, blocks, own, pairs...  2.54 us
    pallas_call x1, Pallas kernels, by_own_k(): pl.pallas_call(functools.partial(adjoint_kernel, blocks, own), out_shape=...  1.72 us
    pallas_call x1, Pallas kernels, by_own_k(): pl.pallas_call(functools.partial(correlate_kernel, segs, blocks, own), ou...  1.45 us
    pallas_call x1, Pallas kernels, by_own_k(): pl.pallas_call(functools.partial(pack_kernel, blocks, own), out_shape=[pl...  1.29 us
    pallas_call x1, Pallas kernels, by_own_k(): pl.pallas_call(unpack_kernel, out_shape=jax.ShapeDtypeStruct((span, count...  0.94 us
    unnamed x1, local copies, waits for them, and re-layouts  0.75 us
  transfers between devices with their start and end apart: 11, of which 4 were waited for; matrix products, arithmetic and copies ran while one was open for 2% of the time, Pallas kernels for 8%

profile of v4, /device:TPU:0, one launch (start us, length us, event | category | flops | bytes accessed | tf_op | source)
XLA Modules:
  0.0 33.6 jit_solution(1091819039474692766)
XLA Ops:
  0.0 1.3 %shard_map.64 = (bf16[288,128]{1,0:T(8,128)(2,1)S(1)}, bf16[288,128]{1,0:T(8,128)(2,1)S(1)}, bf16[288,128]{1,0:T(8,128)(2,1)S(1)}, bf16[288,128]{1,0:T(8,128)(2,1)S(1)}) custom-call(bf16[512,256]{1,0:T(8,128)(2,1)} %bitcast.2, f32[2,32,256]{2,1,0:T(8,128)} %observed_hbm.1, s32[2,256]{1,0:T(2,128)} %mask_hbm.1), custom_call_target="tpu_custom_call" | custom-call | tf_op jit(solution)/shard_map/pallas_call | solution.py:273
  1.3 3.1 %collective-permute-start = (bf16[288,128]{1,0:T(8,128)(2,1)S(1)}, bf16[288,128]{1,0:T(8,128)(2,1)S(1)}, u32[]{:S(2)}, u32[]{:S(2)}) collective-permute-start(bf16[288,128]{1,0:T(8,128)(2,1)S(1)} %get-tuple-element.22), channel_id=1, source_target_pairs={{0,4},{4,0},{8,12},{12,8},{1,5},{5,1},{9,13},{13,9},{2,6},{6,2},{1... | collective-permute-start | bytes 221192 | tf_op jit(solution)/shard_map/ppermute | solution.py:271
  4.4 2.6 %collective-permute-start.1 = (bf16[288,128]{1,0:T(8,128)(2,1)S(1)}, bf16[288,128]{1,0:T(8,128)(2,1)S(1)}, u32[]{:S(2)}, u32[]{:S(2)}) collective-permute-start(bf16[288,128]{1,0:T(8,128)(2,1)S(1)} %get-tuple-element.23), channel_id=1, source_target_pairs={{0,8},{4,12},{8,0},{12,4},{1,9},{5,13},{9,1},{13,5},{2,10},{6,14},... | collective-permute-start | bytes 221192 | tf_op jit(solution)/shard_map/ppermute | solution.py:271
  7.0 1.7 %collective-permute-start.3 = (bf16[288,128]{1,0:T(8,128)(2,1)S(1)}, bf16[288,128]{1,0:T(8,128)(2,1)S(1)}, u32[]{:S(2)}, u32[]{:S(2)}) collective-permute-start(bf16[288,128]{1,0:T(8,128)(2,1)S(1)} %get-tuple-element.21.refs_0_), channel_id=1, source_target_pairs={{0,2},{2,0},{1,3},{3,1},{4,6},{6,4},{5,7},{7,5},{8,10},{10,8},{9,1... | collective-permute-start | bytes 221192 | tf_op jit(solution)/shard_map/ppermute | solution.py:271
  8.7 0.3 collective-permute-start.4
  9.0 3.2 %collective-permute-done.1.refs_2_ = bf16[288,128]{1,0:T(8,128)(2,1)S(1)} collective-permute-done((bf16[288,128]{1,0:T(8,128)(2,1)S(1)}, bf16[288,128]{1,0:T(8,128)(2,1)S(1)}, u32[]{:S(2)}, u32[]{:S(2)}) %collective-permute-start.1) | collective-permute-done | bytes 73760 | tf_op jit(solution)/shard_map/ppermute | solution.py:271
  12.2 1.5 %collective-permute-start.5 = (bf16[288,128]{1,0:T(8,128)(2,1)S(1)}, bf16[288,128]{1,0:T(8,128)(2,1)S(1)}, u32[]{:S(2)}, u32[]{:S(2)}) collective-permute-start(bf16[288,128]{1,0:T(8,128)(2,1)S(1)} %collective-permute-done.1.refs_2_), channel_id=1, source_target_pairs={{0,2},{2,0},{1,3},{3,1},{4,6},{6,4},{5,7},{7,5},{8,10},{10,8},{9,1... | collective-permute-start | bytes 221192 | tf_op jit(solution)/shard_map/ppermute | solution.py:271
  13.7 0.0 collective-permute-done.2.refs_3_
  13.7 1.1 %collective-permute-start.6 = (bf16[288,128]{1,0:T(8,128)(2,1)S(1)}, bf16[288,128]{1,0:T(8,128)(2,1)S(1)}, u32[]{:S(2)}, u32[]{:S(2)}) collective-permute-start(bf16[288,128]{1,0:T(8,128)(2,1)S(1)} %collective-permute-done.2.refs_3_), channel_id=1, source_target_pairs={{0,2},{2,0},{1,3},{3,1},{4,6},{6,4},{5,7},{7,5},{8,10},{10,8},{9,1... | collective-permute-start | bytes 221192 | tf_op jit(solution)/shard_map/ppermute | solution.py:271
  14.7 0.8 %copy.7.pairs_ref = s32[16,2]{1,0:T(8,128)S(1)} copy(s32[16,2]{0,1:T(2,128)} %param.7) | data formatting | bytes 256 | tf_op args[1]
  15.5 2.5 %shard_map.65 = (bf16[4,512,512]{2,1,0:T(8,128)(2,1)S(1)}, bf16[2048,256]{1,0:T(8,128)(2,1)S(1)}, bf16[256,128]{1,0:T(8,128)(2,1)S(1)}, bf16[64,256]{1,0:T(8,128...) custom-call(s32[16,2]{1,0:T(8,128)S(1)} %copy.7.pairs_ref, ...), custom_call_target="tpu_custom_call" | custom-call | bytes 4194304 | tf_op jit(solution)/shard_map/pallas_call | solution.py:290
  18.0 0.0 collective-permute-done.3.refs_4_
  18.0 0.0 collective-permute-done.5.refs_6_
  18.1 0.0 collective-permute-done.6.refs_7_
  18.1 1.4 %shard_map.66 = (bf16[256,2048]{1,0:T(8,128)(2,1)S(1)}, f32[128,256]{1,0:T(8,128)S(1)}) custom-call(bf16[288,128]{1,0:T(8,128)(2,1)S(1)} %get-tuple-element.21.refs_0_, bf16[288,128]{1,0:T(8,128)(2,1)S(1)} %collective-permute-done.refs_1_, bf16[288,128]{1,0:T(8,128)(2,1)S(1)} %collective-permute-done.1.refs_2_, ...), custom_call_target="tpu_custom_call" | custom-call | tf_op jit(solution)/shard_map/pallas_call | solution.py:305
  19.5 0.1 collective-permute-start.7
  19.6 1.3 %collective-permute-done.7.other_ref = f32[128,256]{1,0:T(8,128)S(1)} collective-permute-done((f32[128,256]{1,0:T(8,128)S(1)}, f32[128,256]{1,0:T(8,128)S(1)}, u32[]{:S(2)}, u32[]{:S(2)}) %collective-permute-start.7) | collective-permute-done | bytes 131104 | tf_op jit(solution)/shard_map/ppermute | solution.py:271
  20.9 1.7 %shard_map.67 = (bf16[64,512]{1,0:T(8,128)(2,1)S(1)}, bf16[64,512]{1,0:T(8,128)(2,1)S(1)}, bf16[64,512]{1,0:T(8,128)(2,1)S(1)}, bf16[64,512]{1,0:T(8,128)(2,1)S(1)}) custom-call(bf16[256,2048]{1,0:T(8,128)(2,1)S(1)} %get-tuple-element.29.chosen_ref, f32[128,256]{1,0:T(8,128)S(1)} %get-tuple-element.30.mine_ref, ...), custom_call_target="tpu_custom_call" | custom-call | tf_op jit(solution)/shard_map/pallas_call | solution.py:315
  22.7 1.1 %collective-permute-start.8 = (bf16[64,512]{1,0:T(8,128)(2,1)S(1)}, bf16[64,512]{1,0:T(8,128)(2,1)S(1)}, u32[]{:S(2)}, u32[]{:S(2)}) collective-permute-start(bf16[64,512]{1,0:T(8,128)(2,1)S(1)} %get-tuple-element.33), channel_id=1, source_target_pairs={{0,4},{4,0},{8,12},{12,8},{1,5},{5,1},{9,13},{13,9},{2,6},{6,2},{1... | collective-permute-start | bytes 196616 | tf_op jit(solution)/shard_map/ppermute | solution.py:271
  23.8 2.7 %collective-permute-start.9 = (bf16[64,512]{1,0:T(8,128)(2,1)S(1)}, bf16[64,512]{1,0:T(8,128)(2,1)S(1)}, u32[]{:S(2)}, u32[]{:S(2)}) collective-permute-start(bf16[64,512]{1,0:T(8,128)(2,1)S(1)} %get-tuple-element.34), channel_id=1, source_target_pairs={{0,8},{4,12},{8,0},{12,4},{1,9},{5,13},{9,1},{13,5},{2,10},{6,14},... | collective-permute-start | bytes 196616 | tf_op jit(solution)/shard_map/ppermute | solution.py:271
  26.5 0.6 %collective-permute-start.10 = (bf16[64,512]{1,0:T(8,128)(2,1)S(1)}, bf16[64,512]{1,0:T(8,128)(2,1)S(1)}, u32[]{:S(2)}, u32[]{:S(2)}) collective-permute-start(bf16[64,512]{1,0:T(8,128)(2,1)S(1)} %get-tuple-element.35), channel_id=1, source_target_pairs={{0,12},{4,8},{8,4},{12,0},{1,13},{5,9},{9,5},{13,1},{2,14},{6,10},... | collective-permute-start | bytes 196616 | tf_op jit(solution)/shard_map/ppermute | solution.py:271
  27.1 4.2 %collective-permute-done.9.refs_2_ = bf16[64,512]{1,0:T(8,128)(2,1)S(1)} collective-permute-done((bf16[64,512]{1,0:T(8,128)(2,1)S(1)}, bf16[64,512]{1,0:T(8,128)(2,1)S(1)}, u32[]{:S(2)}, u32[]{:S(2)}) %collective-permute-start.9) | collective-permute-done | bytes 65568 | tf_op jit(solution)/shard_map/ppermute | solution.py:271
  31.3 1.3 %collective-permute-done.10.refs_3_ = bf16[64,512]{1,0:T(8,128)(2,1)S(1)} collective-permute-done((bf16[64,512]{1,0:T(8,128)(2,1)S(1)}, bf16[64,512]{1,0:T(8,128)(2,1)S(1)}, u32[]{:S(2)}, u32[]{:S(2)}) %collective-permute-start.10) | collective-permute-done | bytes 65568 | tf_op jit(solution)/shard_map/ppermute | solution.py:271
  32.7 0.9 %shard_map.68 = bf16[512,256]{1,0:T(8,128)(2,1)} custom-call(bf16[64,512]{1,0:T(8,128)(2,1)S(1)} %get-tuple-element.32.refs_0_, bf16[64,512]{1,0:T(8,128)(2,1)S(1)} %collective-permute-done.8.refs_1_, bf16[64,512]{1,0:T(8,128)(2,1)S(1)} %collective-permute-done.9.refs_2_, bf16[64,512]{1,0:T(8,128)(2,1)S(1)} %collective-permute-done.10.refs_3_, ...), custom_call_target="tpu_custom_call" | custom-call | tf_op jit(solution)/shard_map/pallas_call | solution.py:323
  (4 shorter events, 0.0 us)
Async XLA Ops:
  1.3 7.4 %collective-permute-start = (bf16[288,128]{1,0:T(8,128)(2,1)S(1)}, bf16[288,128]{1,0:T(8,128)(2,1)S(1)}, u32[]{:S(2)}, u32[]{:S(2)}) collective-permute-start(bf16[288,128]{1,0:T(8,128)(2,1)S(1)} %get-tuple-element.22), channel_id=1, source_target_pairs={{0,4},{4,0},{8,12},{12,8},{1,5},{5,1},{9,13},{13,9},{2,6},{6,2},{1... | collective-permute-start | bytes 221192 | tf_op jit(solution)/shard_map/ppermute | solution.py:271
  4.4 7.8 %collective-permute-start.1 = (bf16[288,128]{1,0:T(8,128)(2,1)S(1)}, bf16[288,128]{1,0:T(8,128)(2,1)S(1)}, u32[]{:S(2)}, u32[]{:S(2)}) collective-permute-start(bf16[288,128]{1,0:T(8,128)(2,1)S(1)} %get-tuple-element.23), channel_id=1, source_target_pairs={{0,8},{4,12},{8,0},{12,4},{1,9},{5,13},{9,1},{13,5},{2,10},{6,14},... | collective-permute-start | bytes 221192 | tf_op jit(solution)/shard_map/ppermute | solution.py:271
  7.0 6.7 %collective-permute-start.2 = (bf16[288,128]{1,0:T(8,128)(2,1)S(1)}, bf16[288,128]{1,0:T(8,128)(2,1)S(1)}, u32[]{:S(2)}, u32[]{:S(2)}) collective-permute-start(bf16[288,128]{1,0:T(8,128)(2,1)S(1)} %get-tuple-element.24), channel_id=1, source_target_pairs={{0,12},{4,8},{8,4},{12,0},{1,13},{5,9},{9,5},{13,1},{2,14},{6,10},... | collective-permute-start | bytes 221192 | tf_op jit(solution)/shard_map/ppermute | solution.py:271
  7.0 11.0 %collective-permute-start.3 = (bf16[288,128]{1,0:T(8,128)(2,1)S(1)}, bf16[288,128]{1,0:T(8,128)(2,1)S(1)}, u32[]{:S(2)}, u32[]{:S(2)}) collective-permute-start(bf16[288,128]{1,0:T(8,128)(2,1)S(1)} %get-tuple-element.21.refs_0_), channel_id=1, source_target_pairs={{0,2},{2,0},{1,3},{3,1},{4,6},{6,4},{5,7},{7,5},{8,10},{10,8},{9,1... | collective-permute-start | bytes 221192 | tf_op jit(solution)/shard_map/ppermute | solution.py:271
  8.7 9.3 %collective-permute-start.4 = (bf16[288,128]{1,0:T(8,128)(2,1)S(1)}, bf16[288,128]{1,0:T(8,128)(2,1)S(1)}, u32[]{:S(2)}, u32[]{:S(2)}) collective-permute-start(bf16[288,128]{1,0:T(8,128)(2,1)S(1)} %collective-permute-done.refs_1_), channel_id=1, source_target_pairs={{0,2},{2,0},{1,3},{3,1},{4,6},{6,4},{5,7},{7,5},{8,10},{10,8},{9,1... | collective-permute-start | bytes 221192 | tf_op jit(solution)/shard_map/ppermute | solution.py:271
  12.2 5.9 %collective-permute-start.5 = (bf16[288,128]{1,0:T(8,128)(2,1)S(1)}, bf16[288,128]{1,0:T(8,128)(2,1)S(1)}, u32[]{:S(2)}, u32[]{:S(2)}) collective-permute-start(bf16[288,128]{1,0:T(8,128)(2,1)S(1)} %collective-permute-done.1.refs_2_), channel_id=1, source_target_pairs={{0,2},{2,0},{1,3},{3,1},{4,6},{6,4},{5,7},{7,5},{8,10},{10,8},{9,1... | collective-permute-start | bytes 221192 | tf_op jit(solution)/shard_map/ppermute | solution.py:271
  13.7 4.4 %collective-permute-start.6 = (bf16[288,128]{1,0:T(8,128)(2,1)S(1)}, bf16[288,128]{1,0:T(8,128)(2,1)S(1)}, u32[]{:S(2)}, u32[]{:S(2)}) collective-permute-start(bf16[288,128]{1,0:T(8,128)(2,1)S(1)} %collective-permute-done.2.refs_3_), channel_id=1, source_target_pairs={{0,2},{2,0},{1,3},{3,1},{4,6},{6,4},{5,7},{7,5},{8,10},{10,8},{9,1... | collective-permute-start | bytes 221192 | tf_op jit(solution)/shard_map/ppermute | solution.py:271
  19.5 1.4 %collective-permute-start.7 = (f32[128,256]{1,0:T(8,128)S(1)}, f32[128,256]{1,0:T(8,128)S(1)}, u32[]{:S(2)}, u32[]{:S(2)}) collective-permute-start(f32[128,256]{1,0:T(8,128)S(1)} %get-tuple-element.30.mine_ref), channel_id=1, source_target_pairs={{0,1},{1,0},{2,3},{3,2},{4,5},{5,4},{6,7},{7,6},{8,9},{9,8},{10,11... | collective-permute-start | bytes 393224 | tf_op jit(solution)/shard_map/ppermute | solution.py:271
  22.7 4.5 %collective-permute-start.8 = (bf16[64,512]{1,0:T(8,128)(2,1)S(1)}, bf16[64,512]{1,0:T(8,128)(2,1)S(1)}, u32[]{:S(2)}, u32[]{:S(2)}) collective-permute-start(bf16[64,512]{1,0:T(8,128)(2,1)S(1)} %get-tuple-element.33), channel_id=1, source_target_pairs={{0,4},{4,0},{8,12},{12,8},{1,5},{5,1},{9,13},{13,9},{2,6},{6,2},{1... | collective-permute-start | bytes 196616 | tf_op jit(solution)/shard_map/ppermute | solution.py:271
  23.8 7.5 %collective-permute-start.9 = (bf16[64,512]{1,0:T(8,128)(2,1)S(1)}, bf16[64,512]{1,0:T(8,128)(2,1)S(1)}, u32[]{:S(2)}, u32[]{:S(2)}) collective-permute-start(bf16[64,512]{1,0:T(8,128)(2,1)S(1)} %get-tuple-element.34), channel_id=1, source_target_pairs={{0,8},{4,12},{8,0},{12,4},{1,9},{5,13},{9,1},{13,5},{2,10},{6,14},... | collective-permute-start | bytes 196616 | tf_op jit(solution)/shard_map/ppermute | solution.py:271
  26.5 6.2 %collective-permute-start.10 = (bf16[64,512]{1,0:T(8,128)(2,1)S(1)}, bf16[64,512]{1,0:T(8,128)(2,1)S(1)}, u32[]{:S(2)}, u32[]{:S(2)}) collective-permute-start(bf16[64,512]{1,0:T(8,128)(2,1)S(1)} %get-tuple-element.35), channel_id=1, source_target_pairs={{0,12},{4,8},{8,4},{12,0},{1,13},{5,9},{9,5},{13,1},{2,14},{6,10},... | collective-permute-start | bytes 196616 | tf_op jit(solution)/shard_map/ppermute | solution.py:271

commit v5 on v4

--- a/solution.py
+++ b/solution.py
@@ -101,24 +101,38 @@
             out_ref[q * rows : (q + 1) * rows, :] = part
 
 
-def prepare_kernel(segs, blocks, own, pairs_dev, share, pairs_ref, *refs):
-    constants = (len(refs) - 5) // 2
-    take_ref, give_ref, find_ref, order_ref, sems = refs[2 * constants :]
+def prepare_kernel(segs, blocks, own, pairs_dev, share, pairs_hbm, *refs):
+    constants = (len(refs) - 6) // 2
+    take_ref, give_ref, find_ref, order_ref, pairs_ref, sems = refs[2 * constants :]
+    pairs_copy = pltpu.make_async_copy(pairs_hbm, pairs_ref, sems.at[constants])
     copies = [pltpu.make_async_copy(refs[i], refs[constants + i], sems.at[i]) for i in range(constants)]
-    for copy in copies:
+    for copy in [pairs_copy] + copies:
         copy.start()
     fibre, seg, rec = (lax.axis_index(axis) for axis in ("fibre", "seg", "rec"))
-    pair_total = pairs_ref.shape[0]
+    pair_total = pairs_ref.shape[1]
     rows = blocks * own
     lines = pair_total * own
 
     def picks(side, line):
         block = jnp.zeros_like(line)
         for n in range(pair_total):
-            block = jnp.where(line // own == n, pairs_ref[n, side], block)
+            block = jnp.where(line // own == n, pairs_ref[side, n], block)
         distance = (seg + segs - block // blocks) % segs
         return distance * rows + block % blocks * own + line % own
 
+    halves = LAGS // LANES
+    extra = 2 * halves * share * own
+
+    def here(half, line, place):
+        part = place % extra
+        owner = (place // extra % SPANS ^ fibre) * segs + (seg + segs - place // (extra * SPANS)) % segs
+        pair = owner * pairs_dev + rec * share + part // (2 * halves * own)
+        return (line // own == pair) & (line % own == part % own) & (part % (halves * own) // own == half)
+
+    for h in range(halves):
+        find_ref[h] = one_hot(lines, segs * SPANS * extra, functools.partial(here, h))
+    order_ref[...] = channel_order(fibre, blocks, own)
+    pairs_copy.wait()
     for side in range(2):
         line = lax.broadcasted_iota(jnp.int32, (lines, segs * rows), 0)
         row = lax.broadcasted_iota(jnp.int32, (lines, segs * rows), 1)
@@ -128,24 +142,12 @@
         row = lax.broadcasted_iota(jnp.int32, (rows, lines), 0)
         hit = jnp.where(picks(side, line) == row, 1.0, 0.0).astype(jnp.bfloat16)
         give_ref[:, side * lines : (side + 1) * lines] = hit
-    halves = LAGS // LANES
-    extra = 2 * halves * share * own
-
-    def here(half, line, place):
-        part = place % extra
-        owner = (place // extra % SPANS ^ fibre) * segs + (seg + segs - place // (extra * SPANS)) % segs
-        pair = owner * pairs_dev + rec * share + part // (2 * halves * own)
-        return (line // own == pair) & (line % own == part % own) & (part % (halves * own) // own == half)
-
-    for h in range(halves):
-        find_ref[h] = one_hot(lines, segs * SPANS * extra, functools.partial(here, h))
-    order_ref[...] = channel_order(fibre, blocks, own)
     for copy in copies:
         copy.wait()
 
 
 def correlate_kernel(segs, blocks, own, *refs):
-    chunks = refs[: segs * SPANS]
+    chunks = refs[segs * SPANS - 1 :: -1]
     table_ref, lag_ref, take_ref, find_ref, chosen_ref, partial_ref = refs[segs * SPANS :]
     fibre = lax.axis_index("fibre")
     span = S // SPANS
@@ -235,7 +237,7 @@
 
 
 def unpack_kernel(*refs):
-    chunks, (order_ref, out_hbm, out, sems) = refs[:SPANS], refs[SPANS:]
+    chunks, (order_ref, out_hbm, out, sems) = refs[SPANS - 1 :: -1], refs[SPANS:]
     span = out.shape[0]
     cuts = [pl.ds(q * LANES, LANES) for q in range(span // LANES)]
     leave = [pltpu.make_async_copy(out.at[cut], out_hbm.at[cut], sems.at[q]) for q, cut in enumerate(cuts)]
@@ -264,7 +266,6 @@
     low = jnp.bfloat16
     vmem = pl.BlockSpec(memory_space=pltpu.VMEM)
     hbm = pl.BlockSpec(memory_space=pl.ANY)
-    smem = pl.BlockSpec(memory_space=pltpu.SMEM)
     limit = pltpu.CompilerParams(vmem_limit_bytes=16 * 2**20)
 
     def along(axis, array, target):
@@ -283,9 +284,8 @@
         ],
         compiler_params=limit,
     )(*(pltpu.with_memory_space_constraint(x, pltpu.HBM) for x in (records[0], observed, lag_mask)))
-    held = [send[0]] + [along("fibre", send[k], lambda i: i ^ k) for k in range(1, SPANS)]
-    for u in range(1, segs):
-        held += [along("seg", chunk, lambda i: (i + u) % segs) for chunk in held[:SPANS]]
+    held = [along("fibre", send[k], lambda i: i ^ k) for k in range(SPANS - 1, 0, -1)]
+    held = [send[0]] + held[::-1]
     constants = [jnp.asarray(c) for c in (table, lags)]
     table, lags, take, give, find, order = pl.pallas_call(
         functools.partial(prepare_kernel, segs, blocks, own, pairs_dev, share),
@@ -296,19 +296,26 @@
             pltpu.VMEM((LAGS // LANES, lines, segs * SPANS * extra), low),
             pltpu.VMEM((count, count), low),
         ],
-        in_specs=[smem] + [hbm] * len(constants),
+        in_specs=[hbm] * (1 + len(constants)),
         out_specs=[vmem] * (len(constants) + 4),
-        scratch_shapes=[pltpu.SemaphoreType.DMA((len(constants),))],
+        scratch_shapes=[pltpu.SMEM(pairs.shape[::-1], jnp.int32), pltpu.SemaphoreType.DMA((1 + len(constants),))],
         compiler_params=limit,
         cost_estimate=pl.CostEstimate(flops=0, bytes_accessed=4 * 2**20, transcendentals=0),
-    )(pairs, *(pltpu.with_memory_space_constraint(c, pltpu.HBM) for c in constants))
+    )(*(pltpu.with_memory_space_constraint(c, pltpu.HBM) for c in [pairs.T] + constants))
+    for u in range(1, segs):
+        held += [
+            along(("fibre", "seg"), send[k], lambda i: (i // segs ^ k) * segs + (i + u) % segs)
+            if k in (1,)
+            else along("seg", held[k], lambda i: (i + u) % segs)
+            for k in range(SPANS - 1, -1, -1)
+        ][::-1]
     chosen, partial = pl.pallas_call(
         functools.partial(correlate_kernel, segs, blocks, own),
         out_shape=[pltpu.VMEM((2 * lines, 2 * F), low), pltpu.VMEM((lines, LAGS), jnp.float32)],
         in_specs=[vmem] * (segs * SPANS + 4),
         out_specs=[vmem] * 2,
         compiler_params=limit,
-    )(*held, table, lags, take, find)
+    )(*held[::-1], table, lags, take, find)
     mine, other = partial, along("rec", partial, lambda i: (i + 1) % recs)
     for _ in range(2, recs):
         mine, other = mine + other, along("rec", other, lambda i: (i + 1) % recs)
@@ -319,7 +326,9 @@
         out_specs=[vmem] * SPANS,
         compiler_params=limit,
     )(chosen, mine, other, table, lags, give)
-    back = [back[0]] + [along("fibre", back[k], lambda i: i ^ k) for k in range(1, SPANS)]
+    own_part = back[0]
+    back = [along("fibre", back[k], lambda i: i ^ k) for k in range(SPANS - 1, 0, -1)][::-1]
+    back = [own_part] + back
     out = pl.pallas_call(
         unpack_kernel,
         out_shape=jax.ShapeDtypeStruct((span, count), low),
@@ -330,7 +339,7 @@
             pltpu.SemaphoreType.DMA((span // LANES,)),
         ],
         compiler_params=limit,
-    )(*back, order)
+    )(*back[::-1], order)
     return out[None]
 
 

time: 33.8 us -> 31.9 us (0.944)
  waiting for transfers between devices: 10.1 us -> 8.26 us
  starting transfers between devices: 14.8 us -> 16.1 us
  local copies, waits for them, and re-layouts: 0.75 us -> 0 us
  Pallas kernels: 7.93 us -> 7.26 us
    ppermute x11, waiting for transfers between devices: 10.1 us -> 8.26 us  [along(): lax.ppermute(array, axis, [(i, target(i)) for i in range(lax.axis_size(ax...]
    ppermute x11, starting transfers between devices: 14.8 us -> 16.1 us  [along(): lax.ppermute(array, axis, [(i, target(i)) for i in range(lax.axis_size(ax...]
    unnamed x1 -> x0, local copies, waits for them, and re-layouts: 0.75 us -> none
    pallas_call x1, Pallas kernels: 2.54 us -> 1.88 us  [by_own_k(): pl.pallas_call(functools.partial(prepare_kernel, segs, blocks, own, pairs...]
  transfers between devices with their start and end apart: 11 -> 11, of which waited for: 4 -> 5; matrix products, arithmetic and copies ran while one was open for 2% -> 0% of each run, Pallas kernels for 8% -> 6%
where the time goes in v5:
time: 31.9 us; the launch traced here: 31.7 us
  starting transfers between devices  16.1 us (50%)
  waiting for transfers between devices  8.26 us (26%)
  Pallas kernels  7.26 us (23%)
    ppermute x11, starting transfers between devices, along(): lax.ppermute(array, axis, [(i, target(i)) for i in range(lax.axis_size(ax...  16.1 us
    ppermute x11, waiting for transfers between devices, along(): lax.ppermute(array, axis, [(i, target(i)) for i in range(lax.axis_size(ax...  8.26 us
    pallas_call x1, Pallas kernels, by_own_k(): pl.pallas_call(functools.partial(prepare_kernel, segs, blocks, own, pairs...  1.88 us
    pallas_call x1, Pallas kernels, by_own_k(): pl.pallas_call(functools.partial(adjoint_kernel, blocks, own), out_shape=...  1.72 us
    pallas_call x1, Pallas kernels, by_own_k(): pl.pallas_call(functools.partial(correlate_kernel, segs, blocks, own), ou...  1.43 us
    pallas_call x1, Pallas kernels, by_own_k(): pl.pallas_call(functools.partial(pack_kernel, blocks, own), out_shape=[pl...  1.29 us
    pallas_call x1, Pallas kernels, by_own_k(): pl.pallas_call(unpack_kernel, out_shape=jax.ShapeDtypeStruct((span, count...  0.94 us
  transfers between devices with their start and end apart: 11, of which 5 were waited for; matrix products, arithmetic and copies ran while one was open for 0% of the time, Pallas kernels for 6%

profile of v5, /device:TPU:0, one launch (start us, length us, event | category | flops | bytes accessed | tf_op | source)
XLA Modules:
  0.0 31.7 jit_solution(16848350118393537313)
XLA Ops:
  0.0 1.3 %shard_map.64 = (bf16[288,128]{1,0:T(8,128)(2,1)S(1)}, bf16[288,128]{1,0:T(8,128)(2,1)S(1)}, bf16[288,128]{1,0:T(8,128)(2,1)S(1)}, bf16[288,128]{1,0:T(8,128)(2,1)S(1)}) custom-call(bf16[512,256]{1,0:T(8,128)(2,1)} %bitcast.3, f32[2,32,256]{2,1,0:T(8,128)} %observed_hbm.1, s32[2,256]{1,0:T(2,128)} %mask_hbm.1), custom_call_target="tpu_custom_call" | custom-call | tf_op jit(solution)/shard_map/pallas_call | solution.py:274
  1.3 5.1 %collective-permute-start = (bf16[288,128]{1,0:T(8,128)(2,1)S(1)}, bf16[288,128]{1,0:T(8,128)(2,1)S(1)}, u32[]{:S(2)}, u32[]{:S(2)}) collective-permute-start(bf16[288,128]{1,0:T(8,128)(2,1)S(1)} %get-tuple-element.21), channel_id=1, source_target_pairs={{0,12},{4,8},{8,4},{12,0},{1,13},{5,9},{9,5},{13,1},{2,14},{6,10},... | collective-permute-start | bytes 221192 | tf_op jit(solution)/shard_map/ppermute | solution.py:272
  6.4 0.0 collective-permute-start.2
  6.4 0.6 %collective-permute-start.6 = (bf16[288,128]{1,0:T(8,128)(2,1)S(1)}, bf16[288,128]{1,0:T(8,128)(2,1)S(1)}, u32[]{:S(2)}, u32[]{:S(2)}) collective-permute-start(bf16[288,128]{1,0:T(8,128)(2,1)S(1)} %get-tuple-element.23), channel_id=1, source_target_pairs={{0,4},{4,0},{8,12},{12,8},{1,5},{5,1},{9,13},{13,9},{2,6},{6,2},{1... | collective-permute-start | bytes 221192 | tf_op jit(solution)/shard_map/ppermute | solution.py:272
  7.1 2.3 %collective-permute-start.4 = (bf16[288,128]{1,0:T(8,128)(2,1)S(1)}, bf16[288,128]{1,0:T(8,128)(2,1)S(1)}, u32[]{:S(2)}, u32[]{:S(2)}) collective-permute-start(bf16[288,128]{1,0:T(8,128)(2,1)S(1)} %get-tuple-element.23), channel_id=1, source_target_pairs={{0,6},{2,4},{4,2},{6,0},{8,14},{10,12},{12,10},{14,8},{1,7},{3,5},... | collective-permute-start | bytes 221192 | tf_op jit(solution)/shard_map/ppermute | solution.py:272
  9.4 0.5 %collective-permute-start.5 = (bf16[288,128]{1,0:T(8,128)(2,1)S(1)}, bf16[288,128]{1,0:T(8,128)(2,1)S(1)}, u32[]{:S(2)}, u32[]{:S(2)}) collective-permute-start(bf16[288,128]{1,0:T(8,128)(2,1)S(1)} %get-tuple-element.24.refs_7_), channel_id=1, source_target_pairs={{0,2},{2,0},{1,3},{3,1},{4,6},{6,4},{5,7},{7,5},{8,10},{10,8},{9,1... | collective-permute-start | bytes 221192 | tf_op jit(solution)/shard_map/ppermute | solution.py:272
  9.9 1.5 %collective-permute-start.1 = (bf16[288,128]{1,0:T(8,128)(2,1)S(1)}, bf16[288,128]{1,0:T(8,128)(2,1)S(1)}, u32[]{:S(2)}, u32[]{:S(2)}) collective-permute-start(bf16[288,128]{1,0:T(8,128)(2,1)S(1)} %collective-permute-done.refs_4_), channel_id=1, source_target_pairs={{0,2},{2,0},{1,3},{3,1},{4,6},{6,4},{5,7},{7,5},{8,10},{10,8},{9,1... | collective-permute-start | bytes 221192 | tf_op jit(solution)/shard_map/ppermute | solution.py:272
  11.4 1.3 %collective-permute-done.2.refs_5_ = bf16[288,128]{1,0:T(8,128)(2,1)S(1)} collective-permute-done((bf16[288,128]{1,0:T(8,128)(2,1)S(1)}, bf16[288,128]{1,0:T(8,128)(2,1)S(1)}, u32[]{:S(2)}, u32[]{:S(2)}) %collective-permute-start.2) | collective-permute-done | bytes 73760 | tf_op jit(solution)/shard_map/ppermute | solution.py:272
  12.7 1.5 %collective-permute-start.3 = (bf16[288,128]{1,0:T(8,128)(2,1)S(1)}, bf16[288,128]{1,0:T(8,128)(2,1)S(1)}, u32[]{:S(2)}, u32[]{:S(2)}) collective-permute-start(bf16[288,128]{1,0:T(8,128)(2,1)S(1)} %collective-permute-done.2.refs_5_), channel_id=1, source_target_pairs={{0,2},{2,0},{1,3},{3,1},{4,6},{6,4},{5,7},{7,5},{8,10},{10,8},{9,1... | collective-permute-start | bytes 221192 | tf_op jit(solution)/shard_map/ppermute | solution.py:272
  14.2 1.9 %shard_map.65 = (bf16[4,512,512]{2,1,0:T(8,128)(2,1)S(1)}, bf16[2048,256]{1,0:T(8,128)(2,1)S(1)}, bf16[256,128]{1,0:T(8,128)(2,1)S(1)}, bf16[64,256]{1,0:T(8,128...) custom-call(s32[2,16]{1,0:T(2,128)} %bitcast.4, bf16[4,512,512]{2,1,0:T(8,128)(2,1)} %constant.4.clone.refs_0_, ...), custom_call_target="tpu_custom_call" | custom-call | bytes 4194304 | tf_op jit(solution)/shard_map/pallas_call | solution.py:290
  16.1 0.0 collective-permute-done.6.refs_6_
  16.1 0.0 collective-permute-done.1.refs_0_
  16.2 0.9 %collective-permute-done.3.refs_1_ = bf16[288,128]{1,0:T(8,128)(2,1)S(1)} collective-permute-done((bf16[288,128]{1,0:T(8,128)(2,1)S(1)}, bf16[288,128]{1,0:T(8,128)(2,1)S(1)}, u32[]{:S(2)}, u32[]{:S(2)}) %collective-permute-start.3) | collective-permute-done | bytes 73760 | tf_op jit(solution)/shard_map/ppermute | solution.py:272
  17.1 1.4 %shard_map.66 = (bf16[256,2048]{1,0:T(8,128)(2,1)S(1)}, f32[128,256]{1,0:T(8,128)S(1)}) custom-call(bf16[288,128]{1,0:T(8,128)(2,1)S(1)} %collective-permute-done.1.refs_0_, bf16[288,128]{1,0:T(8,128)(2,1)S(1)} %collective-permute-done.3.refs_1_, bf16[288,128]{1,0:T(8,128)(2,1)S(1)} %collective-permute-done.4.refs_2_, ...), custom_call_target="tpu_custom_call" | custom-call | tf_op jit(solution)/shard_map/pallas_call | solution.py:312
  18.6 0.1 collective-permute-start.7
  18.6 1.3 %collective-permute-done.7.other_ref = f32[128,256]{1,0:T(8,128)S(1)} collective-permute-done((f32[128,256]{1,0:T(8,128)S(1)}, f32[128,256]{1,0:T(8,128)S(1)}, u32[]{:S(2)}, u32[]{:S(2)}) %collective-permute-start.7) | collective-permute-done | bytes 131104 | tf_op jit(solution)/shard_map/ppermute | solution.py:272
  20.0 1.7 %shard_map.67 = (bf16[64,512]{1,0:T(8,128)(2,1)S(1)}, bf16[64,512]{1,0:T(8,128)(2,1)S(1)}, bf16[64,512]{1,0:T(8,128)(2,1)S(1)}, bf16[64,512]{1,0:T(8,128)(2,1)S(1)}) custom-call(bf16[256,2048]{1,0:T(8,128)(2,1)S(1)} %get-tuple-element.29.chosen_ref, f32[128,256]{1,0:T(8,128)S(1)} %get-tuple-element.30.mine_ref, ...), custom_call_target="tpu_custom_call" | custom-call | tf_op jit(solution)/shard_map/pallas_call | solution.py:322
  21.7 2.8 %collective-permute-start.8 = (bf16[64,512]{1,0:T(8,128)(2,1)S(1)}, bf16[64,512]{1,0:T(8,128)(2,1)S(1)}, u32[]{:S(2)}, u32[]{:S(2)}) collective-permute-start(bf16[64,512]{1,0:T(8,128)(2,1)S(1)} %get-tuple-element.32), channel_id=1, source_target_pairs={{0,12},{4,8},{8,4},{12,0},{1,13},{5,9},{9,5},{13,1},{2,14},{6,10},... | collective-permute-start | bytes 196616 | tf_op jit(solution)/shard_map/ppermute | solution.py:272
  24.5 0.0 collective-permute-start.9
  24.5 1.6 %collective-permute-start.10 = (bf16[64,512]{1,0:T(8,128)(2,1)S(1)}, bf16[64,512]{1,0:T(8,128)(2,1)S(1)}, u32[]{:S(2)}, u32[]{:S(2)}) collective-permute-start(bf16[64,512]{1,0:T(8,128)(2,1)S(1)} %get-tuple-element.34), channel_id=1, source_target_pairs={{0,4},{4,0},{8,12},{12,8},{1,5},{5,1},{9,13},{13,9},{2,6},{6,2},{1... | collective-permute-start | bytes 196616 | tf_op jit(solution)/shard_map/ppermute | solution.py:272
  26.1 2.3 %collective-permute-done.8.refs_0_ = bf16[64,512]{1,0:T(8,128)(2,1)S(1)} collective-permute-done((bf16[64,512]{1,0:T(8,128)(2,1)S(1)}, bf16[64,512]{1,0:T(8,128)(2,1)S(1)}, u32[]{:S(2)}, u32[]{:S(2)}) %collective-permute-start.8) | collective-permute-done | bytes 65568 | tf_op jit(solution)/shard_map/ppermute | solution.py:272
  28.4 2.3 %collective-permute-done.9.refs_1_ = bf16[64,512]{1,0:T(8,128)(2,1)S(1)} collective-permute-done((bf16[64,512]{1,0:T(8,128)(2,1)S(1)}, bf16[64,512]{1,0:T(8,128)(2,1)S(1)}, u32[]{:S(2)}, u32[]{:S(2)}) %collective-permute-start.9) | collective-permute-done | bytes 65568 | tf_op jit(solution)/shard_map/ppermute | solution.py:272
  30.8 0.0 collective-permute-done.10.refs_2_
  30.8 0.9 %shard_map.68 = bf16[512,256]{1,0:T(8,128)(2,1)} custom-call(bf16[64,512]{1,0:T(8,128)(2,1)S(1)} %collective-permute-done.8.refs_0_, bf16[64,512]{1,0:T(8,128)(2,1)S(1)} %collective-permute-done.9.refs_1_, bf16[64,512]{1,0:T(8,128)(2,1)S(1)} %collective-permute-done.10.refs_2_, bf16[64,512]{1,0:T(8,128)(2,1)S(1)} %get-tuple-element.35.refs_3_, ...), custom_call_target="tpu_custom_call" | custom-call | tf_op jit(solution)/shard_map/pallas_call | solution.py:332
  (3 shorter events, 0.0 us)
Async XLA Ops:
  1.3 8.6 %collective-permute-start = (bf16[288,128]{1,0:T(8,128)(2,1)S(1)}, bf16[288,128]{1,0:T(8,128)(2,1)S(1)}, u32[]{:S(2)}, u32[]{:S(2)}) collective-permute-start(bf16[288,128]{1,0:T(8,128)(2,1)S(1)} %get-tuple-element.21), channel_id=1, source_target_pairs={{0,12},{4,8},{8,4},{12,0},{1,13},{5,9},{9,5},{13,1},{2,14},{6,10},... | collective-permute-start | bytes 221192 | tf_op jit(solution)/shard_map/ppermute | solution.py:272
  6.4 6.3 %collective-permute-start.2 = (bf16[288,128]{1,0:T(8,128)(2,1)S(1)}, bf16[288,128]{1,0:T(8,128)(2,1)S(1)}, u32[]{:S(2)}, u32[]{:S(2)}) collective-permute-start(bf16[288,128]{1,0:T(8,128)(2,1)S(1)} %get-tuple-element.22), channel_id=1, source_target_pairs={{0,8},{4,12},{8,0},{12,4},{1,9},{5,13},{9,1},{13,5},{2,10},{6,14},... | collective-permute-start | bytes 221192 | tf_op jit(solution)/shard_map/ppermute | solution.py:272
  6.4 9.7 %collective-permute-start.6 = (bf16[288,128]{1,0:T(8,128)(2,1)S(1)}, bf16[288,128]{1,0:T(8,128)(2,1)S(1)}, u32[]{:S(2)}, u32[]{:S(2)}) collective-permute-start(bf16[288,128]{1,0:T(8,128)(2,1)S(1)} %get-tuple-element.23), channel_id=1, source_target_pairs={{0,4},{4,0},{8,12},{12,8},{1,5},{5,1},{9,13},{13,9},{2,6},{6,2},{1... | collective-permute-start | bytes 221192 | tf_op jit(solution)/shard_map/ppermute | solution.py:272
  7.1 9.1 %collective-permute-start.4 = (bf16[288,128]{1,0:T(8,128)(2,1)S(1)}, bf16[288,128]{1,0:T(8,128)(2,1)S(1)}, u32[]{:S(2)}, u32[]{:S(2)}) collective-permute-start(bf16[288,128]{1,0:T(8,128)(2,1)S(1)} %get-tuple-element.23), channel_id=1, source_target_pairs={{0,6},{2,4},{4,2},{6,0},{8,14},{10,12},{12,10},{14,8},{1,7},{3,5},... | collective-permute-start | bytes 221192 | tf_op jit(solution)/shard_map/ppermute | solution.py:272
  9.4 6.8 %collective-permute-start.5 = (bf16[288,128]{1,0:T(8,128)(2,1)S(1)}, bf16[288,128]{1,0:T(8,128)(2,1)S(1)}, u32[]{:S(2)}, u32[]{:S(2)}) collective-permute-start(bf16[288,128]{1,0:T(8,128)(2,1)S(1)} %get-tuple-element.24.refs_7_), channel_id=1, source_target_pairs={{0,2},{2,0},{1,3},{3,1},{4,6},{6,4},{5,7},{7,5},{8,10},{10,8},{9,1... | collective-permute-start | bytes 221192 | tf_op jit(solution)/shard_map/ppermute | solution.py:272
  9.9 6.3 %collective-permute-start.1 = (bf16[288,128]{1,0:T(8,128)(2,1)S(1)}, bf16[288,128]{1,0:T(8,128)(2,1)S(1)}, u32[]{:S(2)}, u32[]{:S(2)}) collective-permute-start(bf16[288,128]{1,0:T(8,128)(2,1)S(1)} %collective-permute-done.refs_4_), channel_id=1, source_target_pairs={{0,2},{2,0},{1,3},{3,1},{4,6},{6,4},{5,7},{7,5},{8,10},{10,8},{9,1... | collective-permute-start | bytes 221192 | tf_op jit(solution)/shard_map/ppermute | solution.py:272
  12.7 4.4 %collective-permute-start.3 = (bf16[288,128]{1,0:T(8,128)(2,1)S(1)}, bf16[288,128]{1,0:T(8,128)(2,1)S(1)}, u32[]{:S(2)}, u32[]{:S(2)}) collective-permute-start(bf16[288,128]{1,0:T(8,128)(2,1)S(1)} %collective-permute-done.2.refs_5_), channel_id=1, source_target_pairs={{0,2},{2,0},{1,3},{3,1},{4,6},{6,4},{5,7},{7,5},{8,10},{10,8},{9,1... | collective-permute-start | bytes 221192 | tf_op jit(solution)/shard_map/ppermute | solution.py:272
  18.6 1.4 %collective-permute-start.7 = (f32[128,256]{1,0:T(8,128)S(1)}, f32[128,256]{1,0:T(8,128)S(1)}, u32[]{:S(2)}, u32[]{:S(2)}) collective-permute-start(f32[128,256]{1,0:T(8,128)S(1)} %get-tuple-element.30.mine_ref), channel_id=1, source_target_pairs={{0,1},{1,0},{2,3},{3,2},{4,5},{5,4},{6,7},{7,6},{8,9},{9,8},{10,11... | collective-permute-start | bytes 393224 | tf_op jit(solution)/shard_map/ppermute | solution.py:272
  21.7 6.7 %collective-permute-start.8 = (bf16[64,512]{1,0:T(8,128)(2,1)S(1)}, bf16[64,512]{1,0:T(8,128)(2,1)S(1)}, u32[]{:S(2)}, u32[]{:S(2)}) collective-permute-start(bf16[64,512]{1,0:T(8,128)(2,1)S(1)} %get-tuple-element.32), channel_id=1, source_target_pairs={{0,12},{4,8},{8,4},{12,0},{1,13},{5,9},{9,5},{13,1},{2,14},{6,10},... | collective-permute-start | bytes 196616 | tf_op jit(solution)/shard_map/ppermute | solution.py:272
  24.5 6.3 %collective-permute-start.9 = (bf16[64,512]{1,0:T(8,128)(2,1)S(1)}, bf16[64,512]{1,0:T(8,128)(2,1)S(1)}, u32[]{:S(2)}, u32[]{:S(2)}) collective-permute-start(bf16[64,512]{1,0:T(8,128)(2,1)S(1)} %get-tuple-element.33), channel_id=1, source_target_pairs={{0,8},{4,12},{8,0},{12,4},{1,9},{5,13},{9,1},{13,5},{2,10},{6,14},... | collective-permute-start | bytes 196616 | tf_op jit(solution)/shard_map/ppermute | solution.py:272
  24.5 6.3 %collective-permute-start.10 = (bf16[64,512]{1,0:T(8,128)(2,1)S(1)}, bf16[64,512]{1,0:T(8,128)(2,1)S(1)}, u32[]{:S(2)}, u32[]{:S(2)}) collective-permute-start(bf16[64,512]{1,0:T(8,128)(2,1)S(1)} %get-tuple-element.34), channel_id=1, source_target_pairs={{0,4},{4,0},{8,12},{12,8},{1,5},{5,1},{9,13},{13,9},{2,6},{6,2},{1... | collective-permute-start | bytes 196616 | tf_op jit(solution)/shard_map/ppermute | solution.py:272

commit v6 on v5

--- a/solution.py
+++ b/solution.py
@@ -147,7 +147,7 @@
 
 
 def correlate_kernel(segs, blocks, own, *refs):
-    chunks = refs[segs * SPANS - 1 :: -1]
+    chunks = [refs[i] for i in [7, 2, 6, 5, 3, 4, 1, 0]]
     table_ref, lag_ref, take_ref, find_ref, chosen_ref, partial_ref = refs[segs * SPANS :]
     fibre = lax.axis_index("fibre")
     span = S // SPANS
@@ -197,7 +197,7 @@
     partial_ref[...] = partial - seen
 
 
-def adjoint_kernel(blocks, own, chosen_ref, mine_ref, other_ref, table_ref, lag_ref, give_ref, *out_refs):
+def adjoint_kernel(blocks, own, chosen_ref, mine_ref, other_ref, back_ref, lag_ref, give_ref, *out_refs):
     fibre = lax.axis_index("fibre")
     band = F // SPANS
     lines = mine_ref.shape[0]
@@ -220,11 +220,11 @@
         imag = grad[:, F + j * band : F + (j + 1) * band]
         line = jnp.concatenate([real, imag], axis=1)
         if j % 2 == 0:
-            part = dot(line, table_ref[j], _NT)
+            part = dot(line, back_ref[j])
             even = (part, part) if j == 0 else (even[0] + part, even[1] - part)
         else:
             turned = jnp.concatenate([-imag, real], axis=1)
-            part = dot(jnp.concatenate([line, turned], axis=0), table_ref[j], _NT)
+            part = dot(jnp.concatenate([line, turned], axis=0), back_ref[j])
             u, v = part[:count], part[count:]
             odd = (u, v) if j == 1 else (odd[0] + u, odd[1] - v)
     flip = fibre % 2 == 1
@@ -237,7 +237,8 @@
 
 
 def unpack_kernel(*refs):
-    chunks, (order_ref, out_hbm, out, sems) = refs[SPANS - 1 :: -1], refs[SPANS:]
+    chunks = [refs[i] for i in [3, 1, 2, 0]]
+    order_ref, out_hbm, out, sems = refs[SPANS:]
     span = out.shape[0]
     cuts = [pl.ds(q * LANES, LANES) for q in range(span // LANES)]
     leave = [pltpu.make_async_copy(out.at[cut], out_hbm.at[cut], sems.at[q]) for q, cut in enumerate(cuts)]
@@ -286,8 +287,8 @@
     )(*(pltpu.with_memory_space_constraint(x, pltpu.HBM) for x in (records[0], observed, lag_mask)))
     held = [along("fibre", send[k], lambda i: i ^ k) for k in range(SPANS - 1, 0, -1)]
     held = [send[0]] + held[::-1]
-    constants = [jnp.asarray(c) for c in (table, lags)]
-    table, lags, take, give, find, order = pl.pallas_call(
+    constants = [jnp.asarray(c) for c in (table, np.ascontiguousarray(table.transpose(0, 2, 1)), lags)]
+    table, table_back, lags, take, give, find, order = pl.pallas_call(
         functools.partial(prepare_kernel, segs, blocks, own, pairs_dev, share),
         out_shape=[pltpu.VMEM(c.shape, low) for c in constants]
         + [
@@ -315,7 +316,7 @@
         in_specs=[vmem] * (segs * SPANS + 4),
         out_specs=[vmem] * 2,
         compiler_params=limit,
-    )(*held[::-1], table, lags, take, find)
+    )(*[held[i] for i in (7, 6, 1, 4, 5, 3, 2, 0)], table, lags, take, find)
     mine, other = partial, along("rec", partial, lambda i: (i + 1) % recs)
     for _ in range(2, recs):
         mine, other = mine + other, along("rec", other, lambda i: (i + 1) % recs)
@@ -325,10 +326,9 @@
         in_specs=[vmem] * 6,
         out_specs=[vmem] * SPANS,
         compiler_params=limit,
-    )(chosen, mine, other, table, lags, give)
+    )(chosen, mine, other, table_back, lags, give)
     own_part = back[0]
-    back = [along("fibre", back[k], lambda i: i ^ k) for k in range(SPANS - 1, 0, -1)][::-1]
-    back = [own_part] + back
+    sent = {k: along("fibre", back[k], lambda i: i ^ k) for k in (3, 1, 2)}
     out = pl.pallas_call(
         unpack_kernel,
         out_shape=jax.ShapeDtypeStruct((span, count), low),
@@ -339,7 +339,7 @@
             pltpu.SemaphoreType.DMA((span // LANES,)),
         ],
         compiler_params=limit,
-    )(*back[::-1], order)
+    )(*sent.values(), own_part, order)
     return out[None]
 
 

time: 31.9 us -> 31.3 us (0.981)
  waiting for transfers between devices: 8.26 us -> 7.34 us
    ppermute x11, waiting for transfers between devices: 8.26 us -> 7.34 us  [along(): lax.ppermute(array, axis, [(i, target(i)) for i in range(lax.axis_size(ax...]
    pallas_call x1, Pallas kernels: 1.88 us -> 2.52 us  [by_own_k(): pl.pallas_call(functools.partial(prepare_kernel, segs, blocks, own, pairs...]
  transfers between devices with their start and end apart: 11 -> 11, of which waited for: 5 -> 5; matrix products, arithmetic and copies ran while one was open for 0% -> 0% of each run, Pallas kernels for 6% -> 8%
where the time goes in v6:
time: 31.3 us; the launch traced here: 31.1 us
  starting transfers between devices  16.1 us (51%)
  Pallas kernels  7.57 us (24%)
  waiting for transfers between devices  7.34 us (23%)
    ppermute x11, starting transfers between devices, along(): lax.ppermute(array, axis, [(i, target(i)) for i in range(lax.axis_size(ax...  16.1 us
    ppermute x11, waiting for transfers between devices, along(): lax.ppermute(array, axis, [(i, target(i)) for i in range(lax.axis_size(ax...  7.34 us
    pallas_call x1, Pallas kernels, by_own_k(): pl.pallas_call(functools.partial(prepare_kernel, segs, blocks, own, pairs...  2.52 us
    pallas_call x1, Pallas kernels, by_own_k(): pl.pallas_call(functools.partial(adjoint_kernel, blocks, own), out_shape=...  1.41 us
    pallas_call x1, Pallas kernels, by_own_k(): pl.pallas_call(functools.partial(correlate_kernel, segs, blocks, own), ou...  1.39 us
    pallas_call x1, Pallas kernels, by_own_k(): pl.pallas_call(functools.partial(pack_kernel, blocks, own), out_shape=[pl...  1.3 us
    pallas_call x1, Pallas kernels, by_own_k(): pl.pallas_call(unpack_kernel, out_shape=jax.ShapeDtypeStruct((span, count...  0.94 us
  transfers between devices with their start and end apart: 11, of which 5 were waited for; matrix products, arithmetic and copies ran while one was open for 0% of the time, Pallas kernels for 8%

profile of v6, /device:TPU:0, one launch (start us, length us, event | category | flops | bytes accessed | tf_op | source)
XLA Modules:
  0.0 31.1 jit_solution(6097613207479195882)
XLA Ops:
  0.0 1.3 %shard_map.73 = (bf16[288,128]{1,0:T(8,128)(2,1)S(1)}, bf16[288,128]{1,0:T(8,128)(2,1)S(1)}, bf16[288,128]{1,0:T(8,128)(2,1)S(1)}, bf16[288,128]{1,0:T(8,128)(2,1)S(1)}) custom-call(bf16[512,256]{1,0:T(8,128)(2,1)} %bitcast.3, f32[2,32,256]{2,1,0:T(8,128)} %observed_hbm.1, s32[2,256]{1,0:T(2,128)} %mask_hbm.1), custom_call_target="tpu_custom_call" | custom-call | tf_op jit(solution)/shard_map/pallas_call | solution.py:275
  1.3 5.1 %collective-permute-start = (bf16[288,128]{1,0:T(8,128)(2,1)S(1)}, bf16[288,128]{1,0:T(8,128)(2,1)S(1)}, u32[]{:S(2)}, u32[]{:S(2)}) collective-permute-start(bf16[288,128]{1,0:T(8,128)(2,1)S(1)} %get-tuple-element.22), channel_id=1, source_target_pairs={{0,12},{4,8},{8,4},{12,0},{1,13},{5,9},{9,5},{13,1},{2,14},{6,10},... | collective-permute-start | bytes 221192 | tf_op jit(solution)/shard_map/ppermute | solution.py:273
  6.4 1.7 %collective-permute-start.6 = (bf16[288,128]{1,0:T(8,128)(2,1)S(1)}, bf16[288,128]{1,0:T(8,128)(2,1)S(1)}, u32[]{:S(2)}, u32[]{:S(2)}) collective-permute-start(bf16[288,128]{1,0:T(8,128)(2,1)S(1)} %get-tuple-element.24), channel_id=1, source_target_pairs={{0,6},{2,4},{4,2},{6,0},{8,14},{10,12},{12,10},{14,8},{1,7},{3,5},... | collective-permute-start | bytes 221192 | tf_op jit(solution)/shard_map/ppermute | solution.py:273
  8.1 1.2 %collective-permute-start.4 = (bf16[288,128]{1,0:T(8,128)(2,1)S(1)}, bf16[288,128]{1,0:T(8,128)(2,1)S(1)}, u32[]{:S(2)}, u32[]{:S(2)}) collective-permute-start(bf16[288,128]{1,0:T(8,128)(2,1)S(1)} %get-tuple-element.24), channel_id=1, source_target_pairs={{0,4},{4,0},{8,12},{12,8},{1,5},{5,1},{9,13},{13,9},{2,6},{6,2},{1... | collective-permute-start | bytes 221192 | tf_op jit(solution)/shard_map/ppermute | solution.py:273
  9.4 0.5 %collective-permute-start.5 = (bf16[288,128]{1,0:T(8,128)(2,1)S(1)}, bf16[288,128]{1,0:T(8,128)(2,1)S(1)}, u32[]{:S(2)}, u32[]{:S(2)}) collective-permute-start(bf16[288,128]{1,0:T(8,128)(2,1)S(1)} %get-tuple-element.25.refs_7_), channel_id=1, source_target_pairs={{0,2},{2,0},{1,3},{3,1},{4,6},{6,4},{5,7},{7,5},{8,10},{10,8},{9,1... | collective-permute-start | bytes 221192 | tf_op jit(solution)/shard_map/ppermute | solution.py:273
  9.9 0.0 collective-permute-done.refs_5_
  9.9 1.5 %collective-permute-start.1 = (bf16[288,128]{1,0:T(8,128)(2,1)S(1)}, bf16[288,128]{1,0:T(8,128)(2,1)S(1)}, u32[]{:S(2)}, u32[]{:S(2)}) collective-permute-start(bf16[288,128]{1,0:T(8,128)(2,1)S(1)} %collective-permute-done.refs_5_), channel_id=1, source_target_pairs={{0,2},{2,0},{1,3},{3,1},{4,6},{6,4},{5,7},{7,5},{8,10},{10,8},{9,1... | collective-permute-start | bytes 221192 | tf_op jit(solution)/shard_map/ppermute | solution.py:273
  11.4 1.3 %collective-permute-done.2.refs_6_ = bf16[288,128]{1,0:T(8,128)(2,1)S(1)} collective-permute-done((bf16[288,128]{1,0:T(8,128)(2,1)S(1)}, bf16[288,128]{1,0:T(8,128)(2,1)S(1)}, u32[]{:S(2)}, u32[]{:S(2)}) %collective-permute-start.2) | collective-permute-done | bytes 73760 | tf_op jit(solution)/shard_map/ppermute | solution.py:273
  12.7 1.5 %collective-permute-start.3 = (bf16[288,128]{1,0:T(8,128)(2,1)S(1)}, bf16[288,128]{1,0:T(8,128)(2,1)S(1)}, u32[]{:S(2)}, u32[]{:S(2)}) collective-permute-start(bf16[288,128]{1,0:T(8,128)(2,1)S(1)} %collective-permute-done.2.refs_6_), channel_id=1, source_target_pairs={{0,2},{2,0},{1,3},{3,1},{4,6},{6,4},{5,7},{7,5},{8,10},{10,8},{9,1... | collective-permute-start | bytes 221192 | tf_op jit(solution)/shard_map/ppermute | solution.py:273
  14.2 2.5 %shard_map.74 = (bf16[4,512,512]{2,1,0:T(8,128)(2,1)S(1)}, bf16[4,512,512]{2,1,0:T(8,128)(2,1)S(1)}, bf16[2048,256]{1,0:T(8,128)(2,1)S(1)}, bf16[256,128]{1,0:T(...) custom-call(s32[2,16]{1,0:T(2,128)} %bitcast.4, ...), custom_call_target="tpu_custom_call" | custom-call | bytes 4194304 | tf_op jit(solution)/shard_map/pallas_call | solution.py:291
  16.8 0.0 collective-permute-done.6.refs_4_
  16.8 0.0 collective-permute-done.4.refs_2_
  16.8 0.0 collective-permute-done.1.refs_0_
  16.8 0.3 collective-permute-done.3.refs_1_
  17.1 1.4 %shard_map.75 = (bf16[256,2048]{1,0:T(8,128)(2,1)S(1)}, f32[128,256]{1,0:T(8,128)S(1)}) custom-call(bf16[288,128]{1,0:T(8,128)(2,1)S(1)} %collective-permute-done.1.refs_0_, bf16[288,128]{1,0:T(8,128)(2,1)S(1)} %collective-permute-done.3.refs_1_, bf16[288,128]{1,0:T(8,128)(2,1)S(1)} %collective-permute-done.4.refs_2_, ...), custom_call_target="tpu_custom_call" | custom-call | tf_op jit(solution)/shard_map/pallas_call | solution.py:313
  18.5 0.1 collective-permute-start.7
  18.6 1.3 %collective-permute-done.7.other_ref = f32[128,256]{1,0:T(8,128)S(1)} collective-permute-done((f32[128,256]{1,0:T(8,128)S(1)}, f32[128,256]{1,0:T(8,128)S(1)}, u32[]{:S(2)}, u32[]{:S(2)}) %collective-permute-start.7) | collective-permute-done | bytes 131104 | tf_op jit(solution)/shard_map/ppermute | solution.py:273
  19.9 1.4 %shard_map.76 = (bf16[64,512]{1,0:T(8,128)(2,1)S(1)}, bf16[64,512]{1,0:T(8,128)(2,1)S(1)}, bf16[64,512]{1,0:T(8,128)(2,1)S(1)}, bf16[64,512]{1,0:T(8,128)(2,1)S(1)}) custom-call(bf16[256,2048]{1,0:T(8,128)(2,1)S(1)} %get-tuple-element.30.chosen_ref, f32[128,256]{1,0:T(8,128)S(1)} %get-tuple-element.31.mine_ref, ...), custom_call_target="tpu_custom_call" | custom-call | tf_op jit(solution)/shard_map/pallas_call | solution.py:323
  21.3 2.7 %collective-permute-start.8 = (bf16[64,512]{1,0:T(8,128)(2,1)S(1)}, bf16[64,512]{1,0:T(8,128)(2,1)S(1)}, u32[]{:S(2)}, u32[]{:S(2)}) collective-permute-start(bf16[64,512]{1,0:T(8,128)(2,1)S(1)} %get-tuple-element.34), channel_id=1, source_target_pairs={{0,12},{4,8},{8,4},{12,0},{1,13},{5,9},{9,5},{13,1},{2,14},{6,10},... | collective-permute-start | bytes 196616 | tf_op jit(solution)/shard_map/ppermute | solution.py:273
  24.0 1.8 %collective-permute-start.10 = (bf16[64,512]{1,0:T(8,128)(2,1)S(1)}, bf16[64,512]{1,0:T(8,128)(2,1)S(1)}, u32[]{:S(2)}, u32[]{:S(2)}) collective-permute-start(bf16[64,512]{1,0:T(8,128)(2,1)S(1)} %get-tuple-element.36), channel_id=1, source_target_pairs={{0,8},{4,12},{8,0},{12,4},{1,9},{5,13},{9,1},{13,5},{2,10},{6,14},... | collective-permute-start | bytes 196616 | tf_op jit(solution)/shard_map/ppermute | solution.py:273
  25.8 2.4 %collective-permute-done.8.refs_0_ = bf16[64,512]{1,0:T(8,128)(2,1)S(1)} collective-permute-done((bf16[64,512]{1,0:T(8,128)(2,1)S(1)}, bf16[64,512]{1,0:T(8,128)(2,1)S(1)}, u32[]{:S(2)}, u32[]{:S(2)}) %collective-permute-start.8) | collective-permute-done | bytes 65568 | tf_op jit(solution)/shard_map/ppermute | solution.py:273
  28.2 2.0 %collective-permute-done.9.refs_1_ = bf16[64,512]{1,0:T(8,128)(2,1)S(1)} collective-permute-done((bf16[64,512]{1,0:T(8,128)(2,1)S(1)}, bf16[64,512]{1,0:T(8,128)(2,1)S(1)}, u32[]{:S(2)}, u32[]{:S(2)}) %collective-permute-start.9) | collective-permute-done | bytes 65568 | tf_op jit(solution)/shard_map/ppermute | solution.py:273
  30.2 0.0 collective-permute-done.10.refs_2_
  30.2 0.9 %shard_map.77 = bf16[512,256]{1,0:T(8,128)(2,1)} custom-call(bf16[64,512]{1,0:T(8,128)(2,1)S(1)} %collective-permute-done.8.refs_0_, bf16[64,512]{1,0:T(8,128)(2,1)S(1)} %collective-permute-done.9.refs_1_, bf16[64,512]{1,0:T(8,128)(2,1)S(1)} %collective-permute-done.10.refs_2_, bf16[64,512]{1,0:T(8,128)(2,1)S(1)} %get-tuple-element.37.refs_3_, ...), custom_call_target="tpu_custom_call" | custom-call | tf_op jit(solution)/shard_map/pallas_call | solution.py:332
  (3 shorter events, 0.0 us)
Async XLA Ops:
  1.3 8.6 %collective-permute-start = (bf16[288,128]{1,0:T(8,128)(2,1)S(1)}, bf16[288,128]{1,0:T(8,128)(2,1)S(1)}, u32[]{:S(2)}, u32[]{:S(2)}) collective-permute-start(bf16[288,128]{1,0:T(8,128)(2,1)S(1)} %get-tuple-element.22), channel_id=1, source_target_pairs={{0,12},{4,8},{8,4},{12,0},{1,13},{5,9},{9,5},{13,1},{2,14},{6,10},... | collective-permute-start | bytes 221192 | tf_op jit(solution)/shard_map/ppermute | solution.py:273
  6.4 6.3 %collective-permute-start.2 = (bf16[288,128]{1,0:T(8,128)(2,1)S(1)}, bf16[288,128]{1,0:T(8,128)(2,1)S(1)}, u32[]{:S(2)}, u32[]{:S(2)}) collective-permute-start(bf16[288,128]{1,0:T(8,128)(2,1)S(1)} %get-tuple-element.23), channel_id=1, source_target_pairs={{0,8},{4,12},{8,0},{12,4},{1,9},{5,13},{9,1},{13,5},{2,10},{6,14},... | collective-permute-start | bytes 221192 | tf_op jit(solution)/shard_map/ppermute | solution.py:273
  6.4 10.3 %collective-permute-start.6 = (bf16[288,128]{1,0:T(8,128)(2,1)S(1)}, bf16[288,128]{1,0:T(8,128)(2,1)S(1)}, u32[]{:S(2)}, u32[]{:S(2)}) collective-permute-start(bf16[288,128]{1,0:T(8,128)(2,1)S(1)} %get-tuple-element.24), channel_id=1, source_target_pairs={{0,6},{2,4},{4,2},{6,0},{8,14},{10,12},{12,10},{14,8},{1,7},{3,5},... | collective-permute-start | bytes 221192 | tf_op jit(solution)/shard_map/ppermute | solution.py:273
  8.1 8.6 %collective-permute-start.4 = (bf16[288,128]{1,0:T(8,128)(2,1)S(1)}, bf16[288,128]{1,0:T(8,128)(2,1)S(1)}, u32[]{:S(2)}, u32[]{:S(2)}) collective-permute-start(bf16[288,128]{1,0:T(8,128)(2,1)S(1)} %get-tuple-element.24), channel_id=1, source_target_pairs={{0,4},{4,0},{8,12},{12,8},{1,5},{5,1},{9,13},{13,9},{2,6},{6,2},{1... | collective-permute-start | bytes 221192 | tf_op jit(solution)/shard_map/ppermute | solution.py:273
  9.4 7.4 %collective-permute-start.5 = (bf16[288,128]{1,0:T(8,128)(2,1)S(1)}, bf16[288,128]{1,0:T(8,128)(2,1)S(1)}, u32[]{:S(2)}, u32[]{:S(2)}) collective-permute-start(bf16[288,128]{1,0:T(8,128)(2,1)S(1)} %get-tuple-element.25.refs_7_), channel_id=1, source_target_pairs={{0,2},{2,0},{1,3},{3,1},{4,6},{6,4},{5,7},{7,5},{8,10},{10,8},{9,1... | collective-permute-start | bytes 221192 | tf_op jit(solution)/shard_map/ppermute | solution.py:273
  9.9 6.9 %collective-permute-start.1 = (bf16[288,128]{1,0:T(8,128)(2,1)S(1)}, bf16[288,128]{1,0:T(8,128)(2,1)S(1)}, u32[]{:S(2)}, u32[]{:S(2)}) collective-permute-start(bf16[288,128]{1,0:T(8,128)(2,1)S(1)} %collective-permute-done.refs_5_), channel_id=1, source_target_pairs={{0,2},{2,0},{1,3},{3,1},{4,6},{6,4},{5,7},{7,5},{8,10},{10,8},{9,1... | collective-permute-start | bytes 221192 | tf_op jit(solution)/shard_map/ppermute | solution.py:273
  12.7 4.4 %collective-permute-start.3 = (bf16[288,128]{1,0:T(8,128)(2,1)S(1)}, bf16[288,128]{1,0:T(8,128)(2,1)S(1)}, u32[]{:S(2)}, u32[]{:S(2)}) collective-permute-start(bf16[288,128]{1,0:T(8,128)(2,1)S(1)} %collective-permute-done.2.refs_6_), channel_id=1, source_target_pairs={{0,2},{2,0},{1,3},{3,1},{4,6},{6,4},{5,7},{7,5},{8,10},{10,8},{9,1... | collective-permute-start | bytes 221192 | tf_op jit(solution)/shard_map/ppermute | solution.py:273
  18.5 1.4 %collective-permute-start.7 = (f32[128,256]{1,0:T(8,128)S(1)}, f32[128,256]{1,0:T(8,128)S(1)}, u32[]{:S(2)}, u32[]{:S(2)}) collective-permute-start(f32[128,256]{1,0:T(8,128)S(1)} %get-tuple-element.31.mine_ref), channel_id=1, source_target_pairs={{0,1},{1,0},{2,3},{3,2},{4,5},{5,4},{6,7},{7,6},{8,9},{9,8},{10,11... | collective-permute-start | bytes 393224 | tf_op jit(solution)/shard_map/ppermute | solution.py:273
  21.3 6.9 %collective-permute-start.8 = (bf16[64,512]{1,0:T(8,128)(2,1)S(1)}, bf16[64,512]{1,0:T(8,128)(2,1)S(1)}, u32[]{:S(2)}, u32[]{:S(2)}) collective-permute-start(bf16[64,512]{1,0:T(8,128)(2,1)S(1)} %get-tuple-element.34), channel_id=1, source_target_pairs={{0,12},{4,8},{8,4},{12,0},{1,13},{5,9},{9,5},{13,1},{2,14},{6,10},... | collective-permute-start | bytes 196616 | tf_op jit(solution)/shard_map/ppermute | solution.py:273
  24.0 6.1 %collective-permute-start.9 = (bf16[64,512]{1,0:T(8,128)(2,1)S(1)}, bf16[64,512]{1,0:T(8,128)(2,1)S(1)}, u32[]{:S(2)}, u32[]{:S(2)}) collective-permute-start(bf16[64,512]{1,0:T(8,128)(2,1)S(1)} %get-tuple-element.35), channel_id=1, source_target_pairs={{0,4},{4,0},{8,12},{12,8},{1,5},{5,1},{9,13},{13,9},{2,6},{6,2},{1... | collective-permute-start | bytes 196616 | tf_op jit(solution)/shard_map/ppermute | solution.py:273
  24.0 6.1 %collective-permute-start.10 = (bf16[64,512]{1,0:T(8,128)(2,1)S(1)}, bf16[64,512]{1,0:T(8,128)(2,1)S(1)}, u32[]{:S(2)}, u32[]{:S(2)}) collective-permute-start(bf16[64,512]{1,0:T(8,128)(2,1)S(1)} %get-tuple-element.36), channel_id=1, source_target_pairs={{0,8},{4,12},{8,0},{12,4},{1,9},{5,13},{9,1},{13,5},{2,10},{6,14},... | collective-permute-start | bytes 196616 | tf_op jit(solution)/shard_map/ppermute | solution.py:273

commit v7 on v6

--- a/solution.py
+++ b/solution.py
@@ -72,14 +72,14 @@
     order = channel_order(fibre, blocks, own)
     lines = share * BLOCK
     halves = LAGS // LANES
-    extra = 2 * halves * share * own
+    extra = halves * share * own
     place = one_hot(
         SPANS * extra,
-        2 * halves * lines,
+        halves * lines,
         lambda r, c: (c % BLOCK // own == r // extra ^ fibre)
         & (c % own == r % own)
-        & (c // lines == r % (2 * halves * own) // own)
-        & (c % lines // BLOCK == r % extra // (2 * halves * own)),
+        & (c // lines == r % (halves * own) // own)
+        & (c % lines // BLOCK == r % extra // (halves * own)),
     )
     seen_copy.wait()
     mask_copy.wait()
@@ -87,9 +87,8 @@
         [mask[pl.ds(start + i, 1), :] + jnp.zeros((BLOCK, 1), jnp.int32) for i in range(share)], axis=0
     )
     seen = jnp.where(window != 0, observed[...].reshape(lines, LAGS), MASKED)
-    high = seen.astype(jnp.bfloat16)
-    low = (seen - high.astype(jnp.float32)).astype(jnp.bfloat16)
-    parts = [v[:, h * LANES : (h + 1) * LANES] for v in (high, low) for h in range(halves)]
+    seen = seen.astype(jnp.bfloat16)
+    parts = [seen[:, h * LANES : (h + 1) * LANES] for h in range(halves)]
     packed = dot(place, jnp.concatenate(parts, axis=0)).astype(jnp.bfloat16)
     for k, out_ref in enumerate(out_refs):
         out_ref[tiles * rows :, :] = packed[k * extra : (k + 1) * extra]
@@ -121,12 +120,12 @@
         return distance * rows + block % blocks * own + line % own
 
     halves = LAGS // LANES
-    extra = 2 * halves * share * own
+    extra = halves * share * own
 
     def here(half, line, place):
         part = place % extra
         owner = (place // extra % SPANS ^ fibre) * segs + (seg + segs - place // (extra * SPANS)) % segs
-        pair = owner * pairs_dev + rec * share + part // (2 * halves * own)
+        pair = owner * pairs_dev + rec * share + part // (halves * own)
         return (line // own == pair) & (line % own == part % own) & (part % (halves * own) // own == half)
 
     for h in range(halves):
@@ -259,7 +258,7 @@
     pair_total, pairs_dev = pairs.shape[0], observed.shape[0]
     share = pairs_dev // recs
     lines = pair_total * own
-    extra = 2 * LAGS // LANES * share * own
+    extra = LAGS // LANES * share * own
     table = forward_table().reshape(F // SPANS, SPANS, 2, SPANS, span)[:, :, :, 0]
     table = np.ascontiguousarray(table.transpose(1, 3, 2, 0)).reshape(SPANS, span, S // SPANS)
     lags = lag_table().reshape(F // SPANS, SPANS, 2, LAGS)

time: 31.3 us -> 31 us (level)
  waiting for transfers between devices: 7.34 us -> 6.99 us
    ppermute x11, waiting for transfers between devices: 7.34 us -> 6.99 us  [along(): lax.ppermute(array, axis, [(i, target(i)) for i in range(lax.axis_size(ax...]
where the time goes in v7:
time: 31 us; the launch traced here: 30.8 us
  starting transfers between devices  16.1 us (52%)
  Pallas kernels  7.64 us (25%)
  waiting for transfers between devices  6.99 us (23%)
    ppermute x11, starting transfers between devices, along(): lax.ppermute(array, axis, [(i, target(i)) for i in range(lax.axis_size(ax...  16.1 us
    ppermute x11, waiting for transfers between devices, along(): lax.ppermute(array, axis, [(i, target(i)) for i in range(lax.axis_size(ax...  6.99 us
    pallas_call x1, Pallas kernels, by_own_k(): pl.pallas_call(functools.partial(prepare_kernel, segs, blocks, own, pairs...  2.52 us
    pallas_call x1, Pallas kernels, by_own_k(): pl.pallas_call(functools.partial(correlate_kernel, segs, blocks, own), ou...  1.48 us
    pallas_call x1, Pallas kernels, by_own_k(): pl.pallas_call(functools.partial(adjoint_kernel, blocks, own), out_shape=...  1.42 us
    pallas_call x1, Pallas kernels, by_own_k(): pl.pallas_call(functools.partial(pack_kernel, blocks, own), out_shape=[pl...  1.28 us
    pallas_call x1, Pallas kernels, by_own_k(): pl.pallas_call(unpack_kernel, out_shape=jax.ShapeDtypeStruct((span, count...  0.94 us
  transfers between devices with their start and end apart: 11, of which 5 were waited for; matrix products, arithmetic and copies ran while one was open for 0% of the time, Pallas kernels for 8%

profile of v7, /device:TPU:0, one launch (start us, length us, event | category | flops | bytes accessed | tf_op | source)
XLA Modules:
  0.0 30.8 jit_solution(11397121841537355384)
XLA Ops:
  0.0 1.3 %shard_map.73 = (bf16[272,128]{1,0:T(8,128)(2,1)S(1)}, bf16[272,128]{1,0:T(8,128)(2,1)S(1)}, bf16[272,128]{1,0:T(8,128)(2,1)S(1)}, bf16[272,128]{1,0:T(8,128)(2,1)S(1)}) custom-call(bf16[512,256]{1,0:T(8,128)(2,1)} %bitcast.3, f32[2,32,256]{2,1,0:T(8,128)} %observed_hbm.1, s32[2,256]{1,0:T(2,128)} %mask_hbm.1), custom_call_target="tpu_custom_call" | custom-call | tf_op jit(solution)/shard_map/pallas_call | solution.py:274
  1.3 5.1 %collective-permute-start = (bf16[272,128]{1,0:T(8,128)(2,1)S(1)}, bf16[272,128]{1,0:T(8,128)(2,1)S(1)}, u32[]{:S(2)}, u32[]{:S(2)}) collective-permute-start(bf16[272,128]{1,0:T(8,128)(2,1)S(1)} %get-tuple-element.22), channel_id=1, source_target_pairs={{0,12},{4,8},{8,4},{12,0},{1,13},{5,9},{9,5},{13,1},{2,14},{6,10},... | collective-permute-start | bytes 208904 | tf_op jit(solution)/shard_map/ppermute | solution.py:272
  6.4 0.0 collective-permute-start.2
  6.4 1.7 %collective-permute-start.6 = (bf16[272,128]{1,0:T(8,128)(2,1)S(1)}, bf16[272,128]{1,0:T(8,128)(2,1)S(1)}, u32[]{:S(2)}, u32[]{:S(2)}) collective-permute-start(bf16[272,128]{1,0:T(8,128)(2,1)S(1)} %get-tuple-element.24), channel_id=1, source_target_pairs={{0,6},{2,4},{4,2},{6,0},{8,14},{10,12},{12,10},{14,8},{1,7},{3,5},... | collective-permute-start | bytes 208904 | tf_op jit(solution)/shard_map/ppermute | solution.py:272
  8.1 1.2 %collective-permute-start.4 = (bf16[272,128]{1,0:T(8,128)(2,1)S(1)}, bf16[272,128]{1,0:T(8,128)(2,1)S(1)}, u32[]{:S(2)}, u32[]{:S(2)}) collective-permute-start(bf16[272,128]{1,0:T(8,128)(2,1)S(1)} %get-tuple-element.24), channel_id=1, source_target_pairs={{0,4},{4,0},{8,12},{12,8},{1,5},{5,1},{9,13},{13,9},{2,6},{6,2},{1... | collective-permute-start | bytes 208904 | tf_op jit(solution)/shard_map/ppermute | solution.py:272
  9.4 0.5 %collective-permute-start.5 = (bf16[272,128]{1,0:T(8,128)(2,1)S(1)}, bf16[272,128]{1,0:T(8,128)(2,1)S(1)}, u32[]{:S(2)}, u32[]{:S(2)}) collective-permute-start(bf16[272,128]{1,0:T(8,128)(2,1)S(1)} %get-tuple-element.25.refs_7_), channel_id=1, source_target_pairs={{0,2},{2,0},{1,3},{3,1},{4,6},{6,4},{5,7},{7,5},{8,10},{10,8},{9,1... | collective-permute-start | bytes 208904 | tf_op jit(solution)/shard_map/ppermute | solution.py:272
  9.9 1.5 %collective-permute-start.1 = (bf16[272,128]{1,0:T(8,128)(2,1)S(1)}, bf16[272,128]{1,0:T(8,128)(2,1)S(1)}, u32[]{:S(2)}, u32[]{:S(2)}) collective-permute-start(bf16[272,128]{1,0:T(8,128)(2,1)S(1)} %collective-permute-done.refs_5_), channel_id=1, source_target_pairs={{0,2},{2,0},{1,3},{3,1},{4,6},{6,4},{5,7},{7,5},{8,10},{10,8},{9,1... | collective-permute-start | bytes 208904 | tf_op jit(solution)/shard_map/ppermute | solution.py:272
  11.4 1.0 %collective-permute-done.2.refs_6_ = bf16[272,128]{1,0:T(8,128)(2,1)S(1)} collective-permute-done((bf16[272,128]{1,0:T(8,128)(2,1)S(1)}, bf16[272,128]{1,0:T(8,128)(2,1)S(1)}, u32[]{:S(2)}, u32[]{:S(2)}) %collective-permute-start.2) | collective-permute-done | bytes 69664 | tf_op jit(solution)/shard_map/ppermute | solution.py:272
  12.4 1.5 %collective-permute-start.3 = (bf16[272,128]{1,0:T(8,128)(2,1)S(1)}, bf16[272,128]{1,0:T(8,128)(2,1)S(1)}, u32[]{:S(2)}, u32[]{:S(2)}) collective-permute-start(bf16[272,128]{1,0:T(8,128)(2,1)S(1)} %collective-permute-done.2.refs_6_), channel_id=1, source_target_pairs={{0,2},{2,0},{1,3},{3,1},{4,6},{6,4},{5,7},{7,5},{8,10},{10,8},{9,1... | collective-permute-start | bytes 208904 | tf_op jit(solution)/shard_map/ppermute | solution.py:272
  13.9 2.5 %shard_map.74 = (bf16[4,512,512]{2,1,0:T(8,128)(2,1)S(1)}, bf16[4,512,512]{2,1,0:T(8,128)(2,1)S(1)}, bf16[2048,256]{1,0:T(8,128)(2,1)S(1)}, bf16[256,128]{1,0:T(...) custom-call(s32[2,16]{1,0:T(2,128)} %bitcast.4, ...), custom_call_target="tpu_custom_call" | custom-call | bytes 4194304 | tf_op jit(solution)/shard_map/pallas_call | solution.py:290
  16.4 0.0 collective-permute-done.6.refs_4_
  16.5 0.0 collective-permute-done.5.refs_3_
  16.5 0.0 collective-permute-done.1.refs_0_
  16.5 0.3 collective-permute-done.3.refs_1_
  16.7 1.5 %shard_map.75 = (bf16[256,2048]{1,0:T(8,128)(2,1)S(1)}, f32[128,256]{1,0:T(8,128)S(1)}) custom-call(bf16[272,128]{1,0:T(8,128)(2,1)S(1)} %collective-permute-done.1.refs_0_, bf16[272,128]{1,0:T(8,128)(2,1)S(1)} %collective-permute-done.3.refs_1_, bf16[272,128]{1,0:T(8,128)(2,1)S(1)} %collective-permute-done.4.refs_2_, ...), custom_call_target="tpu_custom_call" | custom-call | tf_op jit(solution)/shard_map/pallas_call | solution.py:312
  18.2 0.1 collective-permute-start.7
  18.3 1.3 %collective-permute-done.7.other_ref = f32[128,256]{1,0:T(8,128)S(1)} collective-permute-done((f32[128,256]{1,0:T(8,128)S(1)}, f32[128,256]{1,0:T(8,128)S(1)}, u32[]{:S(2)}, u32[]{:S(2)}) %collective-permute-start.7) | collective-permute-done | bytes 131104 | tf_op jit(solution)/shard_map/ppermute | solution.py:272
  19.6 1.4 %shard_map.76 = (bf16[64,512]{1,0:T(8,128)(2,1)S(1)}, bf16[64,512]{1,0:T(8,128)(2,1)S(1)}, bf16[64,512]{1,0:T(8,128)(2,1)S(1)}, bf16[64,512]{1,0:T(8,128)(2,1)S(1)}) custom-call(bf16[256,2048]{1,0:T(8,128)(2,1)S(1)} %get-tuple-element.30.chosen_ref, f32[128,256]{1,0:T(8,128)S(1)} %get-tuple-element.31.mine_ref, ...), custom_call_target="tpu_custom_call" | custom-call | tf_op jit(solution)/shard_map/pallas_call | solution.py:322
  21.1 2.7 %collective-permute-start.8 = (bf16[64,512]{1,0:T(8,128)(2,1)S(1)}, bf16[64,512]{1,0:T(8,128)(2,1)S(1)}, u32[]{:S(2)}, u32[]{:S(2)}) collective-permute-start(bf16[64,512]{1,0:T(8,128)(2,1)S(1)} %get-tuple-element.34), channel_id=1, source_target_pairs={{0,12},{4,8},{8,4},{12,0},{1,13},{5,9},{9,5},{13,1},{2,14},{6,10},... | collective-permute-start | bytes 196616 | tf_op jit(solution)/shard_map/ppermute | solution.py:272
  23.7 0.0 collective-permute-start.9
  23.8 1.7 %collective-permute-start.10 = (bf16[64,512]{1,0:T(8,128)(2,1)S(1)}, bf16[64,512]{1,0:T(8,128)(2,1)S(1)}, u32[]{:S(2)}, u32[]{:S(2)}) collective-permute-start(bf16[64,512]{1,0:T(8,128)(2,1)S(1)} %get-tuple-element.36), channel_id=1, source_target_pairs={{0,8},{4,12},{8,0},{12,4},{1,9},{5,13},{9,1},{13,5},{2,10},{6,14},... | collective-permute-start | bytes 196616 | tf_op jit(solution)/shard_map/ppermute | solution.py:272
  25.5 2.4 %collective-permute-done.8.refs_0_ = bf16[64,512]{1,0:T(8,128)(2,1)S(1)} collective-permute-done((bf16[64,512]{1,0:T(8,128)(2,1)S(1)}, bf16[64,512]{1,0:T(8,128)(2,1)S(1)}, u32[]{:S(2)}, u32[]{:S(2)}) %collective-permute-start.8) | collective-permute-done | bytes 65568 | tf_op jit(solution)/shard_map/ppermute | solution.py:272
  27.9 2.0 %collective-permute-done.9.refs_1_ = bf16[64,512]{1,0:T(8,128)(2,1)S(1)} collective-permute-done((bf16[64,512]{1,0:T(8,128)(2,1)S(1)}, bf16[64,512]{1,0:T(8,128)(2,1)S(1)}, u32[]{:S(2)}, u32[]{:S(2)}) %collective-permute-start.9) | collective-permute-done | bytes 65568 | tf_op jit(solution)/shard_map/ppermute | solution.py:272
  29.9 0.9 %shard_map.77 = bf16[512,256]{1,0:T(8,128)(2,1)} custom-call(bf16[64,512]{1,0:T(8,128)(2,1)S(1)} %collective-permute-done.8.refs_0_, bf16[64,512]{1,0:T(8,128)(2,1)S(1)} %collective-permute-done.9.refs_1_, bf16[64,512]{1,0:T(8,128)(2,1)S(1)} %collective-permute-done.10.refs_2_, bf16[64,512]{1,0:T(8,128)(2,1)S(1)} %get-tuple-element.37.refs_3_, ...), custom_call_target="tpu_custom_call" | custom-call | tf_op jit(solution)/shard_map/pallas_call | solution.py:331
  (3 shorter events, 0.0 us)
Async XLA Ops:
  1.3 8.6 %collective-permute-start = (bf16[272,128]{1,0:T(8,128)(2,1)S(1)}, bf16[272,128]{1,0:T(8,128)(2,1)S(1)}, u32[]{:S(2)}, u32[]{:S(2)}) collective-permute-start(bf16[272,128]{1,0:T(8,128)(2,1)S(1)} %get-tuple-element.22), channel_id=1, source_target_pairs={{0,12},{4,8},{8,4},{12,0},{1,13},{5,9},{9,5},{13,1},{2,14},{6,10},... | collective-permute-start | bytes 208904 | tf_op jit(solution)/shard_map/ppermute | solution.py:272
  6.4 6.0 %collective-permute-start.2 = (bf16[272,128]{1,0:T(8,128)(2,1)S(1)}, bf16[272,128]{1,0:T(8,128)(2,1)S(1)}, u32[]{:S(2)}, u32[]{:S(2)}) collective-permute-start(bf16[272,128]{1,0:T(8,128)(2,1)S(1)} %get-tuple-element.23), channel_id=1, source_target_pairs={{0,8},{4,12},{8,0},{12,4},{1,9},{5,13},{9,1},{13,5},{2,10},{6,14},... | collective-permute-start | bytes 208904 | tf_op jit(solution)/shard_map/ppermute | solution.py:272
  6.4 10.0 %collective-permute-start.6 = (bf16[272,128]{1,0:T(8,128)(2,1)S(1)}, bf16[272,128]{1,0:T(8,128)(2,1)S(1)}, u32[]{:S(2)}, u32[]{:S(2)}) collective-permute-start(bf16[272,128]{1,0:T(8,128)(2,1)S(1)} %get-tuple-element.24), channel_id=1, source_target_pairs={{0,6},{2,4},{4,2},{6,0},{8,14},{10,12},{12,10},{14,8},{1,7},{3,5},... | collective-permute-start | bytes 208904 | tf_op jit(solution)/shard_map/ppermute | solution.py:272
  8.1 8.3 %collective-permute-start.4 = (bf16[272,128]{1,0:T(8,128)(2,1)S(1)}, bf16[272,128]{1,0:T(8,128)(2,1)S(1)}, u32[]{:S(2)}, u32[]{:S(2)}) collective-permute-start(bf16[272,128]{1,0:T(8,128)(2,1)S(1)} %get-tuple-element.24), channel_id=1, source_target_pairs={{0,4},{4,0},{8,12},{12,8},{1,5},{5,1},{9,13},{13,9},{2,6},{6,2},{1... | collective-permute-start | bytes 208904 | tf_op jit(solution)/shard_map/ppermute | solution.py:272
  9.4 7.1 %collective-permute-start.5 = (bf16[272,128]{1,0:T(8,128)(2,1)S(1)}, bf16[272,128]{1,0:T(8,128)(2,1)S(1)}, u32[]{:S(2)}, u32[]{:S(2)}) collective-permute-start(bf16[272,128]{1,0:T(8,128)(2,1)S(1)} %get-tuple-element.25.refs_7_), channel_id=1, source_target_pairs={{0,2},{2,0},{1,3},{3,1},{4,6},{6,4},{5,7},{7,5},{8,10},{10,8},{9,1... | collective-permute-start | bytes 208904 | tf_op jit(solution)/shard_map/ppermute | solution.py:272
  9.9 6.6 %collective-permute-start.1 = (bf16[272,128]{1,0:T(8,128)(2,1)S(1)}, bf16[272,128]{1,0:T(8,128)(2,1)S(1)}, u32[]{:S(2)}, u32[]{:S(2)}) collective-permute-start(bf16[272,128]{1,0:T(8,128)(2,1)S(1)} %collective-permute-done.refs_5_), channel_id=1, source_target_pairs={{0,2},{2,0},{1,3},{3,1},{4,6},{6,4},{5,7},{7,5},{8,10},{10,8},{9,1... | collective-permute-start | bytes 208904 | tf_op jit(solution)/shard_map/ppermute | solution.py:272
  12.4 4.3 %collective-permute-start.3 = (bf16[272,128]{1,0:T(8,128)(2,1)S(1)}, bf16[272,128]{1,0:T(8,128)(2,1)S(1)}, u32[]{:S(2)}, u32[]{:S(2)}) collective-permute-start(bf16[272,128]{1,0:T(8,128)(2,1)S(1)} %collective-permute-done.2.refs_6_), channel_id=1, source_target_pairs={{0,2},{2,0},{1,3},{3,1},{4,6},{6,4},{5,7},{7,5},{8,10},{10,8},{9,1... | collective-permute-start | bytes 208904 | tf_op jit(solution)/shard_map/ppermute | solution.py:272
  18.2 1.4 %collective-permute-start.7 = (f32[128,256]{1,0:T(8,128)S(1)}, f32[128,256]{1,0:T(8,128)S(1)}, u32[]{:S(2)}, u32[]{:S(2)}) collective-permute-start(f32[128,256]{1,0:T(8,128)S(1)} %get-tuple-element.31.mine_ref), channel_id=1, source_target_pairs={{0,1},{1,0},{2,3},{3,2},{4,5},{5,4},{6,7},{7,6},{8,9},{9,8},{10,11... | collective-permute-start | bytes 393224 | tf_op jit(solution)/shard_map/ppermute | solution.py:272
  21.1 6.9 %collective-permute-start.8 = (bf16[64,512]{1,0:T(8,128)(2,1)S(1)}, bf16[64,512]{1,0:T(8,128)(2,1)S(1)}, u32[]{:S(2)}, u32[]{:S(2)}) collective-permute-start(bf16[64,512]{1,0:T(8,128)(2,1)S(1)} %get-tuple-element.34), channel_id=1, source_target_pairs={{0,12},{4,8},{8,4},{12,0},{1,13},{5,9},{9,5},{13,1},{2,14},{6,10},... | collective-permute-start | bytes 196616 | tf_op jit(solution)/shard_map/ppermute | solution.py:272
  23.7 6.1 %collective-permute-start.9 = (bf16[64,512]{1,0:T(8,128)(2,1)S(1)}, bf16[64,512]{1,0:T(8,128)(2,1)S(1)}, u32[]{:S(2)}, u32[]{:S(2)}) collective-permute-start(bf16[64,512]{1,0:T(8,128)(2,1)S(1)} %get-tuple-element.35), channel_id=1, source_target_pairs={{0,4},{4,0},{8,12},{12,8},{1,5},{5,1},{9,13},{13,9},{2,6},{6,2},{1... | collective-permute-start | bytes 196616 | tf_op jit(solution)/shard_map/ppermute | solution.py:272
  23.8 6.1 %collective-permute-start.10 = (bf16[64,512]{1,0:T(8,128)(2,1)S(1)}, bf16[64,512]{1,0:T(8,128)(2,1)S(1)}, u32[]{:S(2)}, u32[]{:S(2)}) collective-permute-start(bf16[64,512]{1,0:T(8,128)(2,1)S(1)} %get-tuple-element.36), channel_id=1, source_target_pairs={{0,8},{4,12},{8,0},{12,4},{1,9},{5,13},{9,1},{13,5},{2,10},{6,14},... | collective-permute-start | bytes 196616 | tf_op jit(solution)/shard_map/ppermute | solution.py:272

commit v8 on v7

--- a/solution.py
+++ b/solution.py
@@ -145,23 +145,14 @@
         copy.wait()
 
 
-def correlate_kernel(segs, blocks, own, *refs):
-    chunks = [refs[i] for i in [7, 2, 6, 5, 3, 4, 1, 0]]
-    table_ref, lag_ref, take_ref, find_ref, chosen_ref, partial_ref = refs[segs * SPANS :]
+def transform(chunks, rows, table_ref):
     fibre = lax.axis_index("fibre")
     span = S // SPANS
     band = F // SPANS
-    rows = blocks * own
-    count = segs * rows
-    lines = take_ref.shape[0] // 2
-    tiles = span // LANES
     folds = []
-    for k in range(SPANS):
-        whole = [
-            jnp.concatenate([chunks[u * SPANS + k][q * rows : (q + 1) * rows, :] for q in range(tiles)], axis=1)
-            for u in range(segs)
-        ]
-        folds.append(jnp.concatenate(whole, axis=0).astype(jnp.float32))
+    for chunk in chunks:
+        whole = [chunk[q * rows : (q + 1) * rows, :] for q in range(span // LANES)]
+        folds.append(jnp.concatenate(whole, axis=1).astype(jnp.float32))
     flip = fibre % 2 == 1
     turn = jnp.where(flip, -1.0, 1.0)
     late = jnp.where(fibre >= 2, -1.0, 1.0)
@@ -178,12 +169,28 @@
             real, imag = part[:, :band], part[:, band:]
         else:
             mixed = dot(both, table_ref[j])
-            e_c, e_s = mixed[:count, :band], mixed[:count, band:]
-            d_c, d_s = mixed[count:, :band], mixed[count:, band:]
+            e_c, e_s = mixed[:rows, :band], mixed[:rows, band:]
+            d_c, d_s = mixed[rows:, :band], mixed[rows:, band:]
             real, imag = (e_c + d_s, e_s - d_c) if j == 1 else (e_c - d_s, e_s + d_c)
         reals.append(real.astype(jnp.bfloat16))
         imags.append(imag.astype(jnp.bfloat16))
-    spectra = jnp.concatenate(reals + imags, axis=1)
+    return jnp.concatenate(reals + imags, axis=1)
+
+
+def spectra_kernel(blocks, own, *refs):
+    refs[-1][...] = transform(refs[:SPANS], blocks * own, refs[SPANS])
+
+
+def correlate_kernel(segs, blocks, own, *refs):
+    chunks = [refs[i] for i in [7, 2, 6, 5, 3, 4, 1, 0]]
+    own_ref, table_ref, lag_ref, take_ref, find_ref, chosen_ref, partial_ref = refs[segs * SPANS :]
+    rows = blocks * own
+    lines = take_ref.shape[0] // 2
+    tiles = S // SPANS // LANES
+    spectra = [own_ref[...]] + [
+        transform(chunks[u * SPANS : (u + 1) * SPANS], rows, table_ref) for u in range(1, segs)
+    ]
+    spectra = jnp.concatenate(spectra, axis=0)
     chosen = dot(take_ref[...], spectra)
     chosen_ref[...] = chosen.astype(jnp.bfloat16)
     a0, a1 = chosen[:lines, :F], chosen[:lines, F:]
@@ -286,8 +293,9 @@
     )(*(pltpu.with_memory_space_constraint(x, pltpu.HBM) for x in (records[0], observed, lag_mask)))
     held = [along("fibre", send[k], lambda i: i ^ k) for k in range(SPANS - 1, 0, -1)]
     held = [send[0]] + held[::-1]
-    constants = [jnp.asarray(c) for c in (table, np.ascontiguousarray(table.transpose(0, 2, 1)), lags)]
-    table, table_back, lags, take, give, find, order = pl.pallas_call(
+    table_back = jnp.asarray(np.ascontiguousarray(table.transpose(0, 2, 1)))
+    constants = [jnp.asarray(c) for c in (table, lags)]
+    table, lags, take, give, find, order = pl.pallas_call(
         functools.partial(prepare_kernel, segs, blocks, own, pairs_dev, share),
         out_shape=[pltpu.VMEM(c.shape, low) for c in constants]
         + [
@@ -309,13 +317,20 @@
             else along("seg", held[k], lambda i: (i + u) % segs)
             for k in range(SPANS - 1, -1, -1)
         ][::-1]
+    spectra = pl.pallas_call(
+        functools.partial(spectra_kernel, blocks, own),
+        out_shape=pltpu.VMEM((rows, 2 * F), low),
+        in_specs=[vmem] * (SPANS + 1),
+        out_specs=vmem,
+        compiler_params=limit,
+    )(*held[:SPANS], table)
     chosen, partial = pl.pallas_call(
         functools.partial(correlate_kernel, segs, blocks, own),
         out_shape=[pltpu.VMEM((2 * lines, 2 * F), low), pltpu.VMEM((lines, LAGS), jnp.float32)],
-        in_specs=[vmem] * (segs * SPANS + 4),
+        in_specs=[vmem] * (segs * SPANS + 5),
         out_specs=[vmem] * 2,
         compiler_params=limit,
-    )(*[held[i] for i in (7, 6, 1, 4, 5, 3, 2, 0)], table, lags, take, find)
+    )(*[held[i] for i in (7, 6, 1, 4, 5, 3, 2, 0)], spectra, table, lags, take, find)
     mine, other = partial, along("rec", partial, lambda i: (i + 1) % recs)
     for _ in range(2, recs):
         mine, other = mine + other, along("rec", other, lambda i: (i + 1) % recs)

time: 31 us -> 30.6 us (0.987)
  Pallas kernels: 7.64 us -> 7.11 us
    pallas_call x1, Pallas kernels: 2.52 us -> 1.88 us  [by_own_k(): pl.pallas_call(functools.partial(prepare_kernel, segs, blocks, own, pairs...]
    pallas_call x0 -> x1, Pallas kernels: none -> 0.47 us  [by_own_k(): pl.pallas_call(functools.partial(spectra_kernel, blocks, own), out_shape=...]
    pallas_call x1, Pallas kernels: 1.48 us -> 1.12 us  [by_own_k(): pl.pallas_call(functools.partial(correlate_kernel, segs, blocks, own), ou...]
where the time goes in v8:
time: 30.6 us; the launch traced here: 30.5 us
  starting transfers between devices  16.1 us (53%)
  waiting for transfers between devices  7.14 us (23%)
  Pallas kernels  7.11 us (23%)
    ppermute x11, starting transfers between devices, along(): lax.ppermute(array, axis, [(i, target(i)) for i in range(lax.axis_size(ax...  16.1 us
    ppermute x11, waiting for transfers between devices, along(): lax.ppermute(array, axis, [(i, target(i)) for i in range(lax.axis_size(ax...  7.14 us
    pallas_call x1, Pallas kernels, by_own_k(): pl.pallas_call(functools.partial(prepare_kernel, segs, blocks, own, pairs...  1.88 us
    pallas_call x1, Pallas kernels, by_own_k(): pl.pallas_call(functools.partial(adjoint_kernel, blocks, own), out_shape=...  1.42 us
    pallas_call x1, Pallas kernels, by_own_k(): pl.pallas_call(functools.partial(pack_kernel, blocks, own), out_shape=[pl...  1.28 us
    pallas_call x1, Pallas kernels, by_own_k(): pl.pallas_call(functools.partial(correlate_kernel, segs, blocks, own), ou...  1.12 us
    pallas_call x1, Pallas kernels, by_own_k(): pl.pallas_call(unpack_kernel, out_shape=jax.ShapeDtypeStruct((span, count...  0.94 us
  transfers between devices with their start and end apart: 11, of which 5 were waited for; matrix products, arithmetic and copies ran while one was open for 0% of the time, Pallas kernels for 8%

profile of v8, /device:TPU:0, one launch (start us, length us, event | category | flops | bytes accessed | tf_op | source)
XLA Modules:
  0.0 30.5 jit_solution(12013941412086725181)
XLA Ops:
  0.0 1.3 %shard_map.73 = (bf16[272,128]{1,0:T(8,128)(2,1)S(1)}, bf16[272,128]{1,0:T(8,128)(2,1)S(1)}, bf16[272,128]{1,0:T(8,128)(2,1)S(1)}, bf16[272,128]{1,0:T(8,128)(2,1)S(1)}) custom-call(bf16[512,256]{1,0:T(8,128)(2,1)} %bitcast.3, f32[2,32,256]{2,1,0:T(8,128)} %observed_hbm.1, s32[2,256]{1,0:T(2,128)} %mask_hbm.1), custom_call_target="tpu_custom_call" | custom-call | tf_op jit(solution)/shard_map/pallas_call | solution.py:281
  1.3 5.1 %collective-permute-start = (bf16[272,128]{1,0:T(8,128)(2,1)S(1)}, bf16[272,128]{1,0:T(8,128)(2,1)S(1)}, u32[]{:S(2)}, u32[]{:S(2)}) collective-permute-start(bf16[272,128]{1,0:T(8,128)(2,1)S(1)} %get-tuple-element.21), channel_id=1, source_target_pairs={{0,12},{4,8},{8,4},{12,0},{1,13},{5,9},{9,5},{13,1},{2,14},{6,10},... | collective-permute-start | bytes 208904 | tf_op jit(solution)/shard_map/ppermute | solution.py:279
  6.4 0.0 collective-permute-start.2
  6.4 1.7 %collective-permute-start.6 = (bf16[272,128]{1,0:T(8,128)(2,1)S(1)}, bf16[272,128]{1,0:T(8,128)(2,1)S(1)}, u32[]{:S(2)}, u32[]{:S(2)}) collective-permute-start(bf16[272,128]{1,0:T(8,128)(2,1)S(1)} %get-tuple-element.23), channel_id=1, source_target_pairs={{0,6},{2,4},{4,2},{6,0},{8,14},{10,12},{12,10},{14,8},{1,7},{3,5},... | collective-permute-start | bytes 208904 | tf_op jit(solution)/shard_map/ppermute | solution.py:279
  8.1 1.2 %collective-permute-start.4 = (bf16[272,128]{1,0:T(8,128)(2,1)S(1)}, bf16[272,128]{1,0:T(8,128)(2,1)S(1)}, u32[]{:S(2)}, u32[]{:S(2)}) collective-permute-start(bf16[272,128]{1,0:T(8,128)(2,1)S(1)} %get-tuple-element.23), channel_id=1, source_target_pairs={{0,4},{4,0},{8,12},{12,8},{1,5},{5,1},{9,13},{13,9},{2,6},{6,2},{1... | collective-permute-start | bytes 208904 | tf_op jit(solution)/shard_map/ppermute | solution.py:279
  9.4 0.5 %collective-permute-start.5 = (bf16[272,128]{1,0:T(8,128)(2,1)S(1)}, bf16[272,128]{1,0:T(8,128)(2,1)S(1)}, u32[]{:S(2)}, u32[]{:S(2)}) collective-permute-start(bf16[272,128]{1,0:T(8,128)(2,1)S(1)} %get-tuple-element.24.refs_0_.refs_7_), channel_id=1, source_target_pairs={{0,2},{2,0},{1,3},{3,1},{4,6},{6,4},{5,7},{7,5},{8,10},{10,8},{9,1... | collective-permute-start | bytes 208904 | tf_op jit(solution)/shard_map/ppermute | solution.py:279
  9.9 1.5 %collective-permute-start.1 = (bf16[272,128]{1,0:T(8,128)(2,1)S(1)}, bf16[272,128]{1,0:T(8,128)(2,1)S(1)}, u32[]{:S(2)}, u32[]{:S(2)}) collective-permute-start(bf16[272,128]{1,0:T(8,128)(2,1)S(1)} %collective-permute-done.refs_3_.refs_5_), channel_id=1, source_target_pairs={{0,2},{2,0},{1,3},{3,1},{4,6},{6,4},{5,7},{7,5},{8,10},{10,8},{9,1... | collective-permute-start | bytes 208904 | tf_op jit(solution)/shard_map/ppermute | solution.py:279
  11.4 1.0 %collective-permute-done.2.refs_2_.refs_6_ = bf16[272,128]{1,0:T(8,128)(2,1)S(1)} collective-permute-done((bf16[272,128]{1,0:T(8,128)(2,1)S(1)}, bf16[272,128]{1,0:T(8,128)(2,1)S(1)}, u32[]{:S(2)}, u32[]{:S(2)}) %collective-permute-start.2) | collective-permute-done | bytes 69664 | tf_op jit(solution)/shard_map/ppermute | solution.py:279
  12.4 1.5 %collective-permute-start.3 = (bf16[272,128]{1,0:T(8,128)(2,1)S(1)}, bf16[272,128]{1,0:T(8,128)(2,1)S(1)}, u32[]{:S(2)}, u32[]{:S(2)}) collective-permute-start(bf16[272,128]{1,0:T(8,128)(2,1)S(1)} %collective-permute-done.2.refs_2_.refs_6_), channel_id=1, source_target_pairs={{0,2},{2,0},{1,3},{3,1},{4,6},{6,4},{5,7},{7,5},{8,10},{10,8},{9,1... | collective-permute-start | bytes 208904 | tf_op jit(solution)/shard_map/ppermute | solution.py:279
  13.9 1.9 %shard_map.74 = (bf16[4,512,512]{2,1,0:T(8,128)(2,1)S(1)}, bf16[2048,256]{1,0:T(8,128)(2,1)S(1)}, bf16[256,128]{1,0:T(8,128)(2,1)S(1)}, bf16[64,256]{1,0:T(8,128...) custom-call(s32[2,16]{1,0:T(2,128)} %bitcast.4, bf16[4,512,512]{2,1,0:T(8,128)(2,1)} %constant.7.clone.refs_0_, ...), custom_call_target="tpu_custom_call" | custom-call | bytes 4194304 | tf_op jit(solution)/shard_map/pallas_call | solution.py:298
  15.8 0.5 %shard_map.75.refs_8_ = bf16[64,2048]{1,0:T(8,128)(2,1)S(1)} custom-call(bf16[272,128]{1,0:T(8,128)(2,1)S(1)} %get-tuple-element.24.refs_0_.refs_7_, bf16[272,128]{1,0:T(8,128)(2,1)S(1)} %collective-permute-done.4.refs_1_.refs_2_, bf16[272,128]{1,0:T(8,128)(2,1)S(1)} %collective-permute-done.2.refs_2_.refs_6_, ...), custom_call_target="tpu_custom_call" | custom-call | tf_op jit(solution)/shard_map/pallas_call | solution.py:320
  16.3 0.0 copy-start
  16.3 0.0 collective-permute-done.6.refs_4_
  16.3 0.4 %collective-permute-done.3.refs_1_ = bf16[272,128]{1,0:T(8,128)(2,1)S(1)} collective-permute-done((bf16[272,128]{1,0:T(8,128)(2,1)S(1)}, bf16[272,128]{1,0:T(8,128)(2,1)S(1)}, u32[]{:S(2)}, u32[]{:S(2)}) %collective-permute-start.3) | collective-permute-done | bytes 69664 | tf_op jit(solution)/shard_map/ppermute | solution.py:279
  16.7 1.1 %shard_map.76 = (bf16[256,2048]{1,0:T(8,128)(2,1)S(1)}, f32[128,256]{1,0:T(8,128)S(1)}) custom-call(bf16[272,128]{1,0:T(8,128)(2,1)S(1)} %collective-permute-done.1.refs_0_, bf16[272,128]{1,0:T(8,128)(2,1)S(1)} %collective-permute-done.3.refs_1_, bf16[272,128]{1,0:T(8,128)(2,1)S(1)} %collective-permute-done.4.refs_1_.refs_2_, ...), custom_call_target="tpu_custom_call" | custom-call | tf_op jit(solution)/shard_map/pallas_call | solution.py:327
  17.9 0.1 collective-permute-start.7
  17.9 1.3 %collective-permute-done.7.other_ref = f32[128,256]{1,0:T(8,128)S(1)} collective-permute-done((f32[128,256]{1,0:T(8,128)S(1)}, f32[128,256]{1,0:T(8,128)S(1)}, u32[]{:S(2)}, u32[]{:S(2)}) %collective-permute-start.7) | collective-permute-done | bytes 131104 | tf_op jit(solution)/shard_map/ppermute | solution.py:279
  19.3 1.4 %shard_map.77 = (bf16[64,512]{1,0:T(8,128)(2,1)S(1)}, bf16[64,512]{1,0:T(8,128)(2,1)S(1)}, bf16[64,512]{1,0:T(8,128)(2,1)S(1)}, bf16[64,512]{1,0:T(8,128)(2,1)S(1)}) custom-call(bf16[256,2048]{1,0:T(8,128)(2,1)S(1)} %get-tuple-element.29.chosen_ref, f32[128,256]{1,0:T(8,128)S(1)} %get-tuple-element.30.mine_ref, ...), custom_call_target="tpu_custom_call" | custom-call | tf_op jit(solution)/shard_map/pallas_call | solution.py:337
  20.7 2.7 %collective-permute-start.8 = (bf16[64,512]{1,0:T(8,128)(2,1)S(1)}, bf16[64,512]{1,0:T(8,128)(2,1)S(1)}, u32[]{:S(2)}, u32[]{:S(2)}) collective-permute-start(bf16[64,512]{1,0:T(8,128)(2,1)S(1)} %get-tuple-element.32), channel_id=1, source_target_pairs={{0,12},{4,8},{8,4},{12,0},{1,13},{5,9},{9,5},{13,1},{2,14},{6,10},... | collective-permute-start | bytes 196616 | tf_op jit(solution)/shard_map/ppermute | solution.py:279
  23.4 0.0 collective-permute-start.9
  23.4 1.7 %collective-permute-start.10 = (bf16[64,512]{1,0:T(8,128)(2,1)S(1)}, bf16[64,512]{1,0:T(8,128)(2,1)S(1)}, u32[]{:S(2)}, u32[]{:S(2)}) collective-permute-start(bf16[64,512]{1,0:T(8,128)(2,1)S(1)} %get-tuple-element.34), channel_id=1, source_target_pairs={{0,8},{4,12},{8,0},{12,4},{1,9},{5,13},{9,1},{13,5},{2,10},{6,14},... | collective-permute-start | bytes 196616 | tf_op jit(solution)/shard_map/ppermute | solution.py:279
  25.2 2.4 %collective-permute-done.8.refs_0_ = bf16[64,512]{1,0:T(8,128)(2,1)S(1)} collective-permute-done((bf16[64,512]{1,0:T(8,128)(2,1)S(1)}, bf16[64,512]{1,0:T(8,128)(2,1)S(1)}, u32[]{:S(2)}, u32[]{:S(2)}) %collective-permute-start.8) | collective-permute-done | bytes 65568 | tf_op jit(solution)/shard_map/ppermute | solution.py:279
  27.6 2.0 %collective-permute-done.9.refs_1_ = bf16[64,512]{1,0:T(8,128)(2,1)S(1)} collective-permute-done((bf16[64,512]{1,0:T(8,128)(2,1)S(1)}, bf16[64,512]{1,0:T(8,128)(2,1)S(1)}, u32[]{:S(2)}, u32[]{:S(2)}) %collective-permute-start.9) | collective-permute-done | bytes 65568 | tf_op jit(solution)/shard_map/ppermute | solution.py:279
  29.5 0.9 %shard_map.78 = bf16[512,256]{1,0:T(8,128)(2,1)} custom-call(bf16[64,512]{1,0:T(8,128)(2,1)S(1)} %collective-permute-done.8.refs_0_, bf16[64,512]{1,0:T(8,128)(2,1)S(1)} %collective-permute-done.9.refs_1_, bf16[64,512]{1,0:T(8,128)(2,1)S(1)} %collective-permute-done.10.refs_2_, bf16[64,512]{1,0:T(8,128)(2,1)S(1)} %get-tuple-element.35.refs_3_, ...), custom_call_target="tpu_custom_call" | custom-call | tf_op jit(solution)/shard_map/pallas_call | solution.py:346
  (6 shorter events, 0.0 us)
Async XLA Ops:
  1.3 8.6 %collective-permute-start = (bf16[272,128]{1,0:T(8,128)(2,1)S(1)}, bf16[272,128]{1,0:T(8,128)(2,1)S(1)}, u32[]{:S(2)}, u32[]{:S(2)}) collective-permute-start(bf16[272,128]{1,0:T(8,128)(2,1)S(1)} %get-tuple-element.21), channel_id=1, source_target_pairs={{0,12},{4,8},{8,4},{12,0},{1,13},{5,9},{9,5},{13,1},{2,14},{6,10},... | collective-permute-start | bytes 208904 | tf_op jit(solution)/shard_map/ppermute | solution.py:279
  6.4 6.0 %collective-permute-start.2 = (bf16[272,128]{1,0:T(8,128)(2,1)S(1)}, bf16[272,128]{1,0:T(8,128)(2,1)S(1)}, u32[]{:S(2)}, u32[]{:S(2)}) collective-permute-start(bf16[272,128]{1,0:T(8,128)(2,1)S(1)} %get-tuple-element.22), channel_id=1, source_target_pairs={{0,8},{4,12},{8,0},{12,4},{1,9},{5,13},{9,1},{13,5},{2,10},{6,14},... | collective-permute-start | bytes 208904 | tf_op jit(solution)/shard_map/ppermute | solution.py:279
  6.4 9.9 %collective-permute-start.6 = (bf16[272,128]{1,0:T(8,128)(2,1)S(1)}, bf16[272,128]{1,0:T(8,128)(2,1)S(1)}, u32[]{:S(2)}, u32[]{:S(2)}) collective-permute-start(bf16[272,128]{1,0:T(8,128)(2,1)S(1)} %get-tuple-element.23), channel_id=1, source_target_pairs={{0,6},{2,4},{4,2},{6,0},{8,14},{10,12},{12,10},{14,8},{1,7},{3,5},... | collective-permute-start | bytes 208904 | tf_op jit(solution)/shard_map/ppermute | solution.py:279
  8.1 7.7 %collective-permute-start.4 = (bf16[272,128]{1,0:T(8,128)(2,1)S(1)}, bf16[272,128]{1,0:T(8,128)(2,1)S(1)}, u32[]{:S(2)}, u32[]{:S(2)}) collective-permute-start(bf16[272,128]{1,0:T(8,128)(2,1)S(1)} %get-tuple-element.23), channel_id=1, source_target_pairs={{0,4},{4,0},{8,12},{12,8},{1,5},{5,1},{9,13},{13,9},{2,6},{6,2},{1... | collective-permute-start | bytes 208904 | tf_op jit(solution)/shard_map/ppermute | solution.py:279
  9.4 6.9 %collective-permute-start.5 = (bf16[272,128]{1,0:T(8,128)(2,1)S(1)}, bf16[272,128]{1,0:T(8,128)(2,1)S(1)}, u32[]{:S(2)}, u32[]{:S(2)}) collective-permute-start(bf16[272,128]{1,0:T(8,128)(2,1)S(1)} %get-tuple-element.24.refs_0_.refs_7_), channel_id=1, source_target_pairs={{0,2},{2,0},{1,3},{3,1},{4,6},{6,4},{5,7},{7,5},{8,10},{10,8},{9,1... | collective-permute-start | bytes 208904 | tf_op jit(solution)/shard_map/ppermute | solution.py:279
  9.9 6.4 %collective-permute-start.1 = (bf16[272,128]{1,0:T(8,128)(2,1)S(1)}, bf16[272,128]{1,0:T(8,128)(2,1)S(1)}, u32[]{:S(2)}, u32[]{:S(2)}) collective-permute-start(bf16[272,128]{1,0:T(8,128)(2,1)S(1)} %collective-permute-done.refs_3_.refs_5_), channel_id=1, source_target_pairs={{0,2},{2,0},{1,3},{3,1},{4,6},{6,4},{5,7},{7,5},{8,10},{10,8},{9,1... | collective-permute-start | bytes 208904 | tf_op jit(solution)/shard_map/ppermute | solution.py:279
  12.4 4.3 %collective-permute-start.3 = (bf16[272,128]{1,0:T(8,128)(2,1)S(1)}, bf16[272,128]{1,0:T(8,128)(2,1)S(1)}, u32[]{:S(2)}, u32[]{:S(2)}) collective-permute-start(bf16[272,128]{1,0:T(8,128)(2,1)S(1)} %collective-permute-done.2.refs_2_.refs_6_), channel_id=1, source_target_pairs={{0,2},{2,0},{1,3},{3,1},{4,6},{6,4},{5,7},{7,5},{8,10},{10,8},{9,1... | collective-permute-start | bytes 208904 | tf_op jit(solution)/shard_map/ppermute | solution.py:279
  16.3 3.0 %copy-start = (bf16[4,512,512]{2,1,0:T(8,128)(2,1)S(1)}, bf16[4,512,512]{2,1,0:T(8,128)(2,1)}, u32[]{:S(2)}) copy-start(bf16[4,512,512]{2,1,0:T(8,128)(2,1)} %constant.6.clone.back_ref) | copy-start | bytes 6291460
  17.9 1.4 %collective-permute-start.7 = (f32[128,256]{1,0:T(8,128)S(1)}, f32[128,256]{1,0:T(8,128)S(1)}, u32[]{:S(2)}, u32[]{:S(2)}) collective-permute-start(f32[128,256]{1,0:T(8,128)S(1)} %get-tuple-element.30.mine_ref), channel_id=1, source_target_pairs={{0,1},{1,0},{2,3},{3,2},{4,5},{5,4},{6,7},{7,6},{8,9},{9,8},{10,11... | collective-permute-start | bytes 393224 | tf_op jit(solution)/shard_map/ppermute | solution.py:279
  20.7 6.9 %collective-permute-start.8 = (bf16[64,512]{1,0:T(8,128)(2,1)S(1)}, bf16[64,512]{1,0:T(8,128)(2,1)S(1)}, u32[]{:S(2)}, u32[]{:S(2)}) collective-permute-start(bf16[64,512]{1,0:T(8,128)(2,1)S(1)} %get-tuple-element.32), channel_id=1, source_target_pairs={{0,12},{4,8},{8,4},{12,0},{1,13},{5,9},{9,5},{13,1},{2,14},{6,10},... | collective-permute-start | bytes 196616 | tf_op jit(solution)/shard_map/ppermute | solution.py:279
  23.4 6.1 %collective-permute-start.9 = (bf16[64,512]{1,0:T(8,128)(2,1)S(1)}, bf16[64,512]{1,0:T(8,128)(2,1)S(1)}, u32[]{:S(2)}, u32[]{:S(2)}) collective-permute-start(bf16[64,512]{1,0:T(8,128)(2,1)S(1)} %get-tuple-element.33), channel_id=1, source_target_pairs={{0,4},{4,0},{8,12},{12,8},{1,5},{5,1},{9,13},{13,9},{2,6},{6,2},{1... | collective-permute-start | bytes 196616 | tf_op jit(solution)/shard_map/ppermute | solution.py:279
  23.4 6.1 %collective-permute-start.10 = (bf16[64,512]{1,0:T(8,128)(2,1)S(1)}, bf16[64,512]{1,0:T(8,128)(2,1)S(1)}, u32[]{:S(2)}, u32[]{:S(2)}) collective-permute-start(bf16[64,512]{1,0:T(8,128)(2,1)S(1)} %get-tuple-element.34), channel_id=1, source_target_pairs={{0,8},{4,12},{8,0},{12,4},{1,9},{5,13},{9,1},{13,5},{2,10},{6,14},... | collective-permute-start | bytes 196616 | tf_op jit(solution)/shard_map/ppermute | solution.py:279

commit v9 on v8

--- a/solution.py
+++ b/solution.py
@@ -183,7 +183,7 @@
 
 def correlate_kernel(segs, blocks, own, *refs):
     chunks = [refs[i] for i in [7, 2, 6, 5, 3, 4, 1, 0]]
-    own_ref, table_ref, lag_ref, take_ref, find_ref, chosen_ref, partial_ref = refs[segs * SPANS :]
+    own_ref, table_ref, lag_ref, take_ref, find_ref, chosen_ref, partial_ref, sent_ref = refs[segs * SPANS :]
     rows = blocks * own
     lines = take_ref.shape[0] // 2
     tiles = S // SPANS // LANES
@@ -201,6 +201,7 @@
     packed = jnp.concatenate([chunk[tiles * rows :, :] for chunk in chunks], axis=0)
     seen = jnp.concatenate([dot(find_ref[h], packed) for h in range(LAGS // LANES)], axis=1)
     partial_ref[...] = partial - seen
+    sent_ref[...] = (partial - seen).astype(jnp.bfloat16)
 
 
 def adjoint_kernel(blocks, own, chosen_ref, mine_ref, other_ref, back_ref, lag_ref, give_ref, *out_refs):
@@ -208,14 +209,14 @@
     band = F // SPANS
     lines = mine_ref.shape[0]
     count = blocks * own
-    misfit = mine_ref[...] + other_ref[...]
+    misfit = mine_ref[...] + other_ref[...].astype(jnp.float32)
     weights = jnp.where(misfit > -0.5 * MASKED, jnp.tanh(misfit), 0.0).astype(jnp.bfloat16)
-    adjoint = dot(weights, lag_ref[...], _NT).astype(jnp.bfloat16).astype(jnp.float32)
+    adjoint = dot(weights, lag_ref[...], _NT).astype(jnp.bfloat16)
     g0, g1 = adjoint[:, :F], adjoint[:, F:]
-    a0 = chosen_ref[:lines, :F].astype(jnp.float32)
-    a1 = chosen_ref[:lines, F:].astype(jnp.float32)
-    b0 = chosen_ref[lines:, :F].astype(jnp.float32)
-    b1 = chosen_ref[lines:, F:].astype(jnp.float32)
+    a0 = chosen_ref[:lines, :F]
+    a1 = chosen_ref[:lines, F:]
+    b0 = chosen_ref[lines:, :F]
+    b1 = chosen_ref[lines:, F:]
     low = jnp.bfloat16
     first = jnp.concatenate([(g0 * b0 - g1 * b1).astype(low), (g0 * b1 + g1 * b0).astype(low)], axis=1)
     second = jnp.concatenate([(g0 * a0 + g1 * a1).astype(low), (g0 * a1 - g1 * a0).astype(low)], axis=1)
@@ -324,14 +325,14 @@
         out_specs=vmem,
         compiler_params=limit,
     )(*held[:SPANS], table)
-    chosen, partial = pl.pallas_call(
+    chosen, partial, rounded = pl.pallas_call(
         functools.partial(correlate_kernel, segs, blocks, own),
-        out_shape=[pltpu.VMEM((2 * lines, 2 * F), low), pltpu.VMEM((lines, LAGS), jnp.float32)],
+        out_shape=[pltpu.VMEM((2 * lines, 2 * F), low), pltpu.VMEM((lines, LAGS), jnp.float32), pltpu.VMEM((lines, LAGS), low)],
         in_specs=[vmem] * (segs * SPANS + 5),
-        out_specs=[vmem] * 2,
+        out_specs=[vmem] * 3,
         compiler_params=limit,
     )(*[held[i] for i in (7, 6, 1, 4, 5, 3, 2, 0)], spectra, table, lags, take, find)
-    mine, other = partial, along("rec", partial, lambda i: (i + 1) % recs)
+    mine, other = partial, along("rec", rounded, lambda i: (i + 1) % recs)
     for _ in range(2, recs):
         mine, other = mine + other, along("rec", other, lambda i: (i + 1) % recs)
     back = pl.pallas_call(

time: 30.6 us -> 30.4 us (level)
  no operation moved by 1% of the time
where the time goes in v9:
time: 30.4 us; the launch traced here: 30.2 us
  starting transfers between devices  16.1 us (53%)
  waiting for transfers between devices  7.06 us (23%)
  Pallas kernels  6.95 us (23%)
    ppermute x11, starting transfers between devices, along(): lax.ppermute(array, axis, [(i, target(i)) for i in range(lax.axis_size(ax...  16.1 us
    ppermute x11, waiting for transfers between devices, along(): lax.ppermute(array, axis, [(i, target(i)) for i in range(lax.axis_size(ax...  7.06 us
    pallas_call x1, Pallas kernels, by_own_k(): pl.pallas_call(functools.partial(prepare_kernel, segs, blocks, own, pairs...  1.88 us
    pallas_call x1, Pallas kernels, by_own_k(): pl.pallas_call(functools.partial(pack_kernel, blocks, own), out_shape=[pl...  1.28 us
    pallas_call x1, Pallas kernels, by_own_k(): pl.pallas_call(functools.partial(adjoint_kernel, blocks, own), out_shape=...  1.25 us
    pallas_call x1, Pallas kernels, by_own_k(): pl.pallas_call(functools.partial(correlate_kernel, segs, blocks, own), ou...  1.12 us
    pallas_call x1, Pallas kernels, by_own_k(): pl.pallas_call(unpack_kernel, out_shape=jax.ShapeDtypeStruct((span, count...  0.94 us
  transfers between devices with their start and end apart: 11, of which 5 were waited for; matrix products, arithmetic and copies ran while one was open for 0% of the time, Pallas kernels for 8%

profile of v9, /device:TPU:0, one launch (start us, length us, event | category | flops | bytes accessed | tf_op | source)
XLA Modules:
  0.0 30.2 jit_solution(5397252485718138049)
XLA Ops:
  0.0 1.3 %shard_map.73 = (bf16[272,128]{1,0:T(8,128)(2,1)S(1)}, bf16[272,128]{1,0:T(8,128)(2,1)S(1)}, bf16[272,128]{1,0:T(8,128)(2,1)S(1)}, bf16[272,128]{1,0:T(8,128)(2,1)S(1)}) custom-call(bf16[512,256]{1,0:T(8,128)(2,1)} %bitcast.3, f32[2,32,256]{2,1,0:T(8,128)} %observed_hbm.1, s32[2,256]{1,0:T(2,128)} %mask_hbm.1), custom_call_target="tpu_custom_call" | custom-call | tf_op jit(solution)/shard_map/pallas_call | solution.py:282
  1.3 5.1 %collective-permute-start = (bf16[272,128]{1,0:T(8,128)(2,1)S(1)}, bf16[272,128]{1,0:T(8,128)(2,1)S(1)}, u32[]{:S(2)}, u32[]{:S(2)}) collective-permute-start(bf16[272,128]{1,0:T(8,128)(2,1)S(1)} %get-tuple-element.22), channel_id=1, source_target_pairs={{0,12},{4,8},{8,4},{12,0},{1,13},{5,9},{9,5},{13,1},{2,14},{6,10},... | collective-permute-start | bytes 208904 | tf_op jit(solution)/shard_map/ppermute | solution.py:280
  6.4 1.7 %collective-permute-start.6 = (bf16[272,128]{1,0:T(8,128)(2,1)S(1)}, bf16[272,128]{1,0:T(8,128)(2,1)S(1)}, u32[]{:S(2)}, u32[]{:S(2)}) collective-permute-start(bf16[272,128]{1,0:T(8,128)(2,1)S(1)} %get-tuple-element.24), channel_id=1, source_target_pairs={{0,6},{2,4},{4,2},{6,0},{8,14},{10,12},{12,10},{14,8},{1,7},{3,5},... | collective-permute-start | bytes 208904 | tf_op jit(solution)/shard_map/ppermute | solution.py:280
  8.1 1.2 %collective-permute-start.4 = (bf16[272,128]{1,0:T(8,128)(2,1)S(1)}, bf16[272,128]{1,0:T(8,128)(2,1)S(1)}, u32[]{:S(2)}, u32[]{:S(2)}) collective-permute-start(bf16[272,128]{1,0:T(8,128)(2,1)S(1)} %get-tuple-element.24), channel_id=1, source_target_pairs={{0,4},{4,0},{8,12},{12,8},{1,5},{5,1},{9,13},{13,9},{2,6},{6,2},{1... | collective-permute-start | bytes 208904 | tf_op jit(solution)/shard_map/ppermute | solution.py:280
  9.4 0.5 %collective-permute-start.5 = (bf16[272,128]{1,0:T(8,128)(2,1)S(1)}, bf16[272,128]{1,0:T(8,128)(2,1)S(1)}, u32[]{:S(2)}, u32[]{:S(2)}) collective-permute-start(bf16[272,128]{1,0:T(8,128)(2,1)S(1)} %get-tuple-element.25.refs_0_.refs_7_), channel_id=1, source_target_pairs={{0,2},{2,0},{1,3},{3,1},{4,6},{6,4},{5,7},{7,5},{8,10},{10,8},{9,1... | collective-permute-start | bytes 208904 | tf_op jit(solution)/shard_map/ppermute | solution.py:280
  9.9 1.5 %collective-permute-start.1 = (bf16[272,128]{1,0:T(8,128)(2,1)S(1)}, bf16[272,128]{1,0:T(8,128)(2,1)S(1)}, u32[]{:S(2)}, u32[]{:S(2)}) collective-permute-start(bf16[272,128]{1,0:T(8,128)(2,1)S(1)} %collective-permute-done.refs_3_.refs_5_), channel_id=1, source_target_pairs={{0,2},{2,0},{1,3},{3,1},{4,6},{6,4},{5,7},{7,5},{8,10},{10,8},{9,1... | collective-permute-start | bytes 208904 | tf_op jit(solution)/shard_map/ppermute | solution.py:280
  11.4 1.0 %collective-permute-done.2.refs_2_.refs_6_ = bf16[272,128]{1,0:T(8,128)(2,1)S(1)} collective-permute-done((bf16[272,128]{1,0:T(8,128)(2,1)S(1)}, bf16[272,128]{1,0:T(8,128)(2,1)S(1)}, u32[]{:S(2)}, u32[]{:S(2)}) %collective-permute-start.2) | collective-permute-done | bytes 69664 | tf_op jit(solution)/shard_map/ppermute | solution.py:280
  12.4 1.5 %collective-permute-start.3 = (bf16[272,128]{1,0:T(8,128)(2,1)S(1)}, bf16[272,128]{1,0:T(8,128)(2,1)S(1)}, u32[]{:S(2)}, u32[]{:S(2)}) collective-permute-start(bf16[272,128]{1,0:T(8,128)(2,1)S(1)} %collective-permute-done.2.refs_2_.refs_6_), channel_id=1, source_target_pairs={{0,2},{2,0},{1,3},{3,1},{4,6},{6,4},{5,7},{7,5},{8,10},{10,8},{9,1... | collective-permute-start | bytes 208904 | tf_op jit(solution)/shard_map/ppermute | solution.py:280
  13.9 1.9 %shard_map.74 = (bf16[4,512,512]{2,1,0:T(8,128)(2,1)S(1)}, bf16[2048,256]{1,0:T(8,128)(2,1)S(1)}, bf16[256,128]{1,0:T(8,128)(2,1)S(1)}, bf16[64,256]{1,0:T(8,128...) custom-call(s32[2,16]{1,0:T(2,128)} %bitcast.4, bf16[4,512,512]{2,1,0:T(8,128)(2,1)} %constant.7.clone.refs_0_, ...), custom_call_target="tpu_custom_call" | custom-call | bytes 4194304 | tf_op jit(solution)/shard_map/pallas_call | solution.py:299
  15.8 0.5 %shard_map.75.refs_8_ = bf16[64,2048]{1,0:T(8,128)(2,1)S(1)} custom-call(bf16[272,128]{1,0:T(8,128)(2,1)S(1)} %get-tuple-element.25.refs_0_.refs_7_, bf16[272,128]{1,0:T(8,128)(2,1)S(1)} %collective-permute-done.4.refs_1_.refs_2_, bf16[272,128]{1,0:T(8,128)(2,1)S(1)} %collective-permute-done.2.refs_2_.refs_6_, ...), custom_call_target="tpu_custom_call" | custom-call | tf_op jit(solution)/shard_map/pallas_call | solution.py:321
  16.3 0.0 copy-start
  16.3 0.0 collective-permute-done.6.refs_4_
  16.3 0.0 collective-permute-done.5.refs_3_
  16.3 0.4 %collective-permute-done.3.refs_1_ = bf16[272,128]{1,0:T(8,128)(2,1)S(1)} collective-permute-done((bf16[272,128]{1,0:T(8,128)(2,1)S(1)}, bf16[272,128]{1,0:T(8,128)(2,1)S(1)}, u32[]{:S(2)}, u32[]{:S(2)}) %collective-permute-start.3) | collective-permute-done | bytes 69664 | tf_op jit(solution)/shard_map/ppermute | solution.py:280
  16.7 1.1 %shard_map.76 = (bf16[256,2048]{1,0:T(8,128)(2,1)S(1)}, f32[128,256]{1,0:T(8,128)S(1)}, bf16[128,256]{1,0:T(8,128)(2,1)S(1)}) custom-call(bf16[272,128]{1,0:T(8,128)(2,1)S(1)} %collective-permute-done.1.refs_0_, bf16[272,128]{1,0:T(8,128)(2,1)S(1)} %collective-permute-done.3.refs_1_, bf16[272,128]{1,0:T(8,128)(2,1)S(1)} %collective-permute-done.4.refs_1_.refs_2_, ...), custom_call_target="tpu_custom_call" | custom-call | tf_op jit(solution)/shard_map/pallas_call | solution.py:328
  17.9 0.1 collective-permute-start.7
  17.9 1.2 %collective-permute-done.7.other_ref = bf16[128,256]{1,0:T(8,128)(2,1)S(1)} collective-permute-done((bf16[128,256]{1,0:T(8,128)(2,1)S(1)}, bf16[128,256]{1,0:T(8,128)(2,1)S(1)}, u32[]{:S(2)}, u32[]{:S(2)}) %collective-permute-start.7) | collective-permute-done | bytes 65568 | tf_op jit(solution)/shard_map/ppermute | solution.py:280
  19.2 1.2 %shard_map.77 = (bf16[64,512]{1,0:T(8,128)(2,1)S(1)}, bf16[64,512]{1,0:T(8,128)(2,1)S(1)}, bf16[64,512]{1,0:T(8,128)(2,1)S(1)}, bf16[64,512]{1,0:T(8,128)(2,1)S(1)}) custom-call(bf16[256,2048]{1,0:T(8,128)(2,1)S(1)} %get-tuple-element.30.chosen_ref, f32[128,256]{1,0:T(8,128)S(1)} %get-tuple-element.31.mine_ref, ...), custom_call_target="tpu_custom_call" | custom-call | tf_op jit(solution)/shard_map/pallas_call | solution.py:338
  20.4 2.7 %collective-permute-start.8 = (bf16[64,512]{1,0:T(8,128)(2,1)S(1)}, bf16[64,512]{1,0:T(8,128)(2,1)S(1)}, u32[]{:S(2)}, u32[]{:S(2)}) collective-permute-start(bf16[64,512]{1,0:T(8,128)(2,1)S(1)} %get-tuple-element.34), channel_id=1, source_target_pairs={{0,12},{4,8},{8,4},{12,0},{1,13},{5,9},{9,5},{13,1},{2,14},{6,10},... | collective-permute-start | bytes 196616 | tf_op jit(solution)/shard_map/ppermute | solution.py:280
  23.1 0.0 collective-permute-start.9
  23.2 1.7 %collective-permute-start.10 = (bf16[64,512]{1,0:T(8,128)(2,1)S(1)}, bf16[64,512]{1,0:T(8,128)(2,1)S(1)}, u32[]{:S(2)}, u32[]{:S(2)}) collective-permute-start(bf16[64,512]{1,0:T(8,128)(2,1)S(1)} %get-tuple-element.36), channel_id=1, source_target_pairs={{0,8},{4,12},{8,0},{12,4},{1,9},{5,13},{9,1},{13,5},{2,10},{6,14},... | collective-permute-start | bytes 196616 | tf_op jit(solution)/shard_map/ppermute | solution.py:280
  24.9 2.4 %collective-permute-done.8.refs_0_ = bf16[64,512]{1,0:T(8,128)(2,1)S(1)} collective-permute-done((bf16[64,512]{1,0:T(8,128)(2,1)S(1)}, bf16[64,512]{1,0:T(8,128)(2,1)S(1)}, u32[]{:S(2)}, u32[]{:S(2)}) %collective-permute-start.8) | collective-permute-done | bytes 65568 | tf_op jit(solution)/shard_map/ppermute | solution.py:280
  27.3 2.0 %collective-permute-done.9.refs_1_ = bf16[64,512]{1,0:T(8,128)(2,1)S(1)} collective-permute-done((bf16[64,512]{1,0:T(8,128)(2,1)S(1)}, bf16[64,512]{1,0:T(8,128)(2,1)S(1)}, u32[]{:S(2)}, u32[]{:S(2)}) %collective-permute-start.9) | collective-permute-done | bytes 65568 | tf_op jit(solution)/shard_map/ppermute | solution.py:280
  29.3 0.9 %shard_map.78 = bf16[512,256]{1,0:T(8,128)(2,1)} custom-call(bf16[64,512]{1,0:T(8,128)(2,1)S(1)} %collective-permute-done.8.refs_0_, bf16[64,512]{1,0:T(8,128)(2,1)S(1)} %collective-permute-done.9.refs_1_, bf16[64,512]{1,0:T(8,128)(2,1)S(1)} %collective-permute-done.10.refs_2_, bf16[64,512]{1,0:T(8,128)(2,1)S(1)} %get-tuple-element.37.refs_3_, ...), custom_call_target="tpu_custom_call" | custom-call | tf_op jit(solution)/shard_map/pallas_call | solution.py:347
  (6 shorter events, 0.0 us)
Async XLA Ops:
  1.3 8.6 %collective-permute-start = (bf16[272,128]{1,0:T(8,128)(2,1)S(1)}, bf16[272,128]{1,0:T(8,128)(2,1)S(1)}, u32[]{:S(2)}, u32[]{:S(2)}) collective-permute-start(bf16[272,128]{1,0:T(8,128)(2,1)S(1)} %get-tuple-element.22), channel_id=1, source_target_pairs={{0,12},{4,8},{8,4},{12,0},{1,13},{5,9},{9,5},{13,1},{2,14},{6,10},... | collective-permute-start | bytes 208904 | tf_op jit(solution)/shard_map/ppermute | solution.py:280
  6.4 6.0 %collective-permute-start.2 = (bf16[272,128]{1,0:T(8,128)(2,1)S(1)}, bf16[272,128]{1,0:T(8,128)(2,1)S(1)}, u32[]{:S(2)}, u32[]{:S(2)}) collective-permute-start(bf16[272,128]{1,0:T(8,128)(2,1)S(1)} %get-tuple-element.23), channel_id=1, source_target_pairs={{0,8},{4,12},{8,0},{12,4},{1,9},{5,13},{9,1},{13,5},{2,10},{6,14},... | collective-permute-start | bytes 208904 | tf_op jit(solution)/shard_map/ppermute | solution.py:280
  6.4 9.9 %collective-permute-start.6 = (bf16[272,128]{1,0:T(8,128)(2,1)S(1)}, bf16[272,128]{1,0:T(8,128)(2,1)S(1)}, u32[]{:S(2)}, u32[]{:S(2)}) collective-permute-start(bf16[272,128]{1,0:T(8,128)(2,1)S(1)} %get-tuple-element.24), channel_id=1, source_target_pairs={{0,6},{2,4},{4,2},{6,0},{8,14},{10,12},{12,10},{14,8},{1,7},{3,5},... | collective-permute-start | bytes 208904 | tf_op jit(solution)/shard_map/ppermute | solution.py:280
  8.1 7.7 %collective-permute-start.4 = (bf16[272,128]{1,0:T(8,128)(2,1)S(1)}, bf16[272,128]{1,0:T(8,128)(2,1)S(1)}, u32[]{:S(2)}, u32[]{:S(2)}) collective-permute-start(bf16[272,128]{1,0:T(8,128)(2,1)S(1)} %get-tuple-element.24), channel_id=1, source_target_pairs={{0,4},{4,0},{8,12},{12,8},{1,5},{5,1},{9,13},{13,9},{2,6},{6,2},{1... | collective-permute-start | bytes 208904 | tf_op jit(solution)/shard_map/ppermute | solution.py:280
  9.4 6.9 %collective-permute-start.5 = (bf16[272,128]{1,0:T(8,128)(2,1)S(1)}, bf16[272,128]{1,0:T(8,128)(2,1)S(1)}, u32[]{:S(2)}, u32[]{:S(2)}) collective-permute-start(bf16[272,128]{1,0:T(8,128)(2,1)S(1)} %get-tuple-element.25.refs_0_.refs_7_), channel_id=1, source_target_pairs={{0,2},{2,0},{1,3},{3,1},{4,6},{6,4},{5,7},{7,5},{8,10},{10,8},{9,1... | collective-permute-start | bytes 208904 | tf_op jit(solution)/shard_map/ppermute | solution.py:280
  9.9 6.4 %collective-permute-start.1 = (bf16[272,128]{1,0:T(8,128)(2,1)S(1)}, bf16[272,128]{1,0:T(8,128)(2,1)S(1)}, u32[]{:S(2)}, u32[]{:S(2)}) collective-permute-start(bf16[272,128]{1,0:T(8,128)(2,1)S(1)} %collective-permute-done.refs_3_.refs_5_), channel_id=1, source_target_pairs={{0,2},{2,0},{1,3},{3,1},{4,6},{6,4},{5,7},{7,5},{8,10},{10,8},{9,1... | collective-permute-start | bytes 208904 | tf_op jit(solution)/shard_map/ppermute | solution.py:280
  12.4 4.3 %collective-permute-start.3 = (bf16[272,128]{1,0:T(8,128)(2,1)S(1)}, bf16[272,128]{1,0:T(8,128)(2,1)S(1)}, u32[]{:S(2)}, u32[]{:S(2)}) collective-permute-start(bf16[272,128]{1,0:T(8,128)(2,1)S(1)} %collective-permute-done.2.refs_2_.refs_6_), channel_id=1, source_target_pairs={{0,2},{2,0},{1,3},{3,1},{4,6},{6,4},{5,7},{7,5},{8,10},{10,8},{9,1... | collective-permute-start | bytes 208904 | tf_op jit(solution)/shard_map/ppermute | solution.py:280
  16.3 2.9 %copy-start = (bf16[4,512,512]{2,1,0:T(8,128)(2,1)S(1)}, bf16[4,512,512]{2,1,0:T(8,128)(2,1)}, u32[]{:S(2)}) copy-start(bf16[4,512,512]{2,1,0:T(8,128)(2,1)} %constant.6.clone.back_ref) | copy-start | bytes 6291460
  17.9 1.3 %collective-permute-start.7 = (bf16[128,256]{1,0:T(8,128)(2,1)S(1)}, bf16[128,256]{1,0:T(8,128)(2,1)S(1)}, u32[]{:S(2)}, u32[]{:S(2)}) collective-permute-start(bf16[128,256]{1,0:T(8,128)(2,1)S(1)} %get-tuple-element.32), channel_id=1, source_target_pairs={{0,1},{1,0},{2,3},{3,2},{4,5},{5,4},{6,7},{7,6},{8,9},{9,8},{10,11... | collective-permute-start | bytes 196616 | tf_op jit(solution)/shard_map/ppermute | solution.py:280
  20.4 6.9 %collective-permute-start.8 = (bf16[64,512]{1,0:T(8,128)(2,1)S(1)}, bf16[64,512]{1,0:T(8,128)(2,1)S(1)}, u32[]{:S(2)}, u32[]{:S(2)}) collective-permute-start(bf16[64,512]{1,0:T(8,128)(2,1)S(1)} %get-tuple-element.34), channel_id=1, source_target_pairs={{0,12},{4,8},{8,4},{12,0},{1,13},{5,9},{9,5},{13,1},{2,14},{6,10},... | collective-permute-start | bytes 196616 | tf_op jit(solution)/shard_map/ppermute | solution.py:280
  23.1 6.1 %collective-permute-start.9 = (bf16[64,512]{1,0:T(8,128)(2,1)S(1)}, bf16[64,512]{1,0:T(8,128)(2,1)S(1)}, u32[]{:S(2)}, u32[]{:S(2)}) collective-permute-start(bf16[64,512]{1,0:T(8,128)(2,1)S(1)} %get-tuple-element.35), channel_id=1, source_target_pairs={{0,4},{4,0},{8,12},{12,8},{1,5},{5,1},{9,13},{13,9},{2,6},{6,2},{1... | collective-permute-start | bytes 196616 | tf_op jit(solution)/shard_map/ppermute | solution.py:280
  23.2 6.1 %collective-permute-start.10 = (bf16[64,512]{1,0:T(8,128)(2,1)S(1)}, bf16[64,512]{1,0:T(8,128)(2,1)S(1)}, u32[]{:S(2)}, u32[]{:S(2)}) collective-permute-start(bf16[64,512]{1,0:T(8,128)(2,1)S(1)} %get-tuple-element.36), channel_id=1, source_target_pairs={{0,8},{4,12},{8,0},{12,4},{1,9},{5,13},{9,1},{13,5},{2,10},{6,14},... | collective-permute-start | bytes 196616 | tf_op jit(solution)/shard_map/ppermute | solution.py:280

commit v10 on v8

--- a/solution.py
+++ b/solution.py
@@ -294,8 +294,9 @@
     held = [along("fibre", send[k], lambda i: i ^ k) for k in range(SPANS - 1, 0, -1)]
     held = [send[0]] + held[::-1]
     table_back = jnp.asarray(np.ascontiguousarray(table.transpose(0, 2, 1)))
-    constants = [jnp.asarray(c) for c in (table, lags)]
-    table, lags, take, give, find, order = pl.pallas_call(
+    lags = jnp.asarray(lags)
+    constants = [jnp.asarray(table)]
+    table, take, give, find, order = pl.pallas_call(
         functools.partial(prepare_kernel, segs, blocks, own, pairs_dev, share),
         out_shape=[pltpu.VMEM(c.shape, low) for c in constants]
         + [

time: 30.6 us -> 30.6 us (level)
  transfers between devices with their start and end apart: 11 -> 11, of which waited for: 5 -> 5; matrix products, arithmetic and copies ran while one was open for 0% -> 0% of each run, Pallas kernels for 8% -> 7%
where the time goes in v10:
time: 30.6 us; the launch traced here: 30.5 us
  starting transfers between devices  16.1 us (53%)
  waiting for transfers between devices  7.32 us (24%)
  Pallas kernels  6.94 us (23%)
    ppermute x11, starting transfers between devices, along(): lax.ppermute(array, axis, [(i, target(i)) for i in range(lax.axis_size(ax...  16.1 us
    ppermute x11, waiting for transfers between devices, along(): lax.ppermute(array, axis, [(i, target(i)) for i in range(lax.axis_size(ax...  7.32 us
    pallas_call x1, Pallas kernels, by_own_k(): pl.pallas_call(functools.partial(prepare_kernel, segs, blocks, own, pairs...  1.7 us
    pallas_call x1, Pallas kernels, by_own_k(): pl.pallas_call(functools.partial(adjoint_kernel, blocks, own), out_shape=...  1.42 us
    pallas_call x1, Pallas kernels, by_own_k(): pl.pallas_call(functools.partial(pack_kernel, blocks, own), out_shape=[pl...  1.28 us
    pallas_call x1, Pallas kernels, by_own_k(): pl.pallas_call(functools.partial(correlate_kernel, segs, blocks, own), ou...  1.13 us
    pallas_call x1, Pallas kernels, by_own_k(): pl.pallas_call(unpack_kernel, out_shape=jax.ShapeDtypeStruct((span, count...  0.94 us
  transfers between devices with their start and end apart: 11, of which 5 were waited for; matrix products, arithmetic and copies ran while one was open for 0% of the time, Pallas kernels for 7%

profile of v10, /device:TPU:0, one launch (start us, length us, event | category | flops | bytes accessed | tf_op | source)
XLA Modules:
  0.0 30.5 jit_solution(5922450358366081954)
XLA Ops:
  0.0 1.3 %shard_map.73 = (bf16[272,128]{1,0:T(8,128)(2,1)S(1)}, bf16[272,128]{1,0:T(8,128)(2,1)S(1)}, bf16[272,128]{1,0:T(8,128)(2,1)S(1)}, bf16[272,128]{1,0:T(8,128)(2,1)S(1)}) custom-call(bf16[512,256]{1,0:T(8,128)(2,1)} %bitcast.3, f32[2,32,256]{2,1,0:T(8,128)} %observed_hbm.1, s32[2,256]{1,0:T(2,128)} %mask_hbm.1), custom_call_target="tpu_custom_call" | custom-call | tf_op jit(solution)/shard_map/pallas_call | solution.py:281
  1.3 5.1 %collective-permute-start = (bf16[272,128]{1,0:T(8,128)(2,1)S(1)}, bf16[272,128]{1,0:T(8,128)(2,1)S(1)}, u32[]{:S(2)}, u32[]{:S(2)}) collective-permute-start(bf16[272,128]{1,0:T(8,128)(2,1)S(1)} %get-tuple-element.20), channel_id=1, source_target_pairs={{0,12},{4,8},{8,4},{12,0},{1,13},{5,9},{9,5},{13,1},{2,14},{6,10},... | collective-permute-start | bytes 208904 | tf_op jit(solution)/shard_map/ppermute | solution.py:279
  6.4 0.0 collective-permute-start.2
  6.4 1.7 %collective-permute-start.6 = (bf16[272,128]{1,0:T(8,128)(2,1)S(1)}, bf16[272,128]{1,0:T(8,128)(2,1)S(1)}, u32[]{:S(2)}, u32[]{:S(2)}) collective-permute-start(bf16[272,128]{1,0:T(8,128)(2,1)S(1)} %get-tuple-element.22), channel_id=1, source_target_pairs={{0,6},{2,4},{4,2},{6,0},{8,14},{10,12},{12,10},{14,8},{1,7},{3,5},... | collective-permute-start | bytes 208904 | tf_op jit(solution)/shard_map/ppermute | solution.py:279
  8.1 1.2 %collective-permute-start.4 = (bf16[272,128]{1,0:T(8,128)(2,1)S(1)}, bf16[272,128]{1,0:T(8,128)(2,1)S(1)}, u32[]{:S(2)}, u32[]{:S(2)}) collective-permute-start(bf16[272,128]{1,0:T(8,128)(2,1)S(1)} %get-tuple-element.22), channel_id=1, source_target_pairs={{0,4},{4,0},{8,12},{12,8},{1,5},{5,1},{9,13},{13,9},{2,6},{6,2},{1... | collective-permute-start | bytes 208904 | tf_op jit(solution)/shard_map/ppermute | solution.py:279
  9.4 0.5 %collective-permute-start.5 = (bf16[272,128]{1,0:T(8,128)(2,1)S(1)}, bf16[272,128]{1,0:T(8,128)(2,1)S(1)}, u32[]{:S(2)}, u32[]{:S(2)}) collective-permute-start(bf16[272,128]{1,0:T(8,128)(2,1)S(1)} %get-tuple-element.23.refs_0_.refs_7_), channel_id=1, source_target_pairs={{0,2},{2,0},{1,3},{3,1},{4,6},{6,4},{5,7},{7,5},{8,10},{10,8},{9,1... | collective-permute-start | bytes 208904 | tf_op jit(solution)/shard_map/ppermute | solution.py:279
  9.9 0.0 collective-permute-done.refs_3_.refs_5_
  9.9 1.5 %collective-permute-start.1 = (bf16[272,128]{1,0:T(8,128)(2,1)S(1)}, bf16[272,128]{1,0:T(8,128)(2,1)S(1)}, u32[]{:S(2)}, u32[]{:S(2)}) collective-permute-start(bf16[272,128]{1,0:T(8,128)(2,1)S(1)} %collective-permute-done.refs_3_.refs_5_), channel_id=1, source_target_pairs={{0,2},{2,0},{1,3},{3,1},{4,6},{6,4},{5,7},{7,5},{8,10},{10,8},{9,1... | collective-permute-start | bytes 208904 | tf_op jit(solution)/shard_map/ppermute | solution.py:279
  11.4 1.0 %collective-permute-done.2.refs_2_.refs_6_ = bf16[272,128]{1,0:T(8,128)(2,1)S(1)} collective-permute-done((bf16[272,128]{1,0:T(8,128)(2,1)S(1)}, bf16[272,128]{1,0:T(8,128)(2,1)S(1)}, u32[]{:S(2)}, u32[]{:S(2)}) %collective-permute-start.2) | collective-permute-done | bytes 69664 | tf_op jit(solution)/shard_map/ppermute | solution.py:279
  12.4 1.5 %collective-permute-start.3 = (bf16[272,128]{1,0:T(8,128)(2,1)S(1)}, bf16[272,128]{1,0:T(8,128)(2,1)S(1)}, u32[]{:S(2)}, u32[]{:S(2)}) collective-permute-start(bf16[272,128]{1,0:T(8,128)(2,1)S(1)} %collective-permute-done.2.refs_2_.refs_6_), channel_id=1, source_target_pairs={{0,2},{2,0},{1,3},{3,1},{4,6},{6,4},{5,7},{7,5},{8,10},{10,8},{9,1... | collective-permute-start | bytes 208904 | tf_op jit(solution)/shard_map/ppermute | solution.py:279
  13.9 1.7 %shard_map.74 = (bf16[4,512,512]{2,1,0:T(8,128)(2,1)S(1)}, bf16[256,128]{1,0:T(8,128)(2,1)S(1)}, bf16[64,256]{1,0:T(8,128)(2,1)S(1)}, bf16[2,128,128]{2,1,0:T(8,128)(2,1)S(1)}, bf16[256,256]{1,0:T(8,128)(2,1)S(1)}) custom-call(s32[2,16]{1,0:T(2,128)} %bitcast.4, bf16[4,512,512]{2,1,0:T(8,128)(2,1)} %constant.8.clone.refs_0_), custom_call_target="tpu_custom_call" | custom-call | bytes 4194304 | tf_op jit(solution)/shard_map/pallas_call | solution.py:299
  15.6 0.5 %shard_map.75.refs_8_ = bf16[64,2048]{1,0:T(8,128)(2,1)S(1)} custom-call(bf16[272,128]{1,0:T(8,128)(2,1)S(1)} %get-tuple-element.23.refs_0_.refs_7_, bf16[272,128]{1,0:T(8,128)(2,1)S(1)} %collective-permute-done.4.refs_1_.refs_2_, bf16[272,128]{1,0:T(8,128)(2,1)S(1)} %collective-permute-done.2.refs_2_.refs_6_, ...), custom_call_target="tpu_custom_call" | custom-call | tf_op jit(solution)/shard_map/pallas_call | solution.py:321
  16.1 0.0 copy-start.1
  16.1 0.6 %collective-permute-done.3.refs_1_ = bf16[272,128]{1,0:T(8,128)(2,1)S(1)} collective-permute-done((bf16[272,128]{1,0:T(8,128)(2,1)S(1)}, bf16[272,128]{1,0:T(8,128)(2,1)S(1)}, u32[]{:S(2)}, u32[]{:S(2)}) %collective-permute-start.3) | collective-permute-done | bytes 69664 | tf_op jit(solution)/shard_map/ppermute | solution.py:279
  16.7 1.1 %shard_map.76 = (bf16[256,2048]{1,0:T(8,128)(2,1)S(1)}, f32[128,256]{1,0:T(8,128)S(1)}) custom-call(bf16[272,128]{1,0:T(8,128)(2,1)S(1)} %collective-permute-done.1.refs_0_, bf16[272,128]{1,0:T(8,128)(2,1)S(1)} %collective-permute-done.3.refs_1_, bf16[272,128]{1,0:T(8,128)(2,1)S(1)} %collective-permute-done.4.refs_1_.refs_2_, ...), custom_call_target="tpu_custom_call" | custom-call | tf_op jit(solution)/shard_map/pallas_call | solution.py:328
  17.9 0.1 collective-permute-start.7
  17.9 1.3 %collective-permute-done.7.other_ref = f32[128,256]{1,0:T(8,128)S(1)} collective-permute-done((f32[128,256]{1,0:T(8,128)S(1)}, f32[128,256]{1,0:T(8,128)S(1)}, u32[]{:S(2)}, u32[]{:S(2)}) %collective-permute-start.7) | collective-permute-done | bytes 131104 | tf_op jit(solution)/shard_map/ppermute | solution.py:279
  19.3 1.4 %shard_map.77 = (bf16[64,512]{1,0:T(8,128)(2,1)S(1)}, bf16[64,512]{1,0:T(8,128)(2,1)S(1)}, bf16[64,512]{1,0:T(8,128)(2,1)S(1)}, bf16[64,512]{1,0:T(8,128)(2,1)S(1)}) custom-call(bf16[256,2048]{1,0:T(8,128)(2,1)S(1)} %get-tuple-element.27.chosen_ref, f32[128,256]{1,0:T(8,128)S(1)} %get-tuple-element.28.mine_ref, ...), custom_call_target="tpu_custom_call" | custom-call | tf_op jit(solution)/shard_map/pallas_call | solution.py:338
  20.7 2.7 %collective-permute-start.8 = (bf16[64,512]{1,0:T(8,128)(2,1)S(1)}, bf16[64,512]{1,0:T(8,128)(2,1)S(1)}, u32[]{:S(2)}, u32[]{:S(2)}) collective-permute-start(bf16[64,512]{1,0:T(8,128)(2,1)S(1)} %get-tuple-element.30), channel_id=1, source_target_pairs={{0,12},{4,8},{8,4},{12,0},{1,13},{5,9},{9,5},{13,1},{2,14},{6,10},... | collective-permute-start | bytes 196616 | tf_op jit(solution)/shard_map/ppermute | solution.py:279
  23.4 0.0 collective-permute-start.9
  23.4 1.7 %collective-permute-start.10 = (bf16[64,512]{1,0:T(8,128)(2,1)S(1)}, bf16[64,512]{1,0:T(8,128)(2,1)S(1)}, u32[]{:S(2)}, u32[]{:S(2)}) collective-permute-start(bf16[64,512]{1,0:T(8,128)(2,1)S(1)} %get-tuple-element.32), channel_id=1, source_target_pairs={{0,8},{4,12},{8,0},{12,4},{1,9},{5,13},{9,1},{13,5},{2,10},{6,14},... | collective-permute-start | bytes 196616 | tf_op jit(solution)/shard_map/ppermute | solution.py:279
  25.2 2.4 %collective-permute-done.8.refs_0_ = bf16[64,512]{1,0:T(8,128)(2,1)S(1)} collective-permute-done((bf16[64,512]{1,0:T(8,128)(2,1)S(1)}, bf16[64,512]{1,0:T(8,128)(2,1)S(1)}, u32[]{:S(2)}, u32[]{:S(2)}) %collective-permute-start.8) | collective-permute-done | bytes 65568 | tf_op jit(solution)/shard_map/ppermute | solution.py:279
  27.6 2.0 %collective-permute-done.9.refs_1_ = bf16[64,512]{1,0:T(8,128)(2,1)S(1)} collective-permute-done((bf16[64,512]{1,0:T(8,128)(2,1)S(1)}, bf16[64,512]{1,0:T(8,128)(2,1)S(1)}, u32[]{:S(2)}, u32[]{:S(2)}) %collective-permute-start.9) | collective-permute-done | bytes 65568 | tf_op jit(solution)/shard_map/ppermute | solution.py:279
  29.5 0.9 %shard_map.78 = bf16[512,256]{1,0:T(8,128)(2,1)} custom-call(bf16[64,512]{1,0:T(8,128)(2,1)S(1)} %collective-permute-done.8.refs_0_, bf16[64,512]{1,0:T(8,128)(2,1)S(1)} %collective-permute-done.9.refs_1_, bf16[64,512]{1,0:T(8,128)(2,1)S(1)} %collective-permute-done.10.refs_2_, bf16[64,512]{1,0:T(8,128)(2,1)S(1)} %get-tuple-element.33.refs_3_, ...), custom_call_target="tpu_custom_call" | custom-call | tf_op jit(solution)/shard_map/pallas_call | solution.py:347
  (8 shorter events, 0.0 us)
Async XLA Ops:
  1.3 8.6 %collective-permute-start = (bf16[272,128]{1,0:T(8,128)(2,1)S(1)}, bf16[272,128]{1,0:T(8,128)(2,1)S(1)}, u32[]{:S(2)}, u32[]{:S(2)}) collective-permute-start(bf16[272,128]{1,0:T(8,128)(2,1)S(1)} %get-tuple-element.20), channel_id=1, source_target_pairs={{0,12},{4,8},{8,4},{12,0},{1,13},{5,9},{9,5},{13,1},{2,14},{6,10},... | collective-permute-start | bytes 208904 | tf_op jit(solution)/shard_map/ppermute | solution.py:279
  6.4 6.0 %collective-permute-start.2 = (bf16[272,128]{1,0:T(8,128)(2,1)S(1)}, bf16[272,128]{1,0:T(8,128)(2,1)S(1)}, u32[]{:S(2)}, u32[]{:S(2)}) collective-permute-start(bf16[272,128]{1,0:T(8,128)(2,1)S(1)} %get-tuple-element.21), channel_id=1, source_target_pairs={{0,8},{4,12},{8,0},{12,4},{1,9},{5,13},{9,1},{13,5},{2,10},{6,14},... | collective-permute-start | bytes 208904 | tf_op jit(solution)/shard_map/ppermute | solution.py:279
  6.4 9.7 %collective-permute-start.6 = (bf16[272,128]{1,0:T(8,128)(2,1)S(1)}, bf16[272,128]{1,0:T(8,128)(2,1)S(1)}, u32[]{:S(2)}, u32[]{:S(2)}) collective-permute-start(bf16[272,128]{1,0:T(8,128)(2,1)S(1)} %get-tuple-element.22), channel_id=1, source_target_pairs={{0,6},{2,4},{4,2},{6,0},{8,14},{10,12},{12,10},{14,8},{1,7},{3,5},... | collective-permute-start | bytes 208904 | tf_op jit(solution)/shard_map/ppermute | solution.py:279
  8.1 7.5 %collective-permute-start.4 = (bf16[272,128]{1,0:T(8,128)(2,1)S(1)}, bf16[272,128]{1,0:T(8,128)(2,1)S(1)}, u32[]{:S(2)}, u32[]{:S(2)}) collective-permute-start(bf16[272,128]{1,0:T(8,128)(2,1)S(1)} %get-tuple-element.22), channel_id=1, source_target_pairs={{0,4},{4,0},{8,12},{12,8},{1,5},{5,1},{9,13},{13,9},{2,6},{6,2},{1... | collective-permute-start | bytes 208904 | tf_op jit(solution)/shard_map/ppermute | solution.py:279
  9.4 6.8 %collective-permute-start.5 = (bf16[272,128]{1,0:T(8,128)(2,1)S(1)}, bf16[272,128]{1,0:T(8,128)(2,1)S(1)}, u32[]{:S(2)}, u32[]{:S(2)}) collective-permute-start(bf16[272,128]{1,0:T(8,128)(2,1)S(1)} %get-tuple-element.23.refs_0_.refs_7_), channel_id=1, source_target_pairs={{0,2},{2,0},{1,3},{3,1},{4,6},{6,4},{5,7},{7,5},{8,10},{10,8},{9,1... | collective-permute-start | bytes 208904 | tf_op jit(solution)/shard_map/ppermute | solution.py:279
  9.9 6.2 %collective-permute-start.1 = (bf16[272,128]{1,0:T(8,128)(2,1)S(1)}, bf16[272,128]{1,0:T(8,128)(2,1)S(1)}, u32[]{:S(2)}, u32[]{:S(2)}) collective-permute-start(bf16[272,128]{1,0:T(8,128)(2,1)S(1)} %collective-permute-done.refs_3_.refs_5_), channel_id=1, source_target_pairs={{0,2},{2,0},{1,3},{3,1},{4,6},{6,4},{5,7},{7,5},{8,10},{10,8},{9,1... | collective-permute-start | bytes 208904 | tf_op jit(solution)/shard_map/ppermute | solution.py:279
  12.4 4.3 %collective-permute-start.3 = (bf16[272,128]{1,0:T(8,128)(2,1)S(1)}, bf16[272,128]{1,0:T(8,128)(2,1)S(1)}, u32[]{:S(2)}, u32[]{:S(2)}) collective-permute-start(bf16[272,128]{1,0:T(8,128)(2,1)S(1)} %collective-permute-done.2.refs_2_.refs_6_), channel_id=1, source_target_pairs={{0,2},{2,0},{1,3},{3,1},{4,6},{6,4},{5,7},{7,5},{8,10},{10,8},{9,1... | collective-permute-start | bytes 208904 | tf_op jit(solution)/shard_map/ppermute | solution.py:279
  13.9 2.8 %copy-start = (bf16[2048,256]{1,0:T(8,128)(2,1)S(1)}, bf16[2048,256]{1,0:T(8,128)(2,1)}, u32[]{:S(2)}) copy-start(bf16[2048,256]{1,0:T(8,128)(2,1)} %constant.7.clone.refs_10_.lag_ref) | copy-start | bytes 3145732
  16.1 3.2 %copy-start.1 = (bf16[4,512,512]{2,1,0:T(8,128)(2,1)S(1)}, bf16[4,512,512]{2,1,0:T(8,128)(2,1)}, u32[]{:S(2)}) copy-start(bf16[4,512,512]{2,1,0:T(8,128)(2,1)} %constant.6.clone.back_ref) | copy-start | bytes 6291460
  17.9 1.4 %collective-permute-start.7 = (f32[128,256]{1,0:T(8,128)S(1)}, f32[128,256]{1,0:T(8,128)S(1)}, u32[]{:S(2)}, u32[]{:S(2)}) collective-permute-start(f32[128,256]{1,0:T(8,128)S(1)} %get-tuple-element.28.mine_ref), channel_id=1, source_target_pairs={{0,1},{1,0},{2,3},{3,2},{4,5},{5,4},{6,7},{7,6},{8,9},{9,8},{10,11... | collective-permute-start | bytes 393224 | tf_op jit(solution)/shard_map/ppermute | solution.py:279
  20.7 6.9 %collective-permute-start.8 = (bf16[64,512]{1,0:T(8,128)(2,1)S(1)}, bf16[64,512]{1,0:T(8,128)(2,1)S(1)}, u32[]{:S(2)}, u32[]{:S(2)}) collective-permute-start(bf16[64,512]{1,0:T(8,128)(2,1)S(1)} %get-tuple-element.30), channel_id=1, source_target_pairs={{0,12},{4,8},{8,4},{12,0},{1,13},{5,9},{9,5},{13,1},{2,14},{6,10},... | collective-permute-start | bytes 196616 | tf_op jit(solution)/shard_map/ppermute | solution.py:279
  23.4 6.1 %collective-permute-start.9 = (bf16[64,512]{1,0:T(8,128)(2,1)S(1)}, bf16[64,512]{1,0:T(8,128)(2,1)S(1)}, u32[]{:S(2)}, u32[]{:S(2)}) collective-permute-start(bf16[64,512]{1,0:T(8,128)(2,1)S(1)} %get-tuple-element.31), channel_id=1, source_target_pairs={{0,4},{4,0},{8,12},{12,8},{1,5},{5,1},{9,13},{13,9},{2,6},{6,2},{1... | collective-permute-start | bytes 196616 | tf_op jit(solution)/shard_map/ppermute | solution.py:279
  23.4 6.1 %collective-permute-start.10 = (bf16[64,512]{1,0:T(8,128)(2,1)S(1)}, bf16[64,512]{1,0:T(8,128)(2,1)S(1)}, u32[]{:S(2)}, u32[]{:S(2)}) collective-permute-start(bf16[64,512]{1,0:T(8,128)(2,1)S(1)} %get-tuple-element.32), channel_id=1, source_target_pairs={{0,8},{4,12},{8,0},{12,4},{1,9},{5,13},{9,1},{13,5},{2,10},{6,14},... | collective-permute-start | bytes 196616 | tf_op jit(solution)/shard_map/ppermute | solution.py:279
